TPU v7x, 32 devices: a whole 2x2x4 slice. The times are simulated.
32 devices in a mesh: layer: 2 (over x), tok: 16 (over z, y, core).
Axes of the slice: x: 2, y: 2, z: 4, core: 2. Of those that a mesh axis runs over, the one named last changes fastest.
Arguments:
- tokens: bfloat16 [4096, 7168], P(('layer', 'tok')), parts along dimension 0, may hold values from -22 to 22
- out_grads: bfloat16 [4096, 1024], P(('layer', 'tok')), parts along dimension 0, may hold values from -22 to 22
- routing: int32 [4096, 1], P(('layer', 'tok')), parts along dimension 0, may hold values from 0 to 3; in each aligned block of 128 rows (0 to 127, 128 to 255, ...) at most 48 rows name the same one
- weights: bfloat16 [8, 7168, 1024], P('layer', 'tok'), parts along dimension 0, may hold values from -6 to 6
Outputs:
- fisher: float32 [8, 7168, 1024], P('layer', 'tok'), parts along dimension 0
- merged: bfloat16 [14336, 1024], P(('layer', 'tok')), parts along dimension 0
There are 2 independent parts, one for each index of `layer`. A program takes and returns all parts, laid end to end along the dimension named above; each array names one. Nothing has to cross between parts.
Inputs may be any that keep to these rules, and one draw needn't show every extreme that they name: `routing`: each row names one expert; of the rows of one device at most 48 name the same expert, and that count is reached on some device.
All inputs are finite; a program needn't handle non-finite values.
Results may differ from a plain program's by a relative error of at most 0.0004.
Values may be sent and summed in bfloat16 or wider, within the bound.
No kernel may reach another device: no remote copies, remote signals or barrier semaphores. Data moves between devices by JAX's collectives and lax.ppermute only.
A program may use at most 128 MiB of HBM per device.

v0:
```python
import jax
import jax.numpy as jnp
from jax import lax
from jax.sharding import PartitionSpec as P

D = 7168
F = 1024
CAP = 48


EPSILON = 1e-06


def slot_rows(token_sq, grad_sq, labels, experts):
    row_count = labels.shape[0]
    capacity = min(row_count, CAP)
    member = (labels[:, None] == jnp.arange(experts, dtype=jnp.int32)[None, :]).astype(jnp.int32)
    counts = jnp.sum(member, axis=0)
    starts = jnp.cumsum(counts) - counts
    ranking = jnp.argsort(labels, stable=True)
    token_sq = token_sq[ranking]
    grad_sq = grad_sq[ranking]
    padded_tok = jnp.concatenate(
        [token_sq, jnp.zeros((capacity, token_sq.shape[1]), jnp.float32)], axis=0
    )
    padded_grad = jnp.concatenate(
        [grad_sq, jnp.zeros((capacity, grad_sq.shape[1]), jnp.float32)], axis=0
    )
    slot_ids = jnp.arange(capacity)
    left_rows = []
    right_rows = []
    for expert in range(experts):
        live_mask = (slot_ids < counts[expert]).astype(jnp.float32)
        left_rows.append(
            lax.dynamic_slice_in_dim(padded_tok, starts[expert], capacity, 0) * live_mask[:, None]
        )
        right_rows.append(lax.dynamic_slice_in_dim(padded_grad, starts[expert], capacity, 0))
    return (jnp.stack(left_rows), jnp.stack(right_rows))


def add_block(running, token_sq, grad_block, labels):
    grad_sq = jnp.square(grad_block.astype(jnp.float32))
    left_rows, right_rows = slot_rows(token_sq, grad_sq, labels, running.shape[0])
    return running + jnp.einsum(
        "ecd,ecf->edf", left_rows, right_rows, precision=lax.Precision.HIGHEST
    )


def local(tokens, out_grads, routing, weights):
    rows_dev = tokens.shape[0]
    experts = weights.shape[0]
    hidden = out_grads.shape[1]
    columns = lax.all_to_all(tokens, "tok", split_axis=1, concat_axis=0, tiled=True)
    column_sq = jnp.square(columns.astype(jnp.float32))
    initial = jnp.zeros((experts, columns.shape[1], hidden), jnp.float32)
    running = initial
    grad_piece = lax.all_gather(out_grads, "tok", axis=0, tiled=True)
    route_piece = lax.all_gather(routing, "tok", axis=0, tiled=True)
    row_count = grad_piece.shape[0]
    blocks = row_count // rows_dev
    stacked = (
        column_sq.reshape(blocks, rows_dev, column_sq.shape[1]),
        grad_piece.reshape(blocks, rows_dev, hidden),
        route_piece[:, 0].reshape(blocks, rows_dev),
    )

    def advance(partial_sum, block_item):
        return (add_block(partial_sum, block_item[0], block_item[1], block_item[2]), None)

    running, ignored = lax.scan(advance, running, stacked)
    totals = lax.psum(jnp.sum(running, axis=(1, 2)), "tok")
    scaling = totals / (D * F) + EPSILON
    fisher = running / scaling[:, None, None]
    weights_wide = weights.astype(jnp.float32)
    merged = (jnp.sum(fisher * weights_wide, axis=0) / (jnp.sum(fisher, axis=0) + EPSILON)).astype(
        jnp.bfloat16
    )
    return (fisher, merged)


def solution(mesh):
    in_specs = (
        P(("layer", "tok"), None),
        P(("layer", "tok"), None),
        P(("layer", "tok"), None),
        P("layer", "tok", None),
    )
    out_specs = (P("layer", "tok", None), P(("layer", "tok"), None))
    return jax.shard_map(local, mesh=mesh, in_specs=in_specs, out_specs=out_specs, check_vma=False)
```

profile of v0, /device:TPU:0, one launch (start us, length us, event | category | flops | bytes accessed | tf_op | source)
XLA Modules:
  0.0 601.9 jit_solution(12394697518753936276)
XLA Ops:
  7.9 3.9 copy.8
  11.8 7.4 %all-to-all-start = ((bf16[128,16,448]{0,2,1:T(8,128)(2,1)}), bf16[128,16,448]{0,2,1:T(8,128)(2,1)S(1)}, u32[]{:S(2)}, u32[]{:S(2)}) async-start(bf16[128,16,448]{0,2,1:T(8,128)(2,1)} %bitcast), calls=%async_computation | async-start | bytes 3670016 | tf_op jit(solution)/shard_map/all_to_all | solution.py:53
  19.2 58.7 %all_gather.6 = s32[2048,1]{0,1:T(1,128)S(1)} all-gather(s32[128,1]{0,1:T(1,128)S(1)} %copy-done), channel_id=1, replica_groups=mesh['layer'=2,'tok'=16] {'tok'}, dimensions={0}, use_global_device_ids=true | all-gather | bytes 8704 | tf_op jit(solution)/shard_map/all_gather | solution.py:58
  77.9 2.2 multiply_bitcast_fusion.1
  80.1 4.6 all-gather.2.cloned.1.call-done
  84.7 451.5 %while.11 = (s32[]{:T(128)}, f32[4,448,1024]{2,1,0:T(8,128)}, f32[16,128,448]{1,2,0:T(8,128)}, s32[16,128]{1,0:T(8,128)S(1)}, bf16[16,128,1024]{2,1,0:T(8,128)(2,1)}, /*index=5*/s32[]{:T(128)}, s32[]{:T(128)}, s32[]{:T(128)}) while((s32[]{:T(128)}, f32[4,448,1024]{2,1,0:T(8,128)}, f32[16,128,448]{1,2,0:T(8,128)}, ...), condition=%wide.region_4.5_spmd.clone, body=%wide.region_0.4_spmd.clone.sunk | while | flops 1061834880 | bytes 20918736 | solution.py:70
  85.0 2.6 sort.19
  88.2 1.3 compare_convert_fusion.6
  89.5 1.2 compare_convert_fusion.7
  102.8 8.2 %select_add_fusion.2 = f32[4,448,1024]{2,1,0:T(8,128)} fusion(f32[4,448,1024]{2,1,0:T(8,128)} %get-tuple-element.175, pred[]{:T(512)S(6)} %compare.9, f32[1,48,1024]{2,1,0:T(8,128)S(1)} %get-tuple-element.150, f32[1,48,1024]{2,1,0:T(8,128)S(1)} %get-tuple-element.151, f32[1,48,1024]{2,1,0:T(8,128)S(1)} %get-tuple-element.152, ...), kind=kOutput, calls=%fused_computation.2.clone.1 | convolution fusion | flops 1061482496 | bytes 15810561 | tf_op jit(solution)/shard_map/while/body/eval_jaxpr/ecd,ecf->edf/dot_general | solution.py:44
  111.3 2.6 sort.19
  114.6 1.3 compare_convert_fusion.6
  115.9 1.2 compare_convert_fusion.7
  129.1 10.2 %select_add_fusion.2 = f32[4,448,1024]{2,1,0:T(8,128)} fusion(f32[4,448,1024]{2,1,0:T(8,128)} %get-tuple-element.175, pred[]{:T(512)S(6)} %compare.9, f32[1,48,1024]{2,1,0:T(8,128)S(1)} %get-tuple-element.150, f32[1,48,1024]{2,1,0:T(8,128)S(1)} %get-tuple-element.151, f32[1,48,1024]{2,1,0:T(8,128)S(1)} %get-tuple-element.152, ...), kind=kOutput, calls=%fused_computation.2.clone.1 | convolution fusion | flops 1061482496 | bytes 15810561 | tf_op jit(solution)/shard_map/while/body/eval_jaxpr/ecd,ecf->edf/dot_general | solution.py:44
  139.7 2.6 sort.19
  142.9 1.3 compare_convert_fusion.6
  144.2 1.2 compare_convert_fusion.7
  157.5 10.2 %select_add_fusion.2 = f32[4,448,1024]{2,1,0:T(8,128)} fusion(f32[4,448,1024]{2,1,0:T(8,128)} %get-tuple-element.175, pred[]{:T(512)S(6)} %compare.9, f32[1,48,1024]{2,1,0:T(8,128)S(1)} %get-tuple-element.150, f32[1,48,1024]{2,1,0:T(8,128)S(1)} %get-tuple-element.151, f32[1,48,1024]{2,1,0:T(8,128)S(1)} %get-tuple-element.152, ...), kind=kOutput, calls=%fused_computation.2.clone.1 | convolution fusion | flops 1061482496 | bytes 15810561 | tf_op jit(solution)/shard_map/while/body/eval_jaxpr/ecd,ecf->edf/dot_general | solution.py:44
  168.0 2.6 sort.19
  171.3 1.3 compare_convert_fusion.6
  172.6 1.2 compare_convert_fusion.7
  185.8 10.2 %select_add_fusion.2 = f32[4,448,1024]{2,1,0:T(8,128)} fusion(f32[4,448,1024]{2,1,0:T(8,128)} %get-tuple-element.175, pred[]{:T(512)S(6)} %compare.9, f32[1,48,1024]{2,1,0:T(8,128)S(1)} %get-tuple-element.150, f32[1,48,1024]{2,1,0:T(8,128)S(1)} %get-tuple-element.151, f32[1,48,1024]{2,1,0:T(8,128)S(1)} %get-tuple-element.152, ...), kind=kOutput, calls=%fused_computation.2.clone.1 | convolution fusion | flops 1061482496 | bytes 15810561 | tf_op jit(solution)/shard_map/while/body/eval_jaxpr/ecd,ecf->edf/dot_general | solution.py:44
  196.4 2.6 sort.19
  199.6 1.3 compare_convert_fusion.6
  214.2 10.2 %select_add_fusion.2 = f32[4,448,1024]{2,1,0:T(8,128)} fusion(f32[4,448,1024]{2,1,0:T(8,128)} %get-tuple-element.175, pred[]{:T(512)S(6)} %compare.9, f32[1,48,1024]{2,1,0:T(8,128)S(1)} %get-tuple-element.150, f32[1,48,1024]{2,1,0:T(8,128)S(1)} %get-tuple-element.151, f32[1,48,1024]{2,1,0:T(8,128)S(1)} %get-tuple-element.152, ...), kind=kOutput, calls=%fused_computation.2.clone.1 | convolution fusion | flops 1061482496 | bytes 15810561 | tf_op jit(solution)/shard_map/while/body/eval_jaxpr/ecd,ecf->edf/dot_general | solution.py:44
  224.7 2.6 sort.19
  228.0 1.3 compare_convert_fusion.6
  242.5 10.2 %select_add_fusion.2 = f32[4,448,1024]{2,1,0:T(8,128)} fusion(f32[4,448,1024]{2,1,0:T(8,128)} %get-tuple-element.175, pred[]{:T(512)S(6)} %compare.9, f32[1,48,1024]{2,1,0:T(8,128)S(1)} %get-tuple-element.150, f32[1,48,1024]{2,1,0:T(8,128)S(1)} %get-tuple-element.151, f32[1,48,1024]{2,1,0:T(8,128)S(1)} %get-tuple-element.152, ...), kind=kOutput, calls=%fused_computation.2.clone.1 | convolution fusion | flops 1061482496 | bytes 15810561 | tf_op jit(solution)/shard_map/while/body/eval_jaxpr/ecd,ecf->edf/dot_general | solution.py:44
  253.0 2.6 sort.19
  256.3 1.3 compare_convert_fusion.6
  270.8 10.2 %select_add_fusion.2 = f32[4,448,1024]{2,1,0:T(8,128)} fusion(f32[4,448,1024]{2,1,0:T(8,128)} %get-tuple-element.175, pred[]{:T(512)S(6)} %compare.9, f32[1,48,1024]{2,1,0:T(8,128)S(1)} %get-tuple-element.150, f32[1,48,1024]{2,1,0:T(8,128)S(1)} %get-tuple-element.151, f32[1,48,1024]{2,1,0:T(8,128)S(1)} %get-tuple-element.152, ...), kind=kOutput, calls=%fused_computation.2.clone.1 | convolution fusion | flops 1061482496 | bytes 15810561 | tf_op jit(solution)/shard_map/while/body/eval_jaxpr/ecd,ecf->edf/dot_general | solution.py:44
  281.4 2.6 sort.19
  284.6 1.3 compare_convert_fusion.6
  285.9 1.2 compare_convert_fusion.7
  299.2 10.2 %select_add_fusion.2 = f32[4,448,1024]{2,1,0:T(8,128)} fusion(f32[4,448,1024]{2,1,0:T(8,128)} %get-tuple-element.175, pred[]{:T(512)S(6)} %compare.9, f32[1,48,1024]{2,1,0:T(8,128)S(1)} %get-tuple-element.150, f32[1,48,1024]{2,1,0:T(8,128)S(1)} %get-tuple-element.151, f32[1,48,1024]{2,1,0:T(8,128)S(1)} %get-tuple-element.152, ...), kind=kOutput, calls=%fused_computation.2.clone.1 | convolution fusion | flops 1061482496 | bytes 15810561 | tf_op jit(solution)/shard_map/while/body/eval_jaxpr/ecd,ecf->edf/dot_general | solution.py:44
  309.7 2.6 sort.19
  313.0 1.3 compare_convert_fusion.6
  327.5 10.2 %select_add_fusion.2 = f32[4,448,1024]{2,1,0:T(8,128)} fusion(f32[4,448,1024]{2,1,0:T(8,128)} %get-tuple-element.175, pred[]{:T(512)S(6)} %compare.9, f32[1,48,1024]{2,1,0:T(8,128)S(1)} %get-tuple-element.150, f32[1,48,1024]{2,1,0:T(8,128)S(1)} %get-tuple-element.151, f32[1,48,1024]{2,1,0:T(8,128)S(1)} %get-tuple-element.152, ...), kind=kOutput, calls=%fused_computation.2.clone.1 | convolution fusion | flops 1061482496 | bytes 15810561 | tf_op jit(solution)/shard_map/while/body/eval_jaxpr/ecd,ecf->edf/dot_general | solution.py:44
  338.1 2.6 sort.19
  341.3 1.3 compare_convert_fusion.6
  355.9 10.2 %select_add_fusion.2 = f32[4,448,1024]{2,1,0:T(8,128)} fusion(f32[4,448,1024]{2,1,0:T(8,128)} %get-tuple-element.175, pred[]{:T(512)S(6)} %compare.9, f32[1,48,1024]{2,1,0:T(8,128)S(1)} %get-tuple-element.150, f32[1,48,1024]{2,1,0:T(8,128)S(1)} %get-tuple-element.151, f32[1,48,1024]{2,1,0:T(8,128)S(1)} %get-tuple-element.152, ...), kind=kOutput, calls=%fused_computation.2.clone.1 | convolution fusion | flops 1061482496 | bytes 15810561 | tf_op jit(solution)/shard_map/while/body/eval_jaxpr/ecd,ecf->edf/dot_general | solution.py:44
  366.4 2.6 sort.19
  369.7 1.3 compare_convert_fusion.6
  384.2 10.2 %select_add_fusion.2 = f32[4,448,1024]{2,1,0:T(8,128)} fusion(f32[4,448,1024]{2,1,0:T(8,128)} %get-tuple-element.175, pred[]{:T(512)S(6)} %compare.9, f32[1,48,1024]{2,1,0:T(8,128)S(1)} %get-tuple-element.150, f32[1,48,1024]{2,1,0:T(8,128)S(1)} %get-tuple-element.151, f32[1,48,1024]{2,1,0:T(8,128)S(1)} %get-tuple-element.152, ...), kind=kOutput, calls=%fused_computation.2.clone.1 | convolution fusion | flops 1061482496 | bytes 15810561 | tf_op jit(solution)/shard_map/while/body/eval_jaxpr/ecd,ecf->edf/dot_general | solution.py:44
  394.8 2.6 sort.19
  398.0 1.3 compare_convert_fusion.6
  399.3 1.2 compare_convert_fusion.7
  412.5 10.2 %select_add_fusion.2 = f32[4,448,1024]{2,1,0:T(8,128)} fusion(f32[4,448,1024]{2,1,0:T(8,128)} %get-tuple-element.175, pred[]{:T(512)S(6)} %compare.9, f32[1,48,1024]{2,1,0:T(8,128)S(1)} %get-tuple-element.150, f32[1,48,1024]{2,1,0:T(8,128)S(1)} %get-tuple-element.151, f32[1,48,1024]{2,1,0:T(8,128)S(1)} %get-tuple-element.152, ...), kind=kOutput, calls=%fused_computation.2.clone.1 | convolution fusion | flops 1061482496 | bytes 15810561 | tf_op jit(solution)/shard_map/while/body/eval_jaxpr/ecd,ecf->edf/dot_general | solution.py:44
  423.1 2.6 sort.19
  426.3 1.3 compare_convert_fusion.6
  440.9 10.2 %select_add_fusion.2 = f32[4,448,1024]{2,1,0:T(8,128)} fusion(f32[4,448,1024]{2,1,0:T(8,128)} %get-tuple-element.175, pred[]{:T(512)S(6)} %compare.9, f32[1,48,1024]{2,1,0:T(8,128)S(1)} %get-tuple-element.150, f32[1,48,1024]{2,1,0:T(8,128)S(1)} %get-tuple-element.151, f32[1,48,1024]{2,1,0:T(8,128)S(1)} %get-tuple-element.152, ...), kind=kOutput, calls=%fused_computation.2.clone.1 | convolution fusion | flops 1061482496 | bytes 15810561 | tf_op jit(solution)/shard_map/while/body/eval_jaxpr/ecd,ecf->edf/dot_general | solution.py:44
  451.4 2.6 sort.19
  454.7 1.3 compare_convert_fusion.6
  469.2 10.2 %select_add_fusion.2 = f32[4,448,1024]{2,1,0:T(8,128)} fusion(f32[4,448,1024]{2,1,0:T(8,128)} %get-tuple-element.175, pred[]{:T(512)S(6)} %compare.9, f32[1,48,1024]{2,1,0:T(8,128)S(1)} %get-tuple-element.150, f32[1,48,1024]{2,1,0:T(8,128)S(1)} %get-tuple-element.151, f32[1,48,1024]{2,1,0:T(8,128)S(1)} %get-tuple-element.152, ...), kind=kOutput, calls=%fused_computation.2.clone.1 | convolution fusion | flops 1061482496 | bytes 15810561 | tf_op jit(solution)/shard_map/while/body/eval_jaxpr/ecd,ecf->edf/dot_general | solution.py:44
  479.8 2.6 sort.19
  483.0 1.3 compare_convert_fusion.6
  497.6 10.2 %select_add_fusion.2 = f32[4,448,1024]{2,1,0:T(8,128)} fusion(f32[4,448,1024]{2,1,0:T(8,128)} %get-tuple-element.175, pred[]{:T(512)S(6)} %compare.9, f32[1,48,1024]{2,1,0:T(8,128)S(1)} %get-tuple-element.150, f32[1,48,1024]{2,1,0:T(8,128)S(1)} %get-tuple-element.151, f32[1,48,1024]{2,1,0:T(8,128)S(1)} %get-tuple-element.152, ...), kind=kOutput, calls=%fused_computation.2.clone.1 | convolution fusion | flops 1061482496 | bytes 15810561 | tf_op jit(solution)/shard_map/while/body/eval_jaxpr/ecd,ecf->edf/dot_general | solution.py:44
  508.1 2.6 sort.19
  511.4 1.3 compare_convert_fusion.6
  525.9 10.2 %select_add_fusion.2 = f32[4,448,1024]{2,1,0:T(8,128)} fusion(f32[4,448,1024]{2,1,0:T(8,128)} %get-tuple-element.175, pred[]{:T(512)S(6)} %compare.9, f32[1,48,1024]{2,1,0:T(8,128)S(1)} %get-tuple-element.150, f32[1,48,1024]{2,1,0:T(8,128)S(1)} %get-tuple-element.151, f32[1,48,1024]{2,1,0:T(8,128)S(1)} %get-tuple-element.152, ...), kind=kOutput, calls=%fused_computation.2.clone.1 | convolution fusion | flops 1061482496 | bytes 15810561 | tf_op jit(solution)/shard_map/while/body/eval_jaxpr/ecd,ecf->edf/dot_general | solution.py:44
  536.1 3.8 reduce_sum.36
  539.9 46.0 %psum.7 = f32[4]{0:T(128)S(1)} all-reduce(f32[4]{0:T(128)S(1)} %reduce_sum.36), channel_id=1, replica_groups=mesh['layer'=2,'tok'=16] {'tok'}, use_global_device_ids=true, to_apply=%region_6.7 | all-reduce | flops 4 | bytes 32 | tf_op jit(solution)/shard_map/psum | solution.py:71
  586.0 7.8 %fusion.28 = (f32[448,1024]{1,0:T(8,128)S(1)}, f32[448,1024]{1,0:T(8,128)S(1)}, f32[4,448,1024]{2,1,0:T(8,128)}) fusion(bf16[4,448,1024]{2,1,0:T(8,128)(2,1)} %param.9, f32[4,448,1024]{2,1,0:T(8,128)} %get-tuple-element.30, f32[4]{0:T(128)S(1)} %multiply_add_fusion), kind=kLoop, calls=%fused_computation.56 | loop fusion | flops 8257536 | bytes 22020112 | tf_op jit(solution)/shard_map/reduce_sum | solution.py:75
  593.7 1.3 divide_convert_fusion
  (273 shorter events, 100.9 us)
Async XLA Ops:
  7.2 77.5 %all-gather.2.cloned.1.call-start = ((), (), s32[]{:S(2)}) async-start(), calls=%async_computation.1 | async-start | bytes 4456448 | tf_op jit(solution)/shard_map/all_gather | solution.py:57
  7.9 11.3 %copy-start = (s32[128,1]{0,1:T(1,128)S(1)}, s32[128,1]{0,1:T(1,128)}, u32[]{:S(2)}) copy-start(s32[128,1]{0,1:T(1,128)} %param.8) | copy-start | bytes 1540
  11.8 66.1 %all-to-all-start = ((bf16[128,16,448]{0,2,1:T(8,128)(2,1)}), bf16[128,16,448]{0,2,1:T(8,128)(2,1)S(1)}, u32[]{:S(2)}, u32[]{:S(2)}) async-start(bf16[128,16,448]{0,2,1:T(8,128)(2,1)} %bitcast), calls=%async_computation | async-start | bytes 3670016 | tf_op jit(solution)/shard_map/all_to_all | solution.py:53
Sparse Core Ops, SparseCore 0:
  10.2 74.4 all-gather.1
where the time goes:
time: 605 us; the launch traced here: 602 us
  matrix products  162 us (27%)
  loops' own time  120 us (20%)
  other arithmetic  119 us (20%)
  blocking collectives  105 us (17%)
  local copies, waits for them, and re-layouts  69.6 us (12%)
  between operations  14.1 us (2%)
  starting transfers between devices  7.42 us (1%)
    dot_general x16, matrix products, add_block(): jnp.einsum('ecd,ecf->edf', left_rows, right_rows, precision=lax.Precision...  162 us
    another operation x1, loops' own time, local(): running, ignored = lax.scan(advance, running, stacked)  120 us
    all_gather x1, blocking collectives, local(): route_piece = lax.all_gather(routing, 'tok', axis=0, tiled=True)  58.7 us
    psum x1, blocking collectives, local(): totals = lax.psum(jnp.sum(running, axis=(1, 2)), 'tok')  46 us
    sort x16, other arithmetic, slot_rows(): ranking = jnp.argsort(labels, stable=True)  41.5 us
    convert_element_type x32, other arithmetic, slot_rows(): live_mask = (slot_ids < counts[expert]).astype(jnp.float32)  39.7 us
    dynamic_slice x32, local copies, waits for them, and re-layouts, local(): running, ignored = lax.scan(advance, running, stacked)  17.4 us
    square x16, other arithmetic, add_block(): grad_sq = jnp.square(grad_block.astype(jnp.float32))  16 us
  transfers between devices with their start and end apart: 2, of which 1 were waited for; matrix products, arithmetic and copies ran while one was open for 1% of the time, Pallas kernels for 0%

commit v1 on v0

v1 whole, which is shorter than its diff:
```python
import functools

import jax
import jax.numpy as jnp
from jax import lax
from jax.experimental import pallas as pl
from jax.experimental.pallas import tpu as pltpu
from jax.sharding import PartitionSpec as P

D = 7168
F = 1024
CAP = 48
EPSILON = 1e-06
GROUP = 8
TILE = 256


def summary_kernel(experts, cap, tok_ref, grad_ref, route_ref, out_ref):
    rows, width = tok_ref.shape
    member = (route_ref[...] == lax.broadcasted_iota(jnp.int32, (rows, 128), 1)).astype(jnp.float32)
    row_at = lax.broadcasted_iota(jnp.int32, (rows, rows), 0)
    col_at = lax.broadcasted_iota(jnp.int32, (rows, rows), 1)
    earlier = (col_at < row_at).astype(jnp.bfloat16)
    rank = jnp.dot(earlier, member.astype(jnp.bfloat16), preferred_element_type=jnp.float32)
    rank = jnp.sum(member * rank, axis=1, keepdims=True)
    slot = route_ref[...].astype(jnp.float32) * cap + rank
    tok = jnp.zeros((rows, 128), jnp.float32)
    for start in range(0, width, 128):
        tok = tok + jnp.square(tok_ref[:, start : start + 128].astype(jnp.float32))
    grad = jnp.zeros((rows, 128), jnp.float32)
    for start in range(0, grad_ref.shape[1], 128):
        grad = grad + jnp.square(grad_ref[:, start : start + 128].astype(jnp.float32))
    mass = jnp.sum(tok, axis=1, keepdims=True) * jnp.sum(grad, axis=1, keepdims=True)
    out_ref[...] = jnp.zeros_like(out_ref)
    out_ref[0:1, :] = jnp.sum(jnp.where(row_at == col_at, slot, 0.0), axis=0, keepdims=True)
    out_ref[1:2, :] = jnp.sum(member * mass, axis=0, keepdims=True)


def left_kernel(experts, cap, cols_ref, slot_ref, hi_ref, lo_ref):
    group, depth, rows = cols_ref.shape
    span = group * cap
    columns = jnp.concatenate([cols_ref[b] for b in range(group)], axis=1)
    lane = lax.broadcasted_iota(jnp.int32, (rows, span), 1).astype(jnp.float32)
    for expert in range(experts):
        picks = []
        for b in range(group):
            at = slot_ref[0, :, b : b + 1] - float(expert * cap)
            at = jnp.where((at >= 0.0) & (at < float(cap)), at + float(b * cap), -1.0)
            picks.append((at == lane).astype(jnp.bfloat16))
        placed = jnp.dot(columns, jnp.concatenate(picks, axis=0), preferred_element_type=jnp.float32)
        square = placed * placed
        hi = square.astype(jnp.bfloat16)
        hi_ref[expert] = hi
        lo_ref[expert] = (square - hi.astype(jnp.float32)).astype(jnp.bfloat16)


def merge_kernel(
    experts, cap, rows, scale_ref, slot_ref, hi_ref, lo_ref, grad_ref, weight_ref,
    fisher_ref, merged_ref, pick, right_hi, right_lo,
):
    blocks = slot_ref.shape[0]
    span = experts * cap

    @pl.when(pl.program_id(0) == 0)
    def _():
        at = lax.broadcasted_iota(jnp.int32, (span, rows), 0).astype(jnp.float32)
        for b in range(blocks):
            pick[b] = (slot_ref[b : b + 1, :] == at).astype(jnp.bfloat16)

    for b in range(blocks):
        placed = jnp.dot(
            pick[b], grad_ref[b * rows : (b + 1) * rows, :], preferred_element_type=jnp.float32
        )
        square = placed * placed
        hi = square.astype(jnp.bfloat16)
        lo = (square - hi.astype(jnp.float32)).astype(jnp.bfloat16)
        for expert in range(experts):
            right_hi[expert, b * cap : (b + 1) * cap, :] = hi[expert * cap : (expert + 1) * cap, :]
            right_lo[expert, b * cap : (b + 1) * cap, :] = lo[expert * cap : (expert + 1) * cap, :]

    dot = functools.partial(jnp.dot, preferred_element_type=jnp.float32)
    top = None
    bottom = None
    for expert in range(experts):
        raw = dot(hi_ref[expert], right_hi[expert])
        raw = raw + dot(hi_ref[expert], right_lo[expert])
        raw = raw + dot(lo_ref[expert], right_hi[expert])
        fisher = raw * scale_ref[expert]
        fisher_ref[expert] = fisher
        part = fisher * weight_ref[expert].astype(jnp.float32)
        top = part if top is None else top + part
        bottom = fisher if bottom is None else bottom + fisher
    merged_ref[...] = (top / (bottom + EPSILON)).astype(jnp.bfloat16)


def local(parts, tokens, out_grads, routing, weights):
    rows, width = tokens.shape
    experts, depth, hidden = weights.shape
    cap = min(rows, CAP)
    span = parts * cap
    gathered = lax.all_gather(out_grads, "tok", axis=0, tiled=True)
    turned = tokens.T.reshape(parts, depth, rows)
    columns = lax.all_to_all(turned, "tok", split_axis=0, concat_axis=0, tiled=True)

    summary = pl.pallas_call(
        functools.partial(summary_kernel, experts, cap),
        out_shape=jax.ShapeDtypeStruct((8, 128), jnp.float32),
        name="summary",
    )(tokens, out_grads, routing)
    summaries = lax.all_gather(summary[:2], "tok", axis=0)
    slots = summaries[:, 0, :]
    totals = jnp.sum(summaries[:, 1, :experts], axis=0)
    scale = 1.0 / (totals / (width * hidden) + EPSILON)

    groups = parts // GROUP
    left_hi, left_lo = pl.pallas_call(
        functools.partial(left_kernel, experts, cap),
        grid=(groups,),
        in_specs=[
            pl.BlockSpec((GROUP, depth, rows), lambda g: (g, 0, 0)),
            pl.BlockSpec((1, rows, GROUP), lambda g: (g, 0, 0)),
        ],
        out_specs=[pl.BlockSpec((experts, depth, GROUP * cap), lambda g: (0, 0, g))] * 2,
        out_shape=[jax.ShapeDtypeStruct((experts, depth, span), jnp.bfloat16)] * 2,
        compiler_params=pltpu.CompilerParams(vmem_limit_bytes=48 * 2**20),
        name="left",
    )(columns, jnp.swapaxes(slots.reshape(groups, GROUP, rows), 1, 2))

    whole = lambda *shape: pl.BlockSpec(shape, lambda f: (0,) * len(shape))
    fisher, merged = pl.pallas_call(
        functools.partial(merge_kernel, experts, cap, rows),
        grid=(hidden // TILE,),
        in_specs=[
            pl.BlockSpec(memory_space=pltpu.SMEM),
            whole(parts, rows),
            whole(experts, depth, span),
            whole(experts, depth, span),
            pl.BlockSpec((parts * rows, TILE), lambda f: (0, f)),
            pl.BlockSpec((experts, depth, TILE), lambda f: (0, 0, f)),
        ],
        out_specs=[
            pl.BlockSpec((experts, depth, TILE), lambda f: (0, 0, f)),
            pl.BlockSpec((depth, TILE), lambda f: (0, f)),
        ],
        out_shape=[
            jax.ShapeDtypeStruct((experts, depth, hidden), jnp.float32),
            jax.ShapeDtypeStruct((depth, hidden), jnp.bfloat16),
        ],
        scratch_shapes=[
            pltpu.VMEM((parts, experts * cap, rows), jnp.bfloat16),
            pltpu.VMEM((experts, span, TILE), jnp.bfloat16),
            pltpu.VMEM((experts, span, TILE), jnp.bfloat16),
        ],
        compiler_params=pltpu.CompilerParams(vmem_limit_bytes=48 * 2**20),
        name="merge",
    )(scale, slots, left_hi, left_lo, gathered, weights)
    return (fisher, merged)


def solution(mesh):
    in_specs = (
        P(("layer", "tok"), None),
        P(("layer", "tok"), None),
        P(("layer", "tok"), None),
        P("layer", "tok", None),
    )
    out_specs = (P("layer", "tok", None), P(("layer", "tok"), None))
    body = functools.partial(local, mesh.shape["tok"])
    return jax.shard_map(body, mesh=mesh, in_specs=in_specs, out_specs=out_specs, check_vma=False)
```

time: 605 us -> 128 us (0.21)
  the two profiles are of different devices: /device:TPU:0 before, /device:TPU:13 now
where the time goes in v1:
time: 128 us; the launch traced here: 127 us
  blocking collectives  72.2 us (56%)
  Pallas kernels  22.9 us (18%)
  between operations  14.1 us (11%)
  local copies, waits for them, and re-layouts  10.5 us (8%)
  starting transfers between devices  6.72 us (5%)
    all_gather x1, blocking collectives, local(): summaries = lax.all_gather(summary[:2], 'tok', axis=0)  72.2 us
    pallas_call x1, Pallas kernels, local(): pl.pallas_call(functools.partial(merge_kernel, experts, cap, rows), grid=...  14.3 us
    all_to_all x1, starting transfers between devices, local(): lax.all_to_all(turned, 'tok', split_axis=0, concat_axis=0, tiled=True)  6.69 us
    unnamed x10, local copies, waits for them, and re-layouts  6.54 us
    pallas_call x1, Pallas kernels, local(): pl.pallas_call(functools.partial(left_kernel, experts, cap), grid=(groups...  5.76 us
    transpose x1, local copies, waits for them, and re-layouts, local(): turned = tokens.T.reshape(parts, depth, rows)  3.88 us
    pallas_call x1, Pallas kernels, local(): pl.pallas_call(functools.partial(summary_kernel, experts, cap), out_shape...  2.84 us
  transfers between devices with their start and end apart: 2, of which 0 were waited for; matrix products, arithmetic and copies ran while one was open for 4% of the time, Pallas kernels for 7%

profile of v1, /device:TPU:13, one launch (start us, length us, event | category | flops | bytes accessed | tf_op | source)
XLA Modules:
  0.0 127.1 jit_solution(7067617556700047471)
XLA Ops:
  7.2 0.0 all-gather.4.cloned.1.call-start
  7.2 0.7 all-gather.4.cloned.1.call-update
  7.9 3.9 %copy.11 = bf16[7168,128]{1,0:T(8,128)(2,1)} copy(bf16[7168,128]{0,1:T(8,128)(2,1)} %bitcast.14) | data formatting | bytes 3670016 | tf_op jit(solution)/shard_map/transpose | solution.py:102
  11.8 0.0 copy-start.3
  11.8 6.7 %all-to-all-start = ((bf16[16,448,128]{2,1,0:T(8,128)(2,1)}), bf16[16,448,128]{2,1,0:T(8,128)(2,1)S(1)}, u32[]{:S(2)}, u32[]{:S(2)}) async-start(bf16[16,448,128]{2,1,0:T(8,128)(2,1)} %bitcast.13), calls=%async_computation | async-start | bytes 3670016 | tf_op jit(solution)/shard_map/all_to_all | solution.py:103
  18.5 0.0 copy-done.3
  18.5 0.7 copy.9.route_ref
  19.2 2.8 %summary.1 = f32[8,128]{1,0:T(8,128)} custom-call(bf16[128,7168]{1,0:T(8,128)(2,1)} %tok_ref.1, bf16[128,1024]{1,0:T(8,128)(2,1)} %grad_ref.1, s32[128,1]{1,0:T(8,128)} %copy.9.route_ref), custom_call_target="tpu_custom_call" | custom-call | tf_op jit(solution)/shard_map/summary/pallas_call | solution.py:105
  22.1 0.7 slice_bitcast_fusion
  22.7 72.2 %all-gather.1 = f32[16,2,128]{2,1,0:T(2,128)S(1)} all-gather(f32[1,2,128]{2,1,0:T(2,128)S(1)} %slice_bitcast_fusion), channel_id=2, replica_groups=mesh['layer'=2,'tok'=16] {'tok'}, dimensions={0}, use_global_device_ids=true | all-gather | bytes 17408 | tf_op jit(solution)/shard_map/all_gather | solution.py:110
  94.9 0.1 copy.12
  95.1 0.0 all-to-all-done.cols_ref
  95.1 5.8 %left.1 = (bf16[4,448,768]{2,1,0:T(8,128)(2,1)S(1)}, bf16[4,448,768]{2,1,0:T(8,128)(2,1)}) custom-call(bf16[16,448,128]{2,1,0:T(8,128)(2,1)S(1)} %all-to-all-done.cols_ref, f32[2,128,8]{2,1,0:T(8,128)S(1)} %bitcast.10), custom_call_target="tpu_custom_call" | custom-call | tf_op jit(solution)/shard_map/left/pallas_call | solution.py:116
  100.9 0.0 copy-start
  100.9 1.6 %copy-done = bf16[4,448,768]{2,1,0:T(8,128)(2,1)} copy-done((bf16[4,448,768]{2,1,0:T(8,128)(2,1)}, bf16[4,448,768]{2,1,0:T(8,128)(2,1)S(1)}, u32[]{:S(2)}) %copy-start) | copy-done | bytes 2752536
  102.4 0.0 all-gather.4.cloned.1.call-done.grad_ref
  102.4 0.0 copy-start.1
  102.4 1.8 %copy-done.1 = bf16[4,448,768]{2,1,0:T(8,128)(2,1)S(1)} copy-done((bf16[4,448,768]{2,1,0:T(8,128)(2,1)S(1)}, bf16[4,448,768]{2,1,0:T(8,128)(2,1)}, u32[]{:S(2)}) %copy-start.1) | copy-done | bytes 2752536
  104.2 0.0 copy-start.2
  104.2 1.8 %copy-done.2 = bf16[4,448,768]{2,1,0:T(8,128)(2,1)S(1)} copy-done((bf16[4,448,768]{2,1,0:T(8,128)(2,1)S(1)}, bf16[4,448,768]{2,1,0:T(8,128)(2,1)}, u32[]{:S(2)}) %copy-start.2) | copy-done | bytes 2752536
  106.0 14.3 %merge.1 = (f32[4,448,1024]{2,1,0:T(8,128)}, bf16[448,1024]{1,0:T(8,128)(2,1)}) custom-call(f32[4]{0:T(128)S(1)} %add_divide_fusion.scale_ref, f32[16,128]{1,0:T(8,128)S(1)} %bitcast.12, bf16[4,448,768]{2,1,0:T(8,128)(2,1)S(1)} %copy-done.1, bf16[4,448,768]{2,1,0:T(8,128)(2,1)S(1)} %copy-done.2, bf16[2048,1024]{1,0:T(8,128)(2,1)} %all-gather.4.cloned.1.call-done.grad_ref, ...), custom_call_target="tpu_custom_call" | custom-call | tf_op jit(solution)/shard_map/merge/pallas_call | solution.py:130
  (3 shorter events, 0.1 us)
Async XLA Ops:
  7.2 95.3 %all-gather.4.cloned.1.call-start = ((), (), s32[]{:S(2)}) async-start(), calls=%async_computation.1 | async-start | bytes 4456448 | tf_op jit(solution)/shard_map/all_gather | solution.py:101
  11.8 6.7 %copy-start.3 = (s32[128,1]{0,1:T(1,128)S(1)}, s32[128,1]{0,1:T(1,128)}, u32[]{:S(2)}) copy-start(s32[128,1]{0,1:T(1,128)} %param.6) | copy-start | bytes 1540
  11.8 83.3 %all-to-all-start = ((bf16[16,448,128]{2,1,0:T(8,128)(2,1)}), bf16[16,448,128]{2,1,0:T(8,128)(2,1)S(1)}, u32[]{:S(2)}, u32[]{:S(2)}) async-start(bf16[16,448,128]{2,1,0:T(8,128)(2,1)} %bitcast.13), calls=%async_computation | async-start | bytes 3670016 | tf_op jit(solution)/shard_map/all_to_all | solution.py:103
  100.9 1.6 %copy-start = (bf16[4,448,768]{2,1,0:T(8,128)(2,1)}, bf16[4,448,768]{2,1,0:T(8,128)(2,1)S(1)}, u32[]{:S(2)}) copy-start(bf16[4,448,768]{2,1,0:T(8,128)(2,1)S(1)} %get-tuple-element.4.hi_ref) | copy-start | bytes 8257540
  102.4 1.8 %copy-start.1 = (bf16[4,448,768]{2,1,0:T(8,128)(2,1)S(1)}, bf16[4,448,768]{2,1,0:T(8,128)(2,1)}, u32[]{:S(2)}) copy-start(bf16[4,448,768]{2,1,0:T(8,128)(2,1)} %copy-done) | copy-start | bytes 8257540
  104.2 1.8 %copy-start.2 = (bf16[4,448,768]{2,1,0:T(8,128)(2,1)S(1)}, bf16[4,448,768]{2,1,0:T(8,128)(2,1)}, u32[]{:S(2)}) copy-start(bf16[4,448,768]{2,1,0:T(8,128)(2,1)} %get-tuple-element.5.lo_ref) | copy-start | bytes 8257540
Sparse Core Ops, SparseCore 0:
  10.2 72.5 all-gather.3

commit v2 on v1

v2 whole, which is shorter than its diff:
```python
import functools

import jax
import jax.numpy as jnp
from jax import lax
from jax.experimental import pallas as pl
from jax.experimental.pallas import tpu as pltpu
from jax.sharding import PartitionSpec as P

D = 7168
F = 1024
CAP = 48
EPSILON = 1e-06
TILE = 256


def parcel_kernel(experts, cap, tok_ref, grad_ref, route_ref, out_ref):
    rows, width = tok_ref.shape
    hidden = grad_ref.shape[1]
    expert_at = lax.broadcasted_iota(jnp.int32, (8, rows), 0)
    member = (route_ref[...] == expert_at).astype(jnp.float32)
    row_at = lax.broadcasted_iota(jnp.int32, (rows, rows), 0)
    col_at = lax.broadcasted_iota(jnp.int32, (rows, rows), 1)
    earlier = (row_at < col_at).astype(jnp.bfloat16)
    rank = jnp.dot(member.astype(jnp.bfloat16), earlier, preferred_element_type=jnp.float32)
    base = (expert_at * cap).astype(jnp.float32)
    slot = jnp.sum(member * (rank + base), axis=0, keepdims=True)
    tok = jnp.zeros((rows, 128), jnp.float32)
    for start in range(0, width, 128):
        tok = tok + jnp.square(tok_ref[:, start : start + 128].astype(jnp.float32))
    grad = jnp.zeros((rows, 128), jnp.float32)
    for start in range(0, hidden, 128):
        grad = grad + jnp.square(grad_ref[:, start : start + 128].astype(jnp.float32))
    mass = jnp.sum(tok, axis=1, keepdims=True) * jnp.sum(grad, axis=1, keepdims=True)
    mass = jnp.sum(jnp.where(row_at == col_at, mass, 0.0), axis=0, keepdims=True)
    total = jnp.sum(member * mass, axis=1, keepdims=True)
    high = total.astype(jnp.bfloat16).astype(jnp.float32)
    middle = (total - high).astype(jnp.bfloat16).astype(jnp.float32)
    lane = lax.broadcasted_iota(jnp.int32, (8, 128), 1)
    terms = jnp.where(lane == 0, high, jnp.where(lane == 1, middle, total - high - middle))
    note = jnp.concatenate([jnp.broadcast_to(slot, (8, rows)), terms], axis=0)
    out_ref[:rows, :] = grad_ref[...]
    out_ref[rows:, :] = jnp.zeros((16, hidden), jnp.bfloat16)
    out_ref[rows:, :128] = note.astype(jnp.bfloat16)


def split(value):
    square = value * value
    hi = square.astype(jnp.bfloat16)
    return hi, (square - hi.astype(jnp.float32)).astype(jnp.bfloat16)


def merge_kernel(
    experts, cap, order, me_ref, scale_ref, slot_ref, cols_any, weight_ref, *refs
):
    fisher_ref, merged_ref, left_hi, left_lo, right_hi, right_lo, pick, cols_ref, sem = refs[-9:]
    blocks = [ref.at[i] for ref in refs[:-9] for i in range(ref.shape[0])]
    parts, depth, rows = cols_ref.shape
    span = parts * cap

    @pl.when(pl.program_id(0) == 0)
    def _():
        me = me_ref[0]
        copy = pltpu.make_async_copy(cols_any, cols_ref, sem)
        copy.start()
        at = lax.broadcasted_iota(jnp.int32, (experts * cap, rows), 0).astype(jnp.float32)
        for place, block in enumerate(blocks):
            slot = block[rows : rows + 16, :rows].astype(jnp.float32)[0:1]
            pick[place] = (slot == at).astype(jnp.bfloat16)
        copy.wait()
        for start in range(0, span, TILE):
            first = start // cap
            last = -(-(start + TILE) // cap)
            columns = jnp.concatenate(
                [cols_ref[jnp.bitwise_xor(order[p], me)] for p in range(first, last)], axis=1
            )
            lane = lax.broadcasted_iota(jnp.int32, (rows, TILE), 1).astype(jnp.float32)
            for expert in range(experts):
                picks = []
                for p in range(first, last):
                    at = slot_ref[:, p : p + 1] - float(expert * cap)
                    real = (at >= 0.0) & (at < float(cap))
                    at = jnp.where(real, at + float(p * cap - start), -1.0)
                    picks.append((at == lane).astype(jnp.bfloat16))
                moved = jnp.dot(
                    columns, jnp.concatenate(picks, axis=0), preferred_element_type=jnp.float32
                )
                hi, lo = split(moved)
                left_hi[expert, :, start : start + TILE] = hi
                left_lo[expert, :, start : start + TILE] = lo

    for place, block in enumerate(blocks):
        moved = jnp.dot(pick[place], block[:rows, :], preferred_element_type=jnp.float32)
        hi, lo = split(moved)
        for expert in range(experts):
            own = slice(expert * cap, (expert + 1) * cap)
            at = slice(place * cap, (place + 1) * cap)
            right_hi[expert, at, :] = hi[own, :]
            right_lo[expert, at, :] = lo[own, :]

    dot = functools.partial(jnp.dot, preferred_element_type=jnp.float32)
    top = None
    bottom = None
    for expert in range(experts):
        raw = dot(left_hi[expert], right_hi[expert])
        raw = raw + dot(left_hi[expert], right_lo[expert])
        raw = raw + dot(left_lo[expert], right_hi[expert])
        fisher = raw * scale_ref[expert]
        fisher_ref[expert] = fisher
        part = fisher * weight_ref[expert].astype(jnp.float32)
        top = part if top is None else top + part
        bottom = fisher if bottom is None else bottom + fisher
    merged_ref[...] = (top / (bottom + EPSILON)).astype(jnp.bfloat16)


def local(parts, tokens, out_grads, routing, weights):
    rows, width = tokens.shape
    experts, depth, hidden = weights.shape
    cap = min(rows, CAP)
    span = parts * cap
    me = lax.axis_index("tok")

    def swap(value, flip):
        return lax.ppermute(value, "tok", [(s, s ^ flip) for s in range(parts)])

    turned = tokens.T.reshape(parts, depth, rows)
    parcel = pl.pallas_call(
        functools.partial(parcel_kernel, experts, cap),
        out_shape=jax.ShapeDtypeStruct((rows + 16, hidden), jnp.bfloat16),
        name="parcel",
    )(tokens, out_grads, routing.reshape(1, rows))

    if parts == 16:
        inward = [(s, s + 4) for s in range(4, 8)] + [(s, s - 4) for s in range(8, 12)]
        outward = [(s, s - 4) for s in range(4, 8)] + [(s, s + 4) for s in range(8, 12)]
        inner = (me // 4 == 1) | (me // 4 == 2)
        far = lax.ppermute(parcel, "tok", inward)
        near = swap(parcel, 4)
        far2 = lax.ppermute(near, "tok", inward)
        out = lax.ppermute(far, "tok", outward)
        out2 = lax.ppermute(far2, "tok", outward)
        pair = jnp.stack([parcel, near])
        across = swap(pair, 2)
        turned, pair, across, far, far2, out, out2 = lax.optimization_barrier(
            (turned, pair, across, far, far2, out, out2)
        )
        other = jnp.stack([jnp.where(inner, far, out2), jnp.where(inner, far2, out)])
        halves = [(pair, across, (0, 4)), (other, swap(other, 2), (12, 8))]
    else:
        near = swap(parcel, 4)
        pairs = [(jnp.stack([parcel, near]), (0, 4))]
        flip = 8
        while flip < parts:
            pairs = pairs + [(swap(b, flip), tuple(k ^ flip for k in ks)) for b, ks in pairs]
            flip *= 2
        halves = [(b, swap(b, 2), ks) for b, ks in pairs]
    columns = lax.all_to_all(turned, "tok", split_axis=0, concat_axis=0, tiled=True)

    order = []
    notes = []
    blocks = []
    for block, across, ks in halves:
        for b, flip in ((block, 0), (across, 2), (swap(block, 1), 1), (swap(across, 1), 3)):
            blocks.append(b)
            notes.append(b[:, rows:, :128].astype(jnp.float32))
            order += [k ^ flip for k in ks]

    notes = jnp.concatenate(notes)
    totals = jnp.sum(notes[:, 8 : 8 + experts, :3], axis=(0, 2))
    scale = 1.0 / (totals / (width * hidden) + EPSILON)
    slot_columns = notes[:, 0, :].T

    whole = lambda *shape: pl.BlockSpec(shape, lambda f: (0,) * len(shape))
    fisher, merged = pl.pallas_call(
        functools.partial(merge_kernel, experts, cap, tuple(order)),
        grid=(hidden // TILE,),
        in_specs=[
            pl.BlockSpec(memory_space=pltpu.SMEM),
            pl.BlockSpec(memory_space=pltpu.SMEM),
            whole(rows, parts),
            pl.BlockSpec(memory_space=pl.ANY),
            pl.BlockSpec((experts, depth, TILE), lambda f: (0, 0, f)),
        ]
        + [pl.BlockSpec((2, rows + 16, TILE), lambda f: (0, 0, f))] * len(blocks),
        out_specs=[
            pl.BlockSpec((experts, depth, TILE), lambda f: (0, 0, f)),
            pl.BlockSpec((depth, TILE), lambda f: (0, f)),
        ],
        out_shape=[
            jax.ShapeDtypeStruct((experts, depth, hidden), jnp.float32),
            jax.ShapeDtypeStruct((depth, hidden), jnp.bfloat16),
        ],
        scratch_shapes=[
            pltpu.VMEM((experts, depth, span), jnp.bfloat16),
            pltpu.VMEM((experts, depth, span), jnp.bfloat16),
            pltpu.VMEM((experts, span, TILE), jnp.bfloat16),
            pltpu.VMEM((experts, span, TILE), jnp.bfloat16),
            pltpu.VMEM((parts, experts * cap, rows), jnp.bfloat16),
            pltpu.VMEM((parts, depth, rows), jnp.bfloat16),
            pltpu.SemaphoreType.DMA,
        ],
        compiler_params=pltpu.CompilerParams(vmem_limit_bytes=60 * 2**20),
        name="merge",
    )(me.astype(jnp.int32)[None], scale, slot_columns, columns, weights, *blocks)
    return (fisher, merged)


def solution(mesh):
    in_specs = (
        P(("layer", "tok"), None),
        P(("layer", "tok"), None),
        P(("layer", "tok"), None),
        P("layer", "tok", None),
    )
    out_specs = (P("layer", "tok", None), P(("layer", "tok"), None))
    body = functools.partial(local, mesh.shape["tok"])
    return jax.shard_map(body, mesh=mesh, in_specs=in_specs, out_specs=out_specs, check_vma=False)
```

time: 128 us -> 101 us (0.79)
  blocking collectives: 72.2 us -> 0 us
  waiting for transfers between devices: 0.69 us -> 46.1 us
  starting transfers between devices: 6.72 us -> 23.4 us
  between operations: 14.1 us -> 0.79 us
  local copies, waits for them, and re-layouts: 10.5 us -> 5.98 us
  other arithmetic: 0.04 us -> 2.81 us
    all_gather x1 -> x0, blocking collectives: 72.2 us -> none  [local(): summaries = lax.all_gather(summary[:2], 'tok', axis=0)]
    ppermute x0 -> x11, waiting for transfers between devices: none -> 37.5 us  [the longest x7 30.9 us: swap(): return lax.ppermute(value, 'tok', [(s, s ^ flip) for s in range(parts)])]
    ppermute x0 -> x11, starting transfers between devices: none -> 14.5 us  [the longest x1 4.32 us: local(): far = lax.ppermute(parcel, 'tok', inward)]
    all_to_all x1, waiting for transfers between devices: 0.01 us -> 8.55 us  [local(): lax.all_to_all(turned, 'tok', split_axis=0, concat_axis=0, tiled=True)]
    unnamed x10 -> x28, local copies, waits for them, and re-layouts: 6.54 us -> 2.96 us
    all_to_all x1, starting transfers between devices: 6.69 us -> 8.95 us  [local(): lax.all_to_all(turned, 'tok', split_axis=0, concat_axis=0, tiled=True)]
    another operation x0 -> x3, other arithmetic: none -> 2.17 us  [the longest x2 1.15 us: local(): jnp.stack([jnp.where(inner, far, out2), jnp.where(inner, far2, out)])]
    transpose x1, local copies, waits for them, and re-layouts: 3.88 us -> 2.28 us  [local(): turned = tokens.T.reshape(parts, depth, rows)]
  transfers between devices with their start and end apart: 2 -> 12, of which waited for: 0 -> 6; matrix products, arithmetic and copies ran while one was open for 4% -> 6% of each run, Pallas kernels for 7% -> 0%
where the time goes in v2:
time: 101 us
  waiting for transfers between devices  46.1 us (46%)
  starting transfers between devices  23.4 us (23%)
  Pallas kernels  22 us (22%)
  local copies, waits for them, and re-layouts  5.98 us (6%)
  other arithmetic  2.81 us (3%)
    ppermute x7, waiting for transfers between devices, swap(): return lax.ppermute(value, 'tok', [(s, s ^ flip) for s in range(parts)])  30.9 us
    pallas_call x1, Pallas kernels, local(): pl.pallas_call(functools.partial(merge_kernel, experts, cap, tuple(order)...  19 us
    all_to_all x1, starting transfers between devices, local(): lax.all_to_all(turned, 'tok', split_axis=0, concat_axis=0, tiled=True)  8.95 us
    all_to_all x1, waiting for transfers between devices, local(): lax.all_to_all(turned, 'tok', split_axis=0, concat_axis=0, tiled=True)  8.55 us
    ppermute x1, starting transfers between devices, local(): far = lax.ppermute(parcel, 'tok', inward)  4.32 us
    ppermute x1, waiting for transfers between devices, local(): out2 = lax.ppermute(far2, 'tok', outward)  4.18 us
    ppermute x1, starting transfers between devices, local(): far2 = lax.ppermute(near, 'tok', inward)  3.19 us
    pallas_call x1, Pallas kernels, local(): pl.pallas_call(functools.partial(parcel_kernel, experts, cap), out_shape=...  3.02 us
  transfers between devices with their start and end apart: 12, of which 6 were waited for; matrix products, arithmetic and copies ran while one was open for 6% of the time, Pallas kernels for 0%

profile of v2, /device:TPU:13, one launch (start us, length us, event | category | flops | bytes accessed | tf_op | source)
XLA Modules:
  0.0 101.1 jit_solution(5667823796462855946)
XLA Ops:
  0.6 0.0 copy-start
  0.6 3.0 %parcel.1 = bf16[144,1024]{1,0:T(8,128)(2,1)} custom-call(bf16[128,7168]{1,0:T(8,128)(2,1)} %tok_ref.1, bf16[128,1024]{1,0:T(8,128)(2,1)} %grad_ref.1, s32[1,128]{1,0:T(1,128)} %bitcast.17), custom_call_target="tpu_custom_call" | custom-call | tf_op jit(solution)/shard_map/parcel/pallas_call | solution.py:127
  3.7 0.2 collective-permute-start
  3.8 4.3 %collective-permute-start.2 = (bf16[144,1024]{1,0:T(8,128)(2,1)}, bf16[144,1024]{1,0:T(8,128)(2,1)S(1)}, u32[]{:S(2)}, u32[]{:S(2)}) collective-permute-start(bf16[144,1024]{1,0:T(8,128)(2,1)} %parcel.1), channel_id=1, source_target_pairs={{4,8},{5,9},{6,10},{7,11},{8,4},{9,5},{10,6},{11,7},{20,24},{21,25... | collective-permute-start | bytes 884744 | tf_op jit(solution)/shard_map/ppermute | solution.py:137
  8.2 3.6 %collective-permute-done = bf16[144,1024]{1,0:T(8,128)(2,1)S(1)} collective-permute-done((bf16[144,1024]{1,0:T(8,128)(2,1)}, bf16[144,1024]{1,0:T(8,128)(2,1)S(1)}, u32[]{:S(2)}, u32[]{:S(2)}) %collective-permute-start) | collective-permute-done | bytes 294944 | tf_op jit(solution)/shard_map/ppermute | solution.py:124
  11.8 3.2 %collective-permute-start.3 = (bf16[144,1024]{1,0:T(8,128)(2,1)S(1)}, bf16[144,1024]{1,0:T(8,128)(2,1)}, u32[]{:S(2)}, u32[]{:S(2)}) collective-permute-start(bf16[144,1024]{1,0:T(8,128)(2,1)S(1)} %collective-permute-done), channel_id=1, source_target_pairs={{4,8},{5,9},{6,10},{7,11},{8,4},{9,5},{10,6},{11,7},{20,24},{21,25... | collective-permute-start | bytes 884744 | tf_op jit(solution)/shard_map/ppermute | solution.py:139
  15.0 1.0 %pad_maximum_fusion.1.refs_0_ = bf16[2,144,1024]{2,1,0:T(8,128)(2,1)S(1)} fusion(bf16[1,144,1024]{2,1,0:T(8,128)(2,1)S(1)} %bitcast.15, bf16[1,144,1024]{2,1,0:T(8,128)(2,1)} %bitcast.14), kind=kLoop, calls=%fused_computation.3 | loop fusion | flops 294912 | bytes 1179648 | tf_op jit(solution)/shard_map/stack | solution.py:142
  16.0 0.0 copy-start.2
  16.0 0.3 collective-permute-start.1
  16.3 0.0 collective-permute-done.2
  16.3 2.0 %collective-permute-start.4 = (bf16[144,1024]{1,0:T(8,128)(2,1)S(1)}, bf16[144,1024]{1,0:T(8,128)(2,1)}, u32[]{:S(2)}, u32[]{:S(2)}) collective-permute-start(bf16[144,1024]{1,0:T(8,128)(2,1)S(1)} %collective-permute-done.2), channel_id=1, source_target_pairs={{4,0},{5,1},{6,2},{7,3},{8,12},{9,13},{10,14},{11,15},{20,16},{21,... | collective-permute-start | bytes 884744 | tf_op jit(solution)/shard_map/ppermute | solution.py:140
  18.3 2.4 %collective-permute-done.3 = bf16[144,1024]{1,0:T(8,128)(2,1)} collective-permute-done((bf16[144,1024]{1,0:T(8,128)(2,1)S(1)}, bf16[144,1024]{1,0:T(8,128)(2,1)}, u32[]{:S(2)}, u32[]{:S(2)}) %collective-permute-start.3) | collective-permute-done | bytes 294944 | tf_op jit(solution)/shard_map/ppermute | solution.py:139
  20.7 2.0 %collective-permute-start.5 = (bf16[144,1024]{1,0:T(8,128)(2,1)}, bf16[144,1024]{1,0:T(8,128)(2,1)}, u32[]{:S(2)}, u32[]{:S(2)}) collective-permute-start(bf16[144,1024]{1,0:T(8,128)(2,1)} %collective-permute-done.3), channel_id=1, source_target_pairs={{4,0},{5,1},{6,2},{7,3},{8,12},{9,13},{10,14},{11,15},{20,16},{21,... | collective-permute-start | bytes 884744 | tf_op jit(solution)/shard_map/ppermute | solution.py:141
  22.7 0.0 copy-done
  22.7 2.3 %copy.6 = bf16[7168,128]{1,0:T(8,128)(2,1)} copy(bf16[7168,128]{0,1:T(8,128)(2,1)S(1)} %bitcast.13) | data formatting | bytes 3670016 | tf_op jit(solution)/shard_map/transpose | solution.py:126
  25.0 0.0 collective-permute-done.4
  25.0 4.2 %collective-permute-done.5 = bf16[144,1024]{1,0:T(8,128)(2,1)} collective-permute-done((bf16[144,1024]{1,0:T(8,128)(2,1)}, bf16[144,1024]{1,0:T(8,128)(2,1)}, u32[]{:S(2)}, u32[]{:S(2)}) %collective-permute-start.5) | collective-permute-done | bytes 294944 | tf_op jit(solution)/shard_map/ppermute | solution.py:141
  29.2 0.0 collective-permute-done.1.refs_1_
  29.2 0.0 copy-start.4
  29.2 0.8 copy-done.4
  30.0 9.0 %all-to-all-start = ((bf16[16,448,128]{2,1,0:T(8,128)(2,1)}), bf16[16,448,128]{2,1,0:T(8,128)(2,1)S(1)}, u32[]{:S(2)}, u32[]{:S(2)}) async-start(bf16[16,448,128]{2,1,0:T(8,128)(2,1)} %bitcast.2), calls=%async_computation | async-start | bytes 3670016 | tf_op jit(solution)/shard_map/all_to_all | solution.py:157
  39.0 0.0 copy-start.5
  39.0 1.1 %select_bitcast_fusion = (bf16[1,144,1024]{2,1,0:T(8,128)(2,1)S(1)}, bf16[1,144,1024]{2,1,0:T(8,128)(2,1)S(1)}) fusion(bf16[144,1024]{1,0:T(8,128)(2,1)} %collective-permute-done.3, bf16[144,1024]{1,0:T(8,128)(2,1)} %collective-permute-done.4, pred[]{:T(512)S(6)} %or.3, bf16[144,1024]{1,0:T(8,128)(2,1)S(1)} %collective-permute-done.2, ...), kind=kLoop, calls=%fused_computation.4 | loop fusion | flops 294912 | bytes 1769473 | tf_op jit(solution)/shard_map/stack | solution.py:147
  40.1 0.1 pad_maximum_fusion.refs_4_
  40.1 0.0 copy-start.3
  40.1 0.3 collective-permute-start.8
  40.5 0.6 collective-permute-start.6
  41.1 0.0 collective-permute-start.9
  41.1 0.0 copy-done.5
  41.1 0.5 collective-permute-start.7
  41.6 0.0 copy-done.2
  41.6 25.8 %collective-permute-done.8.refs_5_ = bf16[2,144,1024]{2,1,0:T(8,128)(2,1)S(1)} collective-permute-done((bf16[2,144,1024]{2,1,0:T(8,128)(2,1)S(1)}, bf16[2,144,1024]{2,1,0:T(8,128)(2,1)S(1)}, u32[]{:S(2)}, u32[]{:S(2)}) %collective-permute-start.8) | collective-permute-done | bytes 589856 | tf_op jit(solution)/shard_map/ppermute | solution.py:124
  67.5 0.0 copy-start.6
  67.5 1.0 collective-permute-start.10
  68.5 0.0 collective-permute-done.6.refs_2_
  68.5 0.0 copy-start.7
  68.5 0.0 collective-permute-done.7.refs_3_
  68.5 0.0 copy-start.9
  68.5 0.0 collective-permute-done.9.refs_6_
  68.6 0.0 copy-done.6
  68.6 0.0 copy-start.8
  68.6 1.5 %collective-permute-done.10.refs_7_ = bf16[2,144,1024]{2,1,0:T(8,128)(2,1)S(1)} collective-permute-done((bf16[2,144,1024]{2,1,0:T(8,128)(2,1)S(1)}, bf16[2,144,1024]{2,1,0:T(8,128)(2,1)S(1)}, u32[]{:S(2)}, u32[]{:S(2)}) %collective-permute-start.10) | collective-permute-done | bytes 589856 | tf_op jit(solution)/shard_map/ppermute | solution.py:124
  70.1 0.0 copy-done.7
  70.1 0.0 copy-start.10
  70.1 0.0 copy-done.8
  70.1 0.0 copy-done.9
  70.2 0.8 copy-done.10
  70.9 0.7 copy.7.slot_ref
  71.7 0.1 slice_reduce_fusion
  71.8 0.5 add_divide_fusion.scale_ref
  72.3 8.6 %all-to-all-done.cols_any = bf16[16,448,128]{2,1,0:T(8,128)(2,1)S(1)} async-done(((bf16[16,448,128]{2,1,0:T(8,128)(2,1)}), bf16[16,448,128]{2,1,0:T(8,128)(2,1)S(1)}, u32[]{:S(2)}, u32[]{:S(2)}) %all-to-all-start) | async-done | bytes 1835040 | tf_op jit(solution)/shard_map/all_to_all | solution.py:157
  80.8 0.0 copy-start.1
  80.8 0.0 copy-done.3
  80.8 1.3 %copy-done.1 = bf16[16,448,128]{2,1,0:T(8,128)(2,1)} copy-done((bf16[16,448,128]{2,1,0:T(8,128)(2,1)}, bf16[16,448,128]{2,1,0:T(8,128)(2,1)S(1)}, u32[]{:S(2)}) %copy-start.1) | copy-done | bytes 1835032
  82.1 19.0 %merge.1 = (f32[4,448,1024]{2,1,0:T(8,128)}, bf16[448,1024]{1,0:T(8,128)(2,1)}) custom-call(s32[1]{0:T(128)} %bitcast.me_ref, f32[4]{0:T(128)} %add_divide_fusion.scale_ref, f32[128,16]{1,0:T(8,128)} %copy.7.slot_ref, bf16[16,448,128]{2,1,0:T(8,128)(2,1)} %copy-done.1, bf16[4,448,1024]{2,1,0:T(8,128)(2,1)} %weight_ref.1, bf16[2,144,1024]{2,1,0:T(8,128)(2,1)} %copy-done.2, ...), custom_call_target="tpu_custom_call" | custom-call | tf_op jit(solution)/shard_map/merge/pallas_call | solution.py:174
  (10 shorter events, 0.1 us)
Async XLA Ops:
  0.6 22.1 %copy-start = (bf16[128,7168]{1,0:T(8,128)(2,1)S(1)}, bf16[128,7168]{1,0:T(8,128)(2,1)}, u32[]{:S(2)}) copy-start(bf16[128,7168]{1,0:T(8,128)(2,1)} %tok_ref.1) | copy-start | bytes 5505028
  3.7 8.1 %collective-permute-start = (bf16[144,1024]{1,0:T(8,128)(2,1)}, bf16[144,1024]{1,0:T(8,128)(2,1)S(1)}, u32[]{:S(2)}, u32[]{:S(2)}) collective-permute-start(bf16[144,1024]{1,0:T(8,128)(2,1)} %parcel.1), channel_id=1, source_target_pairs={{0,4},{1,5},{2,6},{3,7},{4,0},{5,1},{6,2},{7,3},{8,12},{9,13},{10,... | collective-permute-start | bytes 884744 | tf_op jit(solution)/shard_map/ppermute | solution.py:124
  3.8 12.4 %collective-permute-start.2 = (bf16[144,1024]{1,0:T(8,128)(2,1)}, bf16[144,1024]{1,0:T(8,128)(2,1)S(1)}, u32[]{:S(2)}, u32[]{:S(2)}) collective-permute-start(bf16[144,1024]{1,0:T(8,128)(2,1)} %parcel.1), channel_id=1, source_target_pairs={{4,8},{5,9},{6,10},{7,11},{8,4},{9,5},{10,6},{11,7},{20,24},{21,25... | collective-permute-start | bytes 884744 | tf_op jit(solution)/shard_map/ppermute | solution.py:137
  11.8 8.9 %collective-permute-start.3 = (bf16[144,1024]{1,0:T(8,128)(2,1)S(1)}, bf16[144,1024]{1,0:T(8,128)(2,1)}, u32[]{:S(2)}, u32[]{:S(2)}) collective-permute-start(bf16[144,1024]{1,0:T(8,128)(2,1)S(1)} %collective-permute-done), channel_id=1, source_target_pairs={{4,8},{5,9},{6,10},{7,11},{8,4},{9,5},{10,6},{11,7},{20,24},{21,25... | collective-permute-start | bytes 884744 | tf_op jit(solution)/shard_map/ppermute | solution.py:139
  16.0 25.7 %copy-start.2 = (bf16[2,144,1024]{2,1,0:T(8,128)(2,1)}, bf16[2,144,1024]{2,1,0:T(8,128)(2,1)S(1)}, u32[]{:S(2)}) copy-start(bf16[2,144,1024]{2,1,0:T(8,128)(2,1)S(1)} %pad_maximum_fusion.1.refs_0_) | copy-start | bytes 1769476
  16.0 13.2 %collective-permute-start.1 = (bf16[2,144,1024]{2,1,0:T(8,128)(2,1)S(1)}, bf16[2,144,1024]{2,1,0:T(8,128)(2,1)S(1)}, u32[]{:S(2)}, u32[]{:S(2)}) collective-permute-start(bf16[2,144,1024]{2,1,0:T(8,128)(2,1)S(1)} %pad_maximum_fusion.1.refs_0_), channel_id=1, source_target_pairs={{0,2},{1,3},{2,0},{3,1},{4,6},{5,7},{6,4},{7,5},{8,10},{9,11},{10,... | collective-permute-start | bytes 1769480 | tf_op jit(solution)/shard_map/ppermute | solution.py:124
  16.3 8.7 %collective-permute-start.4 = (bf16[144,1024]{1,0:T(8,128)(2,1)S(1)}, bf16[144,1024]{1,0:T(8,128)(2,1)}, u32[]{:S(2)}, u32[]{:S(2)}) collective-permute-start(bf16[144,1024]{1,0:T(8,128)(2,1)S(1)} %collective-permute-done.2), channel_id=1, source_target_pairs={{4,0},{5,1},{6,2},{7,3},{8,12},{9,13},{10,14},{11,15},{20,16},{21,... | collective-permute-start | bytes 884744 | tf_op jit(solution)/shard_map/ppermute | solution.py:140
  20.7 8.5 %collective-permute-start.5 = (bf16[144,1024]{1,0:T(8,128)(2,1)}, bf16[144,1024]{1,0:T(8,128)(2,1)}, u32[]{:S(2)}, u32[]{:S(2)}) collective-permute-start(bf16[144,1024]{1,0:T(8,128)(2,1)} %collective-permute-done.3), channel_id=1, source_target_pairs={{4,0},{5,1},{6,2},{7,3},{8,12},{9,13},{10,14},{11,15},{20,16},{21,... | collective-permute-start | bytes 884744 | tf_op jit(solution)/shard_map/ppermute | solution.py:141
  29.2 0.8 copy-start.4
  30.0 50.8 %all-to-all-start = ((bf16[16,448,128]{2,1,0:T(8,128)(2,1)}), bf16[16,448,128]{2,1,0:T(8,128)(2,1)S(1)}, u32[]{:S(2)}, u32[]{:S(2)}) async-start(bf16[16,448,128]{2,1,0:T(8,128)(2,1)} %bitcast.2), calls=%async_computation | async-start | bytes 3670016 | tf_op jit(solution)/shard_map/all_to_all | solution.py:157
  39.0 2.2 %copy-start.5 = (bf16[2,144,1024]{2,1,0:T(8,128)(2,1)S(1)}, bf16[2,144,1024]{2,1,0:T(8,128)(2,1)}, u32[]{:S(2)}) copy-start(bf16[2,144,1024]{2,1,0:T(8,128)(2,1)} %copy-done.4) | copy-start | bytes 1769476
  40.1 40.7 %copy-start.3 = (bf16[2,144,1024]{2,1,0:T(8,128)(2,1)}, bf16[2,144,1024]{2,1,0:T(8,128)(2,1)S(1)}, u32[]{:S(2)}) copy-start(bf16[2,144,1024]{2,1,0:T(8,128)(2,1)S(1)} %pad_maximum_fusion.refs_4_) | copy-start | bytes 1769476
  40.1 27.3 %collective-permute-start.8 = (bf16[2,144,1024]{2,1,0:T(8,128)(2,1)S(1)}, bf16[2,144,1024]{2,1,0:T(8,128)(2,1)S(1)}, u32[]{:S(2)}, u32[]{:S(2)}) collective-permute-start(bf16[2,144,1024]{2,1,0:T(8,128)(2,1)S(1)} %pad_maximum_fusion.refs_4_), channel_id=1, source_target_pairs={{0,2},{1,3},{2,0},{3,1},{4,6},{5,7},{6,4},{7,5},{8,10},{9,11},{10,... | collective-permute-start | bytes 1769480 | tf_op jit(solution)/shard_map/ppermute | solution.py:124
  40.5 28.0 %collective-permute-start.6 = (bf16[2,144,1024]{2,1,0:T(8,128)(2,1)S(1)}, bf16[2,144,1024]{2,1,0:T(8,128)(2,1)S(1)}, u32[]{:S(2)}, u32[]{:S(2)}) collective-permute-start(bf16[2,144,1024]{2,1,0:T(8,128)(2,1)S(1)} %pad_maximum_fusion.1.refs_0_), channel_id=1, source_target_pairs={{0,1},{1,0},{2,3},{3,2},{4,5},{5,4},{6,7},{7,6},{8,9},{9,8},{10,11... | collective-permute-start | bytes 1769480 | tf_op jit(solution)/shard_map/ppermute | solution.py:124
  41.1 27.4 %collective-permute-start.9 = (bf16[2,144,1024]{2,1,0:T(8,128)(2,1)S(1)}, bf16[2,144,1024]{2,1,0:T(8,128)(2,1)S(1)}, u32[]{:S(2)}, u32[]{:S(2)}) collective-permute-start(bf16[2,144,1024]{2,1,0:T(8,128)(2,1)S(1)} %pad_maximum_fusion.refs_4_), channel_id=1, source_target_pairs={{0,1},{1,0},{2,3},{3,2},{4,5},{5,4},{6,7},{7,6},{8,9},{9,8},{10,11... | collective-permute-start | bytes 1769480 | tf_op jit(solution)/shard_map/ppermute | solution.py:124
  41.1 27.4 %collective-permute-start.7 = (bf16[2,144,1024]{2,1,0:T(8,128)(2,1)S(1)}, bf16[2,144,1024]{2,1,0:T(8,128)(2,1)S(1)}, u32[]{:S(2)}, u32[]{:S(2)}) collective-permute-start(bf16[2,144,1024]{2,1,0:T(8,128)(2,1)S(1)} %copy-done.5), channel_id=1, source_target_pairs={{0,1},{1,0},{2,3},{3,2},{4,5},{5,4},{6,7},{7,6},{8,9},{9,8},{10,11... | collective-permute-start | bytes 1769480 | tf_op jit(solution)/shard_map/ppermute | solution.py:124
  67.5 1.1 %copy-start.6 = (bf16[2,144,1024]{2,1,0:T(8,128)(2,1)}, bf16[2,144,1024]{2,1,0:T(8,128)(2,1)S(1)}, u32[]{:S(2)}) copy-start(bf16[2,144,1024]{2,1,0:T(8,128)(2,1)S(1)} %collective-permute-done.8.refs_5_) | copy-start | bytes 1769476
  67.5 2.6 %collective-permute-start.10 = (bf16[2,144,1024]{2,1,0:T(8,128)(2,1)S(1)}, bf16[2,144,1024]{2,1,0:T(8,128)(2,1)S(1)}, u32[]{:S(2)}, u32[]{:S(2)}) collective-permute-start(bf16[2,144,1024]{2,1,0:T(8,128)(2,1)S(1)} %collective-permute-done.8.refs_5_), channel_id=1, source_target_pairs={{0,1},{1,0},{2,3},{3,2},{4,5},{5,4},{6,7},{7,6},{8,9},{9,8},{10,11... | collective-permute-start | bytes 1769480 | tf_op jit(solution)/shard_map/ppermute | solution.py:124
  68.5 1.6 %copy-start.7 = (bf16[2,144,1024]{2,1,0:T(8,128)(2,1)}, bf16[2,144,1024]{2,1,0:T(8,128)(2,1)S(1)}, u32[]{:S(2)}) copy-start(bf16[2,144,1024]{2,1,0:T(8,128)(2,1)S(1)} %collective-permute-done.6.refs_2_) | copy-start | bytes 1769476
  68.5 1.6 %copy-start.9 = (bf16[2,144,1024]{2,1,0:T(8,128)(2,1)}, bf16[2,144,1024]{2,1,0:T(8,128)(2,1)S(1)}, u32[]{:S(2)}) copy-start(bf16[2,144,1024]{2,1,0:T(8,128)(2,1)S(1)} %collective-permute-done.7.refs_3_) | copy-start | bytes 1769476
  68.6 1.5 %copy-start.8 = (bf16[2,144,1024]{2,1,0:T(8,128)(2,1)}, bf16[2,144,1024]{2,1,0:T(8,128)(2,1)S(1)}, u32[]{:S(2)}) copy-start(bf16[2,144,1024]{2,1,0:T(8,128)(2,1)S(1)} %collective-permute-done.9.refs_6_) | copy-start | bytes 1769476
  70.1 0.8 copy-start.10
  80.8 1.3 %copy-start.1 = (bf16[16,448,128]{2,1,0:T(8,128)(2,1)}, bf16[16,448,128]{2,1,0:T(8,128)(2,1)S(1)}, u32[]{:S(2)}) copy-start(bf16[16,448,128]{2,1,0:T(8,128)(2,1)S(1)} %all-to-all-done.cols_any) | copy-start | bytes 5505028

commit v3 on v2

v3 whole, which is shorter than its diff:
```python
import functools

import jax
import jax.numpy as jnp
from jax import lax
from jax.experimental import pallas as pl
from jax.experimental.pallas import tpu as pltpu
from jax.sharding import PartitionSpec as P

D = 7168
F = 1024
CAP = 48
EPSILON = 1e-06
TILE = 256


def turn_kernel(experts, cap, tok_ref, grad_ref, route_ref, turned_ref):
    rows, width = tok_ref.shape
    depth = width // turned_ref.shape[0]
    expert_at = lax.broadcasted_iota(jnp.int32, (8, rows), 0)
    member = (route_ref[...] == expert_at).astype(jnp.float32)
    row_at = lax.broadcasted_iota(jnp.int32, (rows, rows), 0)
    col_at = lax.broadcasted_iota(jnp.int32, (rows, rows), 1)
    earlier = (row_at < col_at).astype(jnp.bfloat16)
    rank = jnp.dot(member.astype(jnp.bfloat16), earlier, preferred_element_type=jnp.float32)
    base = (expert_at * cap).astype(jnp.float32)
    slot = jnp.sum(member * (rank + base), axis=0, keepdims=True)
    tok = jnp.zeros((rows, 128), jnp.float32)
    for start in range(0, width, 128):
        piece = tok_ref[:, start : start + 128]
        tok = tok + jnp.square(piece.astype(jnp.float32))
        down = piece.T
        at = start
        while at < start + 128:
            end = min(start + 128, (at // depth + 1) * depth)
            turned_ref[at // depth, at % depth : at % depth + end - at, :] = down[at - start : end - start]
            at = end
    grad = jnp.zeros((rows, 128), jnp.float32)
    for start in range(0, grad_ref.shape[1], 128):
        grad = grad + jnp.square(grad_ref[:, start : start + 128].astype(jnp.float32))
    mass = jnp.sum(tok, axis=1, keepdims=True) * jnp.sum(grad, axis=1, keepdims=True)
    mass = jnp.sum(jnp.where(row_at == col_at, mass, 0.0), axis=0, keepdims=True)
    total = jnp.sum(member * mass, axis=1, keepdims=True)
    high = total.astype(jnp.bfloat16).astype(jnp.float32)
    middle = (total - high).astype(jnp.bfloat16).astype(jnp.float32)
    lane = lax.broadcasted_iota(jnp.int32, (8, 128), 1)
    terms = jnp.where(lane == 1, middle, jnp.where(lane == 2, total - high - middle, 0.0))
    terms = jnp.where(lane == 0, high, terms)
    note = jnp.concatenate([jnp.broadcast_to(slot, (8, rows)), terms], axis=0)
    for part in range(turned_ref.shape[0]):
        turned_ref[part, depth:, :] = note.astype(jnp.bfloat16)


def split(value):
    square = value * value
    hi = square.astype(jnp.bfloat16)
    return hi, (square - hi.astype(jnp.float32)).astype(jnp.bfloat16)


def merge_kernel(experts, cap, order, count, me_ref, cols_any, weight_ref, *refs):
    fisher_ref, merged_ref, left_hi, left_lo, right_hi, right_lo = refs[-11:-5]
    pick, left_pick, scale_ref, cols_ref, sem = refs[-5:]
    blocks = [ref.at[i] for ref in refs[:-11] for i in range(ref.shape[0])]
    parts, tall, rows = cols_ref.shape
    depth = tall - 16
    span = parts * cap

    @pl.when(pl.program_id(0) == 0)
    def _():
        me = me_ref[0]
        copy = pltpu.make_async_copy(cols_any, cols_ref, sem)
        copy.start()
        copy.wait()
        at = lax.broadcasted_iota(jnp.int32, (experts * cap, rows), 0).astype(jnp.float32)
        total = jnp.zeros((8, rows), jnp.float32)
        for place in range(parts):
            note = cols_ref[jnp.bitwise_xor(order[place], me), depth:, :].astype(jnp.float32)
            pick[place] = (note[0:1] == at).astype(jnp.bfloat16)
            total = total + note[8:]
        total = jnp.sum(total, axis=1, keepdims=True)
        scale_ref[...] = jnp.broadcast_to(1.0 / (total / count + EPSILON), (8, 128))
        for start in range(0, span, TILE):
            left_pick[...] = jnp.zeros_like(left_pick)
            first = start // cap
            last = -(-(start + TILE) // cap)
            for p in range(first, last):
                low = max(p * cap, start)
                high = min((p + 1) * cap, start + TILE)
                for expert in range(experts):
                    slots = slice(low - p * cap + expert * cap, high - p * cap + expert * cap)
                    lanes = slice((p - first) * rows, (p - first + 1) * rows)
                    left_pick[expert, low - start : high - start, lanes] = pick[p, slots, :]
            columns = jnp.concatenate(
                [cols_ref[jnp.bitwise_xor(order[p], me), :depth, :] for p in range(first, last)], axis=1
            )
            for expert in range(experts):
                moved = lax.dot_general(
                    columns,
                    left_pick[expert, :, : (last - first) * rows],
                    (((1,), (1,)), ((), ())),
                    preferred_element_type=jnp.float32,
                )
                hi, lo = split(moved)
                left_hi[expert, :, start : start + TILE] = hi
                left_lo[expert, :, start : start + TILE] = lo

    for place, block in enumerate(blocks):
        moved = jnp.dot(pick[place], block[...], preferred_element_type=jnp.float32)
        hi, lo = split(moved)
        for expert in range(experts):
            own = slice(expert * cap, (expert + 1) * cap)
            at = slice(place * cap, (place + 1) * cap)
            right_hi[expert, at, :] = hi[own, :]
            right_lo[expert, at, :] = lo[own, :]

    dot = functools.partial(jnp.dot, preferred_element_type=jnp.float32)
    top = None
    bottom = None
    for expert in range(experts):
        raw = dot(left_hi[expert], right_hi[expert])
        raw = raw + dot(left_hi[expert], right_lo[expert])
        raw = raw + dot(left_lo[expert], right_hi[expert])
        fisher = raw * scale_ref[expert : expert + 1, 0:1]
        fisher_ref[expert] = fisher
        part = fisher * weight_ref[expert].astype(jnp.float32)
        top = part if top is None else top + part
        bottom = fisher if bottom is None else bottom + fisher
    merged_ref[...] = (top / (bottom + EPSILON)).astype(jnp.bfloat16)


def local(parts, tokens, out_grads, routing, weights):
    rows, width = tokens.shape
    experts, depth, hidden = weights.shape
    cap = min(rows, CAP)
    span = parts * cap
    me = lax.axis_index("tok")

    def swap(value, flip):
        return lax.ppermute(value, "tok", [(s, s ^ flip) for s in range(parts)])

    turned = pl.pallas_call(
        functools.partial(turn_kernel, experts, cap),
        out_shape=pltpu.HBM((parts, depth + 16, rows), jnp.bfloat16),
        compiler_params=pltpu.CompilerParams(vmem_limit_bytes=16 * 2**20),
        name="turn",
    )(tokens, out_grads, routing.reshape(1, rows))

    if parts == 16:
        inward = [(s, s + 4) for s in range(4, 8)] + [(s, s - 4) for s in range(8, 12)]
        outward = [(s, s - 4) for s in range(4, 8)] + [(s, s + 4) for s in range(8, 12)]
        inner = (me // 4 == 1) | (me // 4 == 2)
        far = lax.ppermute(out_grads, "tok", inward)
        near = swap(out_grads, 4)
        far2 = lax.ppermute(near, "tok", inward)
        out = lax.ppermute(far, "tok", outward)
        pair = jnp.stack([out_grads, near])
        across = swap(pair, 2)
        out2 = lax.ppermute(far2, "tok", outward)
        turned, pair, across, far, far2, out, out2 = lax.optimization_barrier(
            (turned, pair, across, far, far2, out, out2)
        )
        other = jnp.stack([jnp.where(inner, far, out2), jnp.where(inner, far2, out)])
        halves = [(pair, across, (0, 4)), (other, swap(other, 2), (12, 8))]
    else:
        near = swap(out_grads, 4)
        pairs = [(jnp.stack([out_grads, near]), (0, 4))]
        flip = 8
        while flip < parts:
            pairs = pairs + [(swap(b, flip), tuple(k ^ flip for k in ks)) for b, ks in pairs]
            flip *= 2
        halves = [(b, swap(b, 2), ks) for b, ks in pairs]
    columns = lax.all_to_all(turned, "tok", split_axis=0, concat_axis=0, tiled=True)

    order = []
    blocks = []
    for block, across, ks in halves:
        for b, flip in ((block, 0), (across, 2), (swap(block, 1), 1), (swap(across, 1), 3)):
            blocks.append(b)
            order += [k ^ flip for k in ks]

    fisher, merged = pl.pallas_call(
        functools.partial(merge_kernel, experts, cap, tuple(order), width * hidden),
        grid=(hidden // TILE,),
        in_specs=[
            pl.BlockSpec(memory_space=pltpu.SMEM),
            pl.BlockSpec(memory_space=pl.ANY),
            pl.BlockSpec((experts, depth, TILE), lambda f: (0, 0, f)),
        ]
        + [pl.BlockSpec((2, rows, TILE), lambda f: (0, 0, f))] * len(blocks),
        out_specs=[
            pl.BlockSpec((experts, depth, TILE), lambda f: (0, 0, f)),
            pl.BlockSpec((depth, TILE), lambda f: (0, f)),
        ],
        out_shape=[
            jax.ShapeDtypeStruct((experts, depth, hidden), jnp.float32),
            jax.ShapeDtypeStruct((depth, hidden), jnp.bfloat16),
        ],
        scratch_shapes=[
            pltpu.VMEM((experts, depth, span), jnp.bfloat16),
            pltpu.VMEM((experts, depth, span), jnp.bfloat16),
            pltpu.VMEM((experts, span, TILE), jnp.bfloat16),
            pltpu.VMEM((experts, span, TILE), jnp.bfloat16),
            pltpu.VMEM((parts, experts * cap, rows), jnp.bfloat16),
            pltpu.VMEM((experts, TILE, (-(-TILE // cap) + 1) * rows), jnp.bfloat16),
            pltpu.VMEM((8, 128), jnp.float32),
            pltpu.VMEM((parts, depth + 16, rows), jnp.bfloat16),
            pltpu.SemaphoreType.DMA,
        ],
        compiler_params=pltpu.CompilerParams(vmem_limit_bytes=60 * 2**20),
        name="merge",
    )(me.astype(jnp.int32)[None], columns, weights, *blocks)
    return (fisher, merged)


def solution(mesh):
    in_specs = (
        P(("layer", "tok"), None),
        P(("layer", "tok"), None),
        P(("layer", "tok"), None),
        P("layer", "tok", None),
    )
    out_specs = (P("layer", "tok", None), P(("layer", "tok"), None))
    body = functools.partial(local, mesh.shape["tok"])
    return jax.shard_map(body, mesh=mesh, in_specs=in_specs, out_specs=out_specs, check_vma=False)
```

time: 101 us -> 96.4 us (0.954)
  waiting for transfers between devices: 46.1 us -> 43.7 us
  other arithmetic: 2.81 us -> 1.11 us
  Pallas kernels: 22 us -> 20.9 us
    all_to_all x1, waiting for transfers between devices: 8.55 us -> 15.1 us  [local(): lax.all_to_all(turned, 'tok', split_axis=0, concat_axis=0, tiled=True)]
    ppermute x7, waiting for transfers between devices: 30.9 us -> 26.8 us  [swap(): return lax.ppermute(value, 'tok', [(s, s ^ flip) for s in range(parts)])]
    ppermute x1, waiting for transfers between devices: 4.18 us -> 0.13 us  [local(): out2 = lax.ppermute(far2, 'tok', outward)]
    unnamed x28 -> x22, local copies, waits for them, and re-layouts: 2.96 us -> 6.19 us
    transpose x2 -> x0, local copies, waits for them, and re-layouts: 3 us -> none  [the longest x1 2.28 us: local(): turned = tokens.T.reshape(parts, depth, rows)]
    another operation x2, other arithmetic: 1.15 us -> 0.11 us  [local(): jnp.stack([jnp.where(inner, far, out2), jnp.where(inner, far2, out)])]
  transfers between devices with their start and end apart: 12 -> 12, of which waited for: 6 -> 6; matrix products, arithmetic and copies ran while one was open for 6% -> 1% of each run, Pallas kernels for 0% -> 2%
where the time goes in v3:
time: 96.4 us; the launch traced here: 96 us
  waiting for transfers between devices  43.7 us (45%)
  starting transfers between devices  23.3 us (24%)
  Pallas kernels  20.9 us (22%)
  local copies, waits for them, and re-layouts  6.19 us (6%)
  other arithmetic  1.11 us (1%)
    ppermute x7, waiting for transfers between devices, swap(): return lax.ppermute(value, 'tok', [(s, s ^ flip) for s in range(parts)])  26.8 us
    pallas_call x1, Pallas kernels, local(): pl.pallas_call(functools.partial(merge_kernel, experts, cap, tuple(order)...  18.7 us
    all_to_all x1, waiting for transfers between devices, local(): lax.all_to_all(turned, 'tok', split_axis=0, concat_axis=0, tiled=True)  15.1 us
    all_to_all x1, starting transfers between devices, local(): lax.all_to_all(turned, 'tok', split_axis=0, concat_axis=0, tiled=True)  8.77 us
    unnamed x22, local copies, waits for them, and re-layouts  6.19 us
    ppermute x1, starting transfers between devices, local(): far = lax.ppermute(out_grads, 'tok', inward)  4.32 us
    ppermute x1, starting transfers between devices, local(): far2 = lax.ppermute(near, 'tok', inward)  3.19 us
    ppermute x7, starting transfers between devices, swap(): return lax.ppermute(value, 'tok', [(s, s ^ flip) for s in range(parts)])  3.06 us
  transfers between devices with their start and end apart: 12, of which 6 were waited for; matrix products, arithmetic and copies ran while one was open for 1% of the time, Pallas kernels for 2%

profile of v3, /device:TPU:13, one launch (start us, length us, event | category | flops | bytes accessed | tf_op | source)
XLA Modules:
  0.0 96.0 jit_solution(10534405696514057870)
XLA Ops:
  0.6 0.2 collective-permute-start
  0.9 4.3 %collective-permute-start.2 = (bf16[128,1024]{1,0:T(8,128)(2,1)}, bf16[128,1024]{1,0:T(8,128)(2,1)S(1)}, u32[]{:S(2)}, u32[]{:S(2)}) collective-permute-start(bf16[128,1024]{1,0:T(8,128)(2,1)} %grad_ref.1), channel_id=1, source_target_pairs={{4,8},{5,9},{6,10},{7,11},{8,4},{9,5},{10,6},{11,7},{20,24},{21,25... | collective-permute-start | bytes 786440 | tf_op jit(solution)/shard_map/ppermute | solution.py:152
  5.2 2.9 %collective-permute-done = bf16[128,1024]{1,0:T(8,128)(2,1)S(1)} collective-permute-done((bf16[128,1024]{1,0:T(8,128)(2,1)}, bf16[128,1024]{1,0:T(8,128)(2,1)S(1)}, u32[]{:S(2)}, u32[]{:S(2)}) %collective-permute-start) | collective-permute-done | bytes 262176 | tf_op jit(solution)/shard_map/ppermute | solution.py:139
  8.1 3.2 %collective-permute-start.3 = (bf16[128,1024]{1,0:T(8,128)(2,1)S(1)}, bf16[128,1024]{1,0:T(8,128)(2,1)S(1)}, u32[]{:S(2)}, u32[]{:S(2)}) collective-permute-start(bf16[128,1024]{1,0:T(8,128)(2,1)S(1)} %collective-permute-done), channel_id=1, source_target_pairs={{4,8},{5,9},{6,10},{7,11},{8,4},{9,5},{10,6},{11,7},{20,24},{21,25... | collective-permute-start | bytes 786440 | tf_op jit(solution)/shard_map/ppermute | solution.py:154
  11.3 1.0 %pad_maximum_fusion.refs_0_ = bf16[2,128,1024]{2,1,0:T(8,128)(2,1)S(1)} fusion(bf16[1,128,1024]{2,1,0:T(8,128)(2,1)S(1)} %bitcast.10, bf16[1,128,1024]{2,1,0:T(8,128)(2,1)} %bitcast.8), kind=kLoop, calls=%fused_computation | loop fusion | flops 262144 | bytes 1048576 | tf_op jit(solution)/shard_map/stack | solution.py:156
  12.3 0.0 copy-start.4
  12.3 0.3 collective-permute-start.1
  12.6 0.0 collective-permute-done.2
  12.6 2.0 %collective-permute-start.4 = (bf16[128,1024]{1,0:T(8,128)(2,1)S(1)}, bf16[128,1024]{1,0:T(8,128)(2,1)}, u32[]{:S(2)}, u32[]{:S(2)}) collective-permute-start(bf16[128,1024]{1,0:T(8,128)(2,1)S(1)} %collective-permute-done.2), channel_id=1, source_target_pairs={{4,0},{5,1},{6,2},{7,3},{8,12},{9,13},{10,14},{11,15},{20,16},{21,... | collective-permute-start | bytes 786440 | tf_op jit(solution)/shard_map/ppermute | solution.py:155
  14.6 1.6 %collective-permute-done.3 = bf16[128,1024]{1,0:T(8,128)(2,1)S(1)} collective-permute-done((bf16[128,1024]{1,0:T(8,128)(2,1)S(1)}, bf16[128,1024]{1,0:T(8,128)(2,1)S(1)}, u32[]{:S(2)}, u32[]{:S(2)}) %collective-permute-start.3) | collective-permute-done | bytes 262176 | tf_op jit(solution)/shard_map/ppermute | solution.py:154
  16.2 2.0 %collective-permute-start.5 = (bf16[128,1024]{1,0:T(8,128)(2,1)S(1)}, bf16[128,1024]{1,0:T(8,128)(2,1)}, u32[]{:S(2)}, u32[]{:S(2)}) collective-permute-start(bf16[128,1024]{1,0:T(8,128)(2,1)S(1)} %collective-permute-done.3), channel_id=1, source_target_pairs={{4,0},{5,1},{6,2},{7,3},{8,12},{9,13},{10,14},{11,15},{20,16},{21,... | collective-permute-start | bytes 786440 | tf_op jit(solution)/shard_map/ppermute | solution.py:158
  18.2 0.0 copy-start
  18.2 1.5 %copy-done = bf16[128,7168]{1,0:T(8,128)(2,1)S(1)} copy-done((bf16[128,7168]{1,0:T(8,128)(2,1)S(1)}, bf16[128,7168]{1,0:T(8,128)(2,1)}, u32[]{:S(2)}) %copy-start) | copy-done | bytes 1835032
  19.7 0.0 copy-start.1
  19.7 0.9 copy-done.1
  20.7 0.0 copy-start.2
  20.7 0.7 copy-done.2
  21.3 2.2 %turn.1 = bf16[16,464,128]{2,1,0:T(8,128)(2,1)} custom-call(bf16[128,7168]{1,0:T(8,128)(2,1)S(1)} %copy-done, bf16[128,1024]{1,0:T(8,128)(2,1)S(1)} %copy-done.1, s32[1,128]{1,0:T(1,128)S(1)} %bitcast.9), custom_call_target="tpu_custom_call" | custom-call | tf_op jit(solution)/shard_map/turn/pallas_call | solution.py:141
  23.5 0.0 collective-permute-done.4
  23.5 0.1 collective-permute-done.5
  23.7 0.3 collective-permute-done.1.refs_1_
  24.0 0.0 copy-start.6
  24.0 8.8 %all-to-all-start = ((bf16[16,464,128]{2,1,0:T(8,128)(2,1)}), bf16[16,464,128]{2,1,0:T(8,128)(2,1)S(1)}, u32[]{:S(2)}, u32[]{:S(2)}) async-start(bf16[16,464,128]{2,1,0:T(8,128)(2,1)} %turn.1), calls=%async_computation | async-start | bytes 3801088 | tf_op jit(solution)/shard_map/all_to_all | solution.py:172
  32.7 0.1 select_bitcast_fusion
  32.8 0.1 pad_maximum_fusion.1.refs_4_
  32.9 0.0 copy-start.5
  32.9 0.3 collective-permute-start.8
  33.2 0.6 collective-permute-start.9
  33.8 0.0 copy-done.4
  33.8 0.0 collective-permute-start.6
  33.8 0.0 copy-done.6
  33.9 0.5 collective-permute-start.7
  34.4 23.6 %collective-permute-done.8.refs_5_ = bf16[2,128,1024]{2,1,0:T(8,128)(2,1)S(1)} collective-permute-done((bf16[2,128,1024]{2,1,0:T(8,128)(2,1)S(1)}, bf16[2,128,1024]{2,1,0:T(8,128)(2,1)S(1)}, u32[]{:S(2)}, u32[]{:S(2)}) %collective-permute-start.8) | collective-permute-done | bytes 524320 | tf_op jit(solution)/shard_map/ppermute | solution.py:139
  58.0 0.0 copy-start.7
  58.0 1.1 %collective-permute-start.10 = (bf16[2,128,1024]{2,1,0:T(8,128)(2,1)S(1)}, bf16[2,128,1024]{2,1,0:T(8,128)(2,1)}, u32[]{:S(2)}, u32[]{:S(2)}) collective-permute-start(bf16[2,128,1024]{2,1,0:T(8,128)(2,1)S(1)} %collective-permute-done.8.refs_5_), channel_id=1, source_target_pairs={{0,1},{1,0},{2,3},{3,2},{4,5},{5,4},{6,7},{7,6},{8,9},{9,8},{10,11... | collective-permute-start | bytes 1572872 | tf_op jit(solution)/shard_map/ppermute | solution.py:139
  59.0 0.0 collective-permute-done.9.refs_6_
  59.1 0.0 copy-start.8
  59.1 0.0 collective-permute-done.6.refs_2_
  59.1 0.0 copy-start.9
  59.1 0.0 collective-permute-done.7.refs_3_
  59.1 0.0 copy-done.7
  59.1 0.8 copy-done.8
  59.9 0.2 copy-done.9
  60.1 0.0 copy-start.10
  60.1 0.8 copy-done.10
  60.9 0.0 collective-permute-done.10.refs_7_
  60.9 15.1 %all-to-all-done.cols_any = bf16[16,464,128]{2,1,0:T(8,128)(2,1)S(1)} async-done(((bf16[16,464,128]{2,1,0:T(8,128)(2,1)}), bf16[16,464,128]{2,1,0:T(8,128)(2,1)S(1)}, u32[]{:S(2)}, u32[]{:S(2)}) %all-to-all-start) | async-done | bytes 1900576 | tf_op jit(solution)/shard_map/all_to_all | solution.py:172
  76.0 0.0 copy-start.3
  76.0 0.0 copy-done.5
  76.0 1.3 %copy-done.3 = bf16[16,464,128]{2,1,0:T(8,128)(2,1)} copy-done((bf16[16,464,128]{2,1,0:T(8,128)(2,1)}, bf16[16,464,128]{2,1,0:T(8,128)(2,1)S(1)}, u32[]{:S(2)}) %copy-start.3) | copy-done | bytes 1900568
  77.3 18.7 %merge.1 = (f32[4,448,1024]{2,1,0:T(8,128)}, bf16[448,1024]{1,0:T(8,128)(2,1)}) custom-call(s32[1]{0:T(128)} %bitcast.me_ref, bf16[16,464,128]{2,1,0:T(8,128)(2,1)} %copy-done.3, bf16[4,448,1024]{2,1,0:T(8,128)(2,1)} %weight_ref.1, bf16[2,128,1024]{2,1,0:T(8,128)(2,1)} %copy-done.4, bf16[2,128,1024]{2,1,0:T(8,128)(2,1)} %copy-done.6, ...), custom_call_target="tpu_custom_call" | custom-call | tf_op jit(solution)/shard_map/merge/pallas_call | solution.py:181
Async XLA Ops:
  0.6 7.5 %collective-permute-start = (bf16[128,1024]{1,0:T(8,128)(2,1)}, bf16[128,1024]{1,0:T(8,128)(2,1)S(1)}, u32[]{:S(2)}, u32[]{:S(2)}) collective-permute-start(bf16[128,1024]{1,0:T(8,128)(2,1)} %grad_ref.1), channel_id=1, source_target_pairs={{0,4},{1,5},{2,6},{3,7},{4,0},{5,1},{6,2},{7,3},{8,12},{9,13},{10,... | collective-permute-start | bytes 786440 | tf_op jit(solution)/shard_map/ppermute | solution.py:139
  0.9 11.7 %collective-permute-start.2 = (bf16[128,1024]{1,0:T(8,128)(2,1)}, bf16[128,1024]{1,0:T(8,128)(2,1)S(1)}, u32[]{:S(2)}, u32[]{:S(2)}) collective-permute-start(bf16[128,1024]{1,0:T(8,128)(2,1)} %grad_ref.1), channel_id=1, source_target_pairs={{4,8},{5,9},{6,10},{7,11},{8,4},{9,5},{10,6},{11,7},{20,24},{21,25... | collective-permute-start | bytes 786440 | tf_op jit(solution)/shard_map/ppermute | solution.py:152
  8.1 8.1 %collective-permute-start.3 = (bf16[128,1024]{1,0:T(8,128)(2,1)S(1)}, bf16[128,1024]{1,0:T(8,128)(2,1)S(1)}, u32[]{:S(2)}, u32[]{:S(2)}) collective-permute-start(bf16[128,1024]{1,0:T(8,128)(2,1)S(1)} %collective-permute-done), channel_id=1, source_target_pairs={{4,8},{5,9},{6,10},{7,11},{8,4},{9,5},{10,6},{11,7},{20,24},{21,25... | collective-permute-start | bytes 786440 | tf_op jit(solution)/shard_map/ppermute | solution.py:154
  12.3 21.6 %copy-start.4 = (bf16[2,128,1024]{2,1,0:T(8,128)(2,1)}, bf16[2,128,1024]{2,1,0:T(8,128)(2,1)S(1)}, u32[]{:S(2)}) copy-start(bf16[2,128,1024]{2,1,0:T(8,128)(2,1)S(1)} %pad_maximum_fusion.refs_0_) | copy-start | bytes 1572868
  12.3 11.7 %collective-permute-start.1 = (bf16[2,128,1024]{2,1,0:T(8,128)(2,1)S(1)}, bf16[2,128,1024]{2,1,0:T(8,128)(2,1)S(1)}, u32[]{:S(2)}, u32[]{:S(2)}) collective-permute-start(bf16[2,128,1024]{2,1,0:T(8,128)(2,1)S(1)} %pad_maximum_fusion.refs_0_), channel_id=1, source_target_pairs={{0,2},{1,3},{2,0},{3,1},{4,6},{5,7},{6,4},{7,5},{8,10},{9,11},{10,... | collective-permute-start | bytes 1572872 | tf_op jit(solution)/shard_map/ppermute | solution.py:139
  12.6 10.9 %collective-permute-start.4 = (bf16[128,1024]{1,0:T(8,128)(2,1)S(1)}, bf16[128,1024]{1,0:T(8,128)(2,1)}, u32[]{:S(2)}, u32[]{:S(2)}) collective-permute-start(bf16[128,1024]{1,0:T(8,128)(2,1)S(1)} %collective-permute-done.2), channel_id=1, source_target_pairs={{4,0},{5,1},{6,2},{7,3},{8,12},{9,13},{10,14},{11,15},{20,16},{21,... | collective-permute-start | bytes 786440 | tf_op jit(solution)/shard_map/ppermute | solution.py:155
  16.2 7.4 %collective-permute-start.5 = (bf16[128,1024]{1,0:T(8,128)(2,1)S(1)}, bf16[128,1024]{1,0:T(8,128)(2,1)}, u32[]{:S(2)}, u32[]{:S(2)}) collective-permute-start(bf16[128,1024]{1,0:T(8,128)(2,1)S(1)} %collective-permute-done.3), channel_id=1, source_target_pairs={{4,0},{5,1},{6,2},{7,3},{8,12},{9,13},{10,14},{11,15},{20,16},{21,... | collective-permute-start | bytes 786440 | tf_op jit(solution)/shard_map/ppermute | solution.py:158
  18.2 1.5 %copy-start = (bf16[128,7168]{1,0:T(8,128)(2,1)S(1)}, bf16[128,7168]{1,0:T(8,128)(2,1)}, u32[]{:S(2)}) copy-start(bf16[128,7168]{1,0:T(8,128)(2,1)} %tok_ref.1) | copy-start | bytes 5505028
  19.7 0.9 copy-start.1
  20.7 0.7 copy-start.2
  24.0 9.9 %copy-start.6 = (bf16[2,128,1024]{2,1,0:T(8,128)(2,1)}, bf16[2,128,1024]{2,1,0:T(8,128)(2,1)S(1)}, u32[]{:S(2)}) copy-start(bf16[2,128,1024]{2,1,0:T(8,128)(2,1)S(1)} %collective-permute-done.1.refs_1_) | copy-start | bytes 1572868
  24.0 52.1 %all-to-all-start = ((bf16[16,464,128]{2,1,0:T(8,128)(2,1)}), bf16[16,464,128]{2,1,0:T(8,128)(2,1)S(1)}, u32[]{:S(2)}, u32[]{:S(2)}) async-start(bf16[16,464,128]{2,1,0:T(8,128)(2,1)} %turn.1), calls=%async_computation | async-start | bytes 3801088 | tf_op jit(solution)/shard_map/all_to_all | solution.py:172
  32.9 43.2 %copy-start.5 = (bf16[2,128,1024]{2,1,0:T(8,128)(2,1)}, bf16[2,128,1024]{2,1,0:T(8,128)(2,1)S(1)}, u32[]{:S(2)}) copy-start(bf16[2,128,1024]{2,1,0:T(8,128)(2,1)S(1)} %pad_maximum_fusion.1.refs_4_) | copy-start | bytes 1572868
  32.9 25.1 %collective-permute-start.8 = (bf16[2,128,1024]{2,1,0:T(8,128)(2,1)S(1)}, bf16[2,128,1024]{2,1,0:T(8,128)(2,1)S(1)}, u32[]{:S(2)}, u32[]{:S(2)}) collective-permute-start(bf16[2,128,1024]{2,1,0:T(8,128)(2,1)S(1)} %pad_maximum_fusion.1.refs_4_), channel_id=1, source_target_pairs={{0,2},{1,3},{2,0},{3,1},{4,6},{5,7},{6,4},{7,5},{8,10},{9,11},{10,... | collective-permute-start | bytes 1572872 | tf_op jit(solution)/shard_map/ppermute | solution.py:139
  33.2 25.9 %collective-permute-start.9 = (bf16[2,128,1024]{2,1,0:T(8,128)(2,1)S(1)}, bf16[2,128,1024]{2,1,0:T(8,128)(2,1)S(1)}, u32[]{:S(2)}, u32[]{:S(2)}) collective-permute-start(bf16[2,128,1024]{2,1,0:T(8,128)(2,1)S(1)} %pad_maximum_fusion.1.refs_4_), channel_id=1, source_target_pairs={{0,1},{1,0},{2,3},{3,2},{4,5},{5,4},{6,7},{7,6},{8,9},{9,8},{10,11... | collective-permute-start | bytes 1572872 | tf_op jit(solution)/shard_map/ppermute | solution.py:139
  33.8 25.2 %collective-permute-start.6 = (bf16[2,128,1024]{2,1,0:T(8,128)(2,1)S(1)}, bf16[2,128,1024]{2,1,0:T(8,128)(2,1)S(1)}, u32[]{:S(2)}, u32[]{:S(2)}) collective-permute-start(bf16[2,128,1024]{2,1,0:T(8,128)(2,1)S(1)} %pad_maximum_fusion.refs_0_), channel_id=1, source_target_pairs={{0,1},{1,0},{2,3},{3,2},{4,5},{5,4},{6,7},{7,6},{8,9},{9,8},{10,11... | collective-permute-start | bytes 1572872 | tf_op jit(solution)/shard_map/ppermute | solution.py:139
  33.9 25.2 %collective-permute-start.7 = (bf16[2,128,1024]{2,1,0:T(8,128)(2,1)S(1)}, bf16[2,128,1024]{2,1,0:T(8,128)(2,1)S(1)}, u32[]{:S(2)}, u32[]{:S(2)}) collective-permute-start(bf16[2,128,1024]{2,1,0:T(8,128)(2,1)S(1)} %collective-permute-done.1.refs_1_), channel_id=1, source_target_pairs={{0,1},{1,0},{2,3},{3,2},{4,5},{5,4},{6,7},{7,6},{8,9},{9,8},{10,11... | collective-permute-start | bytes 1572872 | tf_op jit(solution)/shard_map/ppermute | solution.py:139
  58.0 1.1 %copy-start.7 = (bf16[2,128,1024]{2,1,0:T(8,128)(2,1)}, bf16[2,128,1024]{2,1,0:T(8,128)(2,1)S(1)}, u32[]{:S(2)}) copy-start(bf16[2,128,1024]{2,1,0:T(8,128)(2,1)S(1)} %collective-permute-done.8.refs_5_) | copy-start | bytes 1572868
  58.0 2.9 %collective-permute-start.10 = (bf16[2,128,1024]{2,1,0:T(8,128)(2,1)S(1)}, bf16[2,128,1024]{2,1,0:T(8,128)(2,1)}, u32[]{:S(2)}, u32[]{:S(2)}) collective-permute-start(bf16[2,128,1024]{2,1,0:T(8,128)(2,1)S(1)} %collective-permute-done.8.refs_5_), channel_id=1, source_target_pairs={{0,1},{1,0},{2,3},{3,2},{4,5},{5,4},{6,7},{7,6},{8,9},{9,8},{10,11... | collective-permute-start | bytes 1572872 | tf_op jit(solution)/shard_map/ppermute | solution.py:139
  59.1 0.8 copy-start.8
  59.1 1.0 %copy-start.9 = (bf16[2,128,1024]{2,1,0:T(8,128)(2,1)}, bf16[2,128,1024]{2,1,0:T(8,128)(2,1)S(1)}, u32[]{:S(2)}) copy-start(bf16[2,128,1024]{2,1,0:T(8,128)(2,1)S(1)} %collective-permute-done.6.refs_2_) | copy-start | bytes 1572868
  60.1 0.8 copy-start.10
  76.0 1.3 %copy-start.3 = (bf16[16,464,128]{2,1,0:T(8,128)(2,1)}, bf16[16,464,128]{2,1,0:T(8,128)(2,1)S(1)}, u32[]{:S(2)}) copy-start(bf16[16,464,128]{2,1,0:T(8,128)(2,1)S(1)} %all-to-all-done.cols_any) | copy-start | bytes 5701636

commit v4 on v3

--- a/solution.py
+++ b/solution.py
@@ -60,7 +60,7 @@
 def merge_kernel(experts, cap, order, count, me_ref, cols_any, weight_ref, *refs):
     fisher_ref, merged_ref, left_hi, left_lo, right_hi, right_lo = refs[-11:-5]
     pick, left_pick, scale_ref, cols_ref, sem = refs[-5:]
-    blocks = [ref.at[i] for ref in refs[:-11] for i in range(ref.shape[0])]
+    blocks = refs[:-11]
     parts, tall, rows = cols_ref.shape
     depth = tall - 16
     span = parts * cap
@@ -145,38 +145,35 @@
         name="turn",
     )(tokens, out_grads, routing.reshape(1, rows))
 
+    held = {0: out_grads}
     if parts == 16:
         inward = [(s, s + 4) for s in range(4, 8)] + [(s, s - 4) for s in range(8, 12)]
         outward = [(s, s - 4) for s in range(4, 8)] + [(s, s + 4) for s in range(8, 12)]
         inner = (me // 4 == 1) | (me // 4 == 2)
+        y_own = swap(out_grads, 2)
+        near = swap(out_grads, 4)
+        second = swap(out_grads, 8)
+        y_own, near, second = lax.optimization_barrier((y_own, near, second))
         far = lax.ppermute(out_grads, "tok", inward)
-        near = swap(out_grads, 4)
-        far2 = lax.ppermute(near, "tok", inward)
-        out = lax.ppermute(far, "tok", outward)
-        pair = jnp.stack([out_grads, near])
-        across = swap(pair, 2)
-        out2 = lax.ppermute(far2, "tok", outward)
-        turned, pair, across, far, far2, out, out2 = lax.optimization_barrier(
-            (turned, pair, across, far, far2, out, out2)
+        out = lax.ppermute(second, "tok", outward)
+        y_near = swap(near, 2)
+        (turned, far, out) = lax.optimization_barrier(
+            (turned, far, out)
         )
-        other = jnp.stack([jnp.where(inner, far, out2), jnp.where(inner, far2, out)])
-        halves = [(pair, across, (0, 4)), (other, swap(other, 2), (12, 8))]
+        third = jnp.where(inner, far, out)
+        y_second = swap(second, 2)
+        held.update({4: near, 8: second, 12: third})
+        held.update({2: y_own, 6: y_near, 10: y_second, 14: swap(third, 2)})
     else:
-        near = swap(out_grads, 4)
-        pairs = [(jnp.stack([out_grads, near]), (0, 4))]
-        flip = 8
-        while flip < parts:
-            pairs = pairs + [(swap(b, flip), tuple(k ^ flip for k in ks)) for b, ks in pairs]
-            flip *= 2
-        halves = [(b, swap(b, 2), ks) for b, ks in pairs]
+        flip = parts // 2
+        while flip > 1:
+            held.update({k ^ flip: swap(b, flip) for k, b in held.items()})
+            flip //= 2
+    held.update({k ^ 1: swap(b, 1) for k, b in held.items()})
+    order = sorted(held)
+    blocks = [held[k] for k in order]
+
     columns = lax.all_to_all(turned, "tok", split_axis=0, concat_axis=0, tiled=True)
-
-    order = []
-    blocks = []
-    for block, across, ks in halves:
-        for b, flip in ((block, 0), (across, 2), (swap(block, 1), 1), (swap(across, 1), 3)):
-            blocks.append(b)
-            order += [k ^ flip for k in ks]
 
     fisher, merged = pl.pallas_call(
         functools.partial(merge_kernel, experts, cap, tuple(order), width * hidden),
@@ -186,7 +183,7 @@
             pl.BlockSpec(memory_space=pl.ANY),
             pl.BlockSpec((experts, depth, TILE), lambda f: (0, 0, f)),
         ]
-        + [pl.BlockSpec((2, rows, TILE), lambda f: (0, 0, f))] * len(blocks),
+        + [pl.BlockSpec((rows, TILE), lambda f: (0, f))] * len(blocks),
         out_specs=[
             pl.BlockSpec((experts, depth, TILE), lambda f: (0, 0, f)),
             pl.BlockSpec((depth, TILE), lambda f: (0, f)),

time: 96.4 us -> 95.9 us (level)
  waiting for transfers between devices: 43.7 us -> 42.6 us
  starting transfers between devices: 23.3 us -> 24.3 us
    ppermute x7 -> x14, waiting for transfers between devices: 26.8 us -> 37.6 us  [swap(): return lax.ppermute(value, 'tok', [(s, s ^ flip) for s in range(parts)])]
    all_to_all x1, waiting for transfers between devices: 15.1 us -> 5.01 us  [local(): lax.all_to_all(turned, 'tok', split_axis=0, concat_axis=0, tiled=True)]
    ppermute x7 -> x14, starting transfers between devices: 3.06 us -> 10.3 us  [swap(): return lax.ppermute(value, 'tok', [(s, s ^ flip) for s in range(parts)])]
    ppermute x3 -> x1, starting transfers between devices: 7.19 us -> 2.6 us  [local(): out = lax.ppermute(second, 'tok', outward)]
    ppermute x1, starting transfers between devices: 4.32 us -> 2.09 us  [local(): far = lax.ppermute(out_grads, 'tok', inward)]
    ppermute x3 -> x1, waiting for transfers between devices: 1.75 us -> 0.01 us  [local(): out = lax.ppermute(second, 'tok', outward)]
    another operation x3 -> x0, other arithmetic: 1.11 us -> none  [the longest x1 1 us: local(): pair = jnp.stack([out_grads, near])]
    select_n x0 -> x1, other arithmetic: none -> 0.98 us  [local(): third = jnp.where(inner, far, out)]
  transfers between devices with their start and end apart: 12 -> 17, of which waited for: 6 -> 5; matrix products, arithmetic and copies ran while one was open for 1% -> 1% of each run, Pallas kernels for 2% -> 2%
where the time goes in v4:
time: 95.9 us; the launch traced here: 95.6 us
  waiting for transfers between devices  42.6 us (44%)
  starting transfers between devices  24.3 us (25%)
  Pallas kernels  21.1 us (22%)
  local copies, waits for them, and re-layouts  5.79 us (6%)
  other arithmetic  0.98 us (1%)
    ppermute x14, waiting for transfers between devices, swap(): return lax.ppermute(value, 'tok', [(s, s ^ flip) for s in range(parts)])  37.6 us
    pallas_call x1, Pallas kernels, local(): pl.pallas_call(functools.partial(merge_kernel, experts, cap, tuple(order)...  18.9 us
    ppermute x14, starting transfers between devices, swap(): return lax.ppermute(value, 'tok', [(s, s ^ flip) for s in range(parts)])  10.3 us
    all_to_all x1, starting transfers between devices, local(): lax.all_to_all(turned, 'tok', split_axis=0, concat_axis=0, tiled=True)  9.37 us
    unnamed x38, local copies, waits for them, and re-layouts  5.79 us
    all_to_all x1, waiting for transfers between devices, local(): lax.all_to_all(turned, 'tok', split_axis=0, concat_axis=0, tiled=True)  5.01 us
    ppermute x1, starting transfers between devices, local(): out = lax.ppermute(second, 'tok', outward)  2.6 us
    pallas_call x1, Pallas kernels, local(): pl.pallas_call(functools.partial(turn_kernel, experts, cap), out_shape=pl...  2.2 us
  transfers between devices with their start and end apart: 17, of which 5 were waited for; matrix products, arithmetic and copies ran while one was open for 1% of the time, Pallas kernels for 2%

profile of v4, /device:TPU:13, one launch (start us, length us, event | category | flops | bytes accessed | tf_op | source)
XLA Modules:
  0.0 95.6 jit_solution(4119915983340351839)
XLA Ops:
  0.6 2.4 %collective-permute-start.3 = (bf16[128,1024]{1,0:T(8,128)(2,1)}, bf16[128,1024]{1,0:T(8,128)(2,1)S(1)}, u32[]{:S(2)}, u32[]{:S(2)}) collective-permute-start(bf16[128,1024]{1,0:T(8,128)(2,1)} %refs_0_.1), channel_id=1, source_target_pairs={{0,8},{1,9},{2,10},{3,11},{4,12},{5,13},{6,14},{7,15},{8,0},{9,1},... | collective-permute-start | bytes 786440 | tf_op jit(solution)/shard_map/ppermute | solution.py:139
  3.0 0.2 collective-permute-start.2
  3.2 0.2 collective-permute-start.1
  3.4 2.1 %collective-permute-start = (bf16[128,1024]{1,0:T(8,128)(2,1)}, bf16[128,1024]{1,0:T(8,128)(2,1)}, u32[]{:S(2)}, u32[]{:S(2)}) collective-permute-start(bf16[128,1024]{1,0:T(8,128)(2,1)} %refs_0_.1), channel_id=1, source_target_pairs={{4,8},{5,9},{6,10},{7,11},{8,4},{9,5},{10,6},{11,7},{20,24},{21,25... | collective-permute-start | bytes 786440 | tf_op jit(solution)/shard_map/ppermute | solution.py:157
  5.5 9.3 %collective-permute-done.3.refs_8_ = bf16[128,1024]{1,0:T(8,128)(2,1)S(1)} collective-permute-done((bf16[128,1024]{1,0:T(8,128)(2,1)}, bf16[128,1024]{1,0:T(8,128)(2,1)S(1)}, u32[]{:S(2)}, u32[]{:S(2)}) %collective-permute-start.3) | collective-permute-done | bytes 262176 | tf_op jit(solution)/shard_map/ppermute | solution.py:139
  14.9 0.0 collective-permute-done.2.refs_4_
  14.9 0.0 copy-start.7
  14.9 0.0 collective-permute-done.1.refs_2_
  14.9 0.0 copy-start.8
  14.9 2.6 %collective-permute-start.4 = (bf16[128,1024]{1,0:T(8,128)(2,1)S(1)}, bf16[128,1024]{1,0:T(8,128)(2,1)}, u32[]{:S(2)}, u32[]{:S(2)}) collective-permute-start(bf16[128,1024]{1,0:T(8,128)(2,1)S(1)} %collective-permute-done.3.refs_8_), channel_id=1, source_target_pairs={{4,0},{5,1},{6,2},{7,3},{8,12},{9,13},{10,14},{11,15},{20,16},{21,... | collective-permute-start | bytes 786440 | tf_op jit(solution)/shard_map/ppermute | solution.py:158
  17.5 0.0 copy-start
  17.5 1.5 %copy-done = bf16[128,7168]{1,0:T(8,128)(2,1)S(1)} copy-done((bf16[128,7168]{1,0:T(8,128)(2,1)S(1)}, bf16[128,7168]{1,0:T(8,128)(2,1)}, u32[]{:S(2)}) %copy-start) | copy-done | bytes 1835032
  19.0 0.0 copy-start.1
  19.0 0.9 copy-done.1
  19.9 0.7 copy-done.3
  20.6 2.2 %turn.1 = bf16[16,464,128]{2,1,0:T(8,128)(2,1)} custom-call(bf16[128,7168]{1,0:T(8,128)(2,1)S(1)} %copy-done, bf16[128,1024]{1,0:T(8,128)(2,1)S(1)} %copy-done.1, s32[1,128]{1,0:T(1,128)S(1)} %bitcast.2), custom_call_target="tpu_custom_call" | custom-call | tf_op jit(solution)/shard_map/turn/pallas_call | solution.py:141
  22.8 0.0 collective-permute-done
  22.8 0.0 collective-permute-done.4
  22.8 9.4 %all-to-all-start = ((bf16[16,464,128]{2,1,0:T(8,128)(2,1)}), bf16[16,464,128]{2,1,0:T(8,128)(2,1)S(1)}, u32[]{:S(2)}, u32[]{:S(2)}) async-start(bf16[16,464,128]{2,1,0:T(8,128)(2,1)} %turn.1), calls=%async_computation | async-start | bytes 3801088 | tf_op jit(solution)/shard_map/all_to_all | solution.py:176
  32.2 0.0 copy-done.2
  32.2 0.4 collective-permute-start.5
  32.6 0.3 collective-permute-start.8
  32.9 0.0 copy-done.7
  32.9 0.4 collective-permute-start.7
  33.3 1.2 %collective-permute-start.11 = (bf16[128,1024]{1,0:T(8,128)(2,1)S(1)}, bf16[128,1024]{1,0:T(8,128)(2,1)S(1)}, u32[]{:S(2)}, u32[]{:S(2)}) collective-permute-start(bf16[128,1024]{1,0:T(8,128)(2,1)S(1)} %collective-permute-done.3.refs_8_), channel_id=1, source_target_pairs={{0,2},{1,3},{2,0},{3,1},{4,6},{5,7},{6,4},{7,5},{8,10},{9,11},{10,... | collective-permute-start | bytes 786440 | tf_op jit(solution)/shard_map/ppermute | solution.py:139
  34.5 0.0 copy-done.8
  34.5 0.3 collective-permute-start.6
  34.9 1.0 %broadcast_select_fusion.refs_12_ = bf16[128,1024]{1,0:T(8,128)(2,1)S(1)} fusion(bf16[128,1024]{1,0:T(8,128)(2,1)} %collective-permute-done, bf16[128,1024]{1,0:T(8,128)(2,1)} %collective-permute-done.4, pred[]{:T(512)S(6)} %or.3), kind=kLoop, calls=%fused_computation | loop fusion | flops 131072 | bytes 786433 | tf_op jit(solution)/shard_map/jit(_where)/select_n | solution.py:163
  35.8 0.0 copy-start.5
  35.9 0.0 collective-permute-done.5.refs_1_
  35.9 0.0 copy-start.9
  35.9 0.3 collective-permute-start.14
  36.2 0.0 collective-permute-done.6.refs_3_
  36.2 0.0 copy-done.6
  36.2 0.5 collective-permute-start.10
  36.7 12.5 %collective-permute-done.8.refs_6_ = bf16[128,1024]{1,0:T(8,128)(2,1)S(1)} collective-permute-done((bf16[128,1024]{1,0:T(8,128)(2,1)S(1)}, bf16[128,1024]{1,0:T(8,128)(2,1)S(1)}, u32[]{:S(2)}, u32[]{:S(2)}) %collective-permute-start.8) | collective-permute-done | bytes 262176 | tf_op jit(solution)/shard_map/ppermute | solution.py:139
  49.2 1.4 %collective-permute-start.13 = (bf16[128,1024]{1,0:T(8,128)(2,1)S(1)}, bf16[128,1024]{1,0:T(8,128)(2,1)S(1)}, u32[]{:S(2)}, u32[]{:S(2)}) collective-permute-start(bf16[128,1024]{1,0:T(8,128)(2,1)S(1)} %broadcast_select_fusion.refs_12_), channel_id=1, source_target_pairs={{0,1},{1,0},{2,3},{3,2},{4,5},{5,4},{6,7},{7,6},{8,9},{9,8},{10,11... | collective-permute-start | bytes 786440 | tf_op jit(solution)/shard_map/ppermute | solution.py:139
  50.6 0.0 collective-permute-done.7.refs_5_
  50.6 0.1 collective-permute-start.9
  50.7 6.7 %collective-permute-done.11.refs_10_ = bf16[128,1024]{1,0:T(8,128)(2,1)S(1)} collective-permute-done((bf16[128,1024]{1,0:T(8,128)(2,1)S(1)}, bf16[128,1024]{1,0:T(8,128)(2,1)S(1)}, u32[]{:S(2)}, u32[]{:S(2)}) %collective-permute-start.11) | collective-permute-done | bytes 262176 | tf_op jit(solution)/shard_map/ppermute | solution.py:139
  57.4 1.6 %collective-permute-start.12 = (bf16[128,1024]{1,0:T(8,128)(2,1)S(1)}, bf16[128,1024]{1,0:T(8,128)(2,1)S(1)}, u32[]{:S(2)}, u32[]{:S(2)}) collective-permute-start(bf16[128,1024]{1,0:T(8,128)(2,1)S(1)} %collective-permute-done.11.refs_10_), channel_id=1, source_target_pairs={{0,1},{1,0},{2,3},{3,2},{4,5},{5,4},{6,7},{7,6},{8,9},{9,8},{10,11... | collective-permute-start | bytes 786440 | tf_op jit(solution)/shard_map/ppermute | solution.py:139
  59.1 9.0 %collective-permute-done.14.refs_14_ = bf16[128,1024]{1,0:T(8,128)(2,1)S(1)} collective-permute-done((bf16[128,1024]{1,0:T(8,128)(2,1)S(1)}, bf16[128,1024]{1,0:T(8,128)(2,1)S(1)}, u32[]{:S(2)}, u32[]{:S(2)}) %collective-permute-start.14) | collective-permute-done | bytes 262176 | tf_op jit(solution)/shard_map/ppermute | solution.py:139
  68.1 0.9 collective-permute-start.15
  69.0 0.0 collective-permute-done.10.refs_9_
  69.0 0.0 collective-permute-done.9.refs_7_
  69.0 0.0 copy-start.17
  69.0 0.0 collective-permute-done.12.refs_11_
  69.0 0.0 copy-start.18
  69.0 0.0 collective-permute-done.13.refs_13_
  69.0 0.0 copy-done.13
  69.0 0.0 copy-done.10
  69.0 0.0 copy-done.11
  69.0 0.0 copy-done.12
  69.1 0.7 copy-done.18
  69.7 0.7 copy-done.16
  70.4 0.0 collective-permute-done.15.refs_15_
  70.4 5.0 %all-to-all-done.cols_any = bf16[16,464,128]{2,1,0:T(8,128)(2,1)S(1)} async-done(((bf16[16,464,128]{2,1,0:T(8,128)(2,1)}), bf16[16,464,128]{2,1,0:T(8,128)(2,1)S(1)}, u32[]{:S(2)}, u32[]{:S(2)}) %all-to-all-start) | async-done | bytes 1900576 | tf_op jit(solution)/shard_map/all_to_all | solution.py:176
  75.5 0.0 copy-done.5
  75.5 0.0 copy-done.9
  75.5 0.0 copy-done.14
  75.5 0.0 copy-done.15
  75.5 0.0 copy-done.17
  75.5 1.2 %copy-done.4 = bf16[16,464,128]{2,1,0:T(8,128)(2,1)} copy-done((bf16[16,464,128]{2,1,0:T(8,128)(2,1)}, bf16[16,464,128]{2,1,0:T(8,128)(2,1)S(1)}, u32[]{:S(2)}) %copy-start.4) | copy-done | bytes 1900568
  76.7 18.9 %merge.1 = (f32[4,448,1024]{2,1,0:T(8,128)}, bf16[448,1024]{1,0:T(8,128)(2,1)}) custom-call(s32[1]{0:T(128)} %bitcast.me_ref, bf16[16,464,128]{2,1,0:T(8,128)(2,1)} %copy-done.4, bf16[4,448,1024]{2,1,0:T(8,128)(2,1)} %weight_ref.1, bf16[128,1024]{1,0:T(8,128)(2,1)} %refs_0_.1, bf16[128,1024]{1,0:T(8,128)(2,1)} %copy-done.9, bf16[128,1024]{1,0:T(8,128)(2,1)} %copy-done.8, ...), custom_call_target="tpu_custom_call" | custom-call | tf_op jit(solution)/shard_map/merge/pallas_call | solution.py:178
  (11 shorter events, 0.0 us)
Async XLA Ops:
  0.6 14.2 %collective-permute-start.3 = (bf16[128,1024]{1,0:T(8,128)(2,1)}, bf16[128,1024]{1,0:T(8,128)(2,1)S(1)}, u32[]{:S(2)}, u32[]{:S(2)}) collective-permute-start(bf16[128,1024]{1,0:T(8,128)(2,1)} %refs_0_.1), channel_id=1, source_target_pairs={{0,8},{1,9},{2,10},{3,11},{4,12},{5,13},{6,14},{7,15},{8,0},{9,1},... | collective-permute-start | bytes 786440 | tf_op jit(solution)/shard_map/ppermute | solution.py:139
  3.0 11.9 %collective-permute-start.2 = (bf16[128,1024]{1,0:T(8,128)(2,1)}, bf16[128,1024]{1,0:T(8,128)(2,1)S(1)}, u32[]{:S(2)}, u32[]{:S(2)}) collective-permute-start(bf16[128,1024]{1,0:T(8,128)(2,1)} %refs_0_.1), channel_id=1, source_target_pairs={{0,4},{1,5},{2,6},{3,7},{4,0},{5,1},{6,2},{7,3},{8,12},{9,13},{10,... | collective-permute-start | bytes 786440 | tf_op jit(solution)/shard_map/ppermute | solution.py:139
  3.2 11.7 %collective-permute-start.1 = (bf16[128,1024]{1,0:T(8,128)(2,1)}, bf16[128,1024]{1,0:T(8,128)(2,1)S(1)}, u32[]{:S(2)}, u32[]{:S(2)}) collective-permute-start(bf16[128,1024]{1,0:T(8,128)(2,1)} %refs_0_.1), channel_id=1, source_target_pairs={{0,2},{1,3},{2,0},{3,1},{4,6},{5,7},{6,4},{7,5},{8,10},{9,11},{10,... | collective-permute-start | bytes 786440 | tf_op jit(solution)/shard_map/ppermute | solution.py:139
  3.4 19.4 %collective-permute-start = (bf16[128,1024]{1,0:T(8,128)(2,1)}, bf16[128,1024]{1,0:T(8,128)(2,1)}, u32[]{:S(2)}, u32[]{:S(2)}) collective-permute-start(bf16[128,1024]{1,0:T(8,128)(2,1)} %refs_0_.1), channel_id=1, source_target_pairs={{4,8},{5,9},{6,10},{7,11},{8,4},{9,5},{10,6},{11,7},{20,24},{21,25... | collective-permute-start | bytes 786440 | tf_op jit(solution)/shard_map/ppermute | solution.py:157
  14.9 21.4 %copy-start.6 = (bf16[128,1024]{1,0:T(8,128)(2,1)}, bf16[128,1024]{1,0:T(8,128)(2,1)S(1)}, u32[]{:S(2)}) copy-start(bf16[128,1024]{1,0:T(8,128)(2,1)S(1)} %collective-permute-done.3.refs_8_) | copy-start | bytes 786436
  14.9 18.0 %copy-start.7 = (bf16[128,1024]{1,0:T(8,128)(2,1)}, bf16[128,1024]{1,0:T(8,128)(2,1)S(1)}, u32[]{:S(2)}) copy-start(bf16[128,1024]{1,0:T(8,128)(2,1)S(1)} %collective-permute-done.2.refs_4_) | copy-start | bytes 786436
  14.9 19.6 %copy-start.8 = (bf16[128,1024]{1,0:T(8,128)(2,1)}, bf16[128,1024]{1,0:T(8,128)(2,1)S(1)}, u32[]{:S(2)}) copy-start(bf16[128,1024]{1,0:T(8,128)(2,1)S(1)} %collective-permute-done.1.refs_2_) | copy-start | bytes 786436
  14.9 7.9 %collective-permute-start.4 = (bf16[128,1024]{1,0:T(8,128)(2,1)S(1)}, bf16[128,1024]{1,0:T(8,128)(2,1)}, u32[]{:S(2)}, u32[]{:S(2)}) collective-permute-start(bf16[128,1024]{1,0:T(8,128)(2,1)S(1)} %collective-permute-done.3.refs_8_), channel_id=1, source_target_pairs={{4,0},{5,1},{6,2},{7,3},{8,12},{9,13},{10,14},{11,15},{20,16},{21,... | collective-permute-start | bytes 786440 | tf_op jit(solution)/shard_map/ppermute | solution.py:158
  17.5 1.5 %copy-start = (bf16[128,7168]{1,0:T(8,128)(2,1)S(1)}, bf16[128,7168]{1,0:T(8,128)(2,1)}, u32[]{:S(2)}) copy-start(bf16[128,7168]{1,0:T(8,128)(2,1)} %tok_ref.1) | copy-start | bytes 5505028
  19.0 0.9 copy-start.1
  19.9 0.7 copy-start.3
  22.8 9.4 %copy-start.2 = (bf16[128,1024]{1,0:T(8,128)(2,1)S(1)}, bf16[128,1024]{1,0:T(8,128)(2,1)}, u32[]{:S(2)}) copy-start(bf16[128,1024]{1,0:T(8,128)(2,1)} %refs_0_.1) | copy-start | bytes 786436
  22.8 52.7 %all-to-all-start = ((bf16[16,464,128]{2,1,0:T(8,128)(2,1)}), bf16[16,464,128]{2,1,0:T(8,128)(2,1)S(1)}, u32[]{:S(2)}, u32[]{:S(2)}) async-start(bf16[16,464,128]{2,1,0:T(8,128)(2,1)} %turn.1), calls=%async_computation | async-start | bytes 3801088 | tf_op jit(solution)/shard_map/all_to_all | solution.py:176
  32.2 3.7 %collective-permute-start.5 = (bf16[128,1024]{1,0:T(8,128)(2,1)S(1)}, bf16[128,1024]{1,0:T(8,128)(2,1)S(1)}, u32[]{:S(2)}, u32[]{:S(2)}) collective-permute-start(bf16[128,1024]{1,0:T(8,128)(2,1)S(1)} %copy-done.2), channel_id=1, source_target_pairs={{0,1},{1,0},{2,3},{3,2},{4,5},{5,4},{6,7},{7,6},{8,9},{9,8},{10,11... | collective-permute-start | bytes 786440 | tf_op jit(solution)/shard_map/ppermute | solution.py:139
  32.6 16.6 %collective-permute-start.8 = (bf16[128,1024]{1,0:T(8,128)(2,1)S(1)}, bf16[128,1024]{1,0:T(8,128)(2,1)S(1)}, u32[]{:S(2)}, u32[]{:S(2)}) collective-permute-start(bf16[128,1024]{1,0:T(8,128)(2,1)S(1)} %collective-permute-done.2.refs_4_), channel_id=1, source_target_pairs={{0,2},{1,3},{2,0},{3,1},{4,6},{5,7},{6,4},{7,5},{8,10},{9,11},{10,... | collective-permute-start | bytes 786440 | tf_op jit(solution)/shard_map/ppermute | solution.py:139
  32.9 17.7 %collective-permute-start.7 = (bf16[128,1024]{1,0:T(8,128)(2,1)S(1)}, bf16[128,1024]{1,0:T(8,128)(2,1)S(1)}, u32[]{:S(2)}, u32[]{:S(2)}) collective-permute-start(bf16[128,1024]{1,0:T(8,128)(2,1)S(1)} %collective-permute-done.2.refs_4_), channel_id=1, source_target_pairs={{0,1},{1,0},{2,3},{3,2},{4,5},{5,4},{6,7},{7,6},{8,9},{9,8},{10,11... | collective-permute-start | bytes 786440 | tf_op jit(solution)/shard_map/ppermute | solution.py:139
  33.3 24.1 %collective-permute-start.11 = (bf16[128,1024]{1,0:T(8,128)(2,1)S(1)}, bf16[128,1024]{1,0:T(8,128)(2,1)S(1)}, u32[]{:S(2)}, u32[]{:S(2)}) collective-permute-start(bf16[128,1024]{1,0:T(8,128)(2,1)S(1)} %collective-permute-done.3.refs_8_), channel_id=1, source_target_pairs={{0,2},{1,3},{2,0},{3,1},{4,6},{5,7},{6,4},{7,5},{8,10},{9,11},{10,... | collective-permute-start | bytes 786440 | tf_op jit(solution)/shard_map/ppermute | solution.py:139
  34.5 1.7 %collective-permute-start.6 = (bf16[128,1024]{1,0:T(8,128)(2,1)S(1)}, bf16[128,1024]{1,0:T(8,128)(2,1)S(1)}, u32[]{:S(2)}, u32[]{:S(2)}) collective-permute-start(bf16[128,1024]{1,0:T(8,128)(2,1)S(1)} %collective-permute-done.1.refs_2_), channel_id=1, source_target_pairs={{0,1},{1,0},{2,3},{3,2},{4,5},{5,4},{6,7},{7,6},{8,9},{9,8},{10,11... | collective-permute-start | bytes 786440 | tf_op jit(solution)/shard_map/ppermute | solution.py:139
  35.8 39.6 %copy-start.5 = (bf16[128,1024]{1,0:T(8,128)(2,1)}, bf16[128,1024]{1,0:T(8,128)(2,1)S(1)}, u32[]{:S(2)}) copy-start(bf16[128,1024]{1,0:T(8,128)(2,1)S(1)} %broadcast_select_fusion.refs_12_) | copy-start | bytes 786436
  35.9 39.6 %copy-start.9 = (bf16[128,1024]{1,0:T(8,128)(2,1)}, bf16[128,1024]{1,0:T(8,128)(2,1)S(1)}, u32[]{:S(2)}) copy-start(bf16[128,1024]{1,0:T(8,128)(2,1)S(1)} %collective-permute-done.5.refs_1_) | copy-start | bytes 786436
  35.9 32.2 %collective-permute-start.14 = (bf16[128,1024]{1,0:T(8,128)(2,1)S(1)}, bf16[128,1024]{1,0:T(8,128)(2,1)S(1)}, u32[]{:S(2)}, u32[]{:S(2)}) collective-permute-start(bf16[128,1024]{1,0:T(8,128)(2,1)S(1)} %broadcast_select_fusion.refs_12_), channel_id=1, source_target_pairs={{0,2},{1,3},{2,0},{3,1},{4,6},{5,7},{6,4},{7,5},{8,10},{9,11},{10,... | collective-permute-start | bytes 786440 | tf_op jit(solution)/shard_map/ppermute | solution.py:139
  36.2 32.8 %copy-start.13 = (bf16[128,1024]{1,0:T(8,128)(2,1)}, bf16[128,1024]{1,0:T(8,128)(2,1)S(1)}, u32[]{:S(2)}) copy-start(bf16[128,1024]{1,0:T(8,128)(2,1)S(1)} %collective-permute-done.6.refs_3_) | copy-start | bytes 786436
  36.2 32.7 %collective-permute-start.10 = (bf16[128,1024]{1,0:T(8,128)(2,1)S(1)}, bf16[128,1024]{1,0:T(8,128)(2,1)S(1)}, u32[]{:S(2)}, u32[]{:S(2)}) collective-permute-start(bf16[128,1024]{1,0:T(8,128)(2,1)S(1)} %collective-permute-done.3.refs_8_), channel_id=1, source_target_pairs={{0,1},{1,0},{2,3},{3,2},{4,5},{5,4},{6,7},{7,6},{8,9},{9,8},{10,11... | collective-permute-start | bytes 786440 | tf_op jit(solution)/shard_map/ppermute | solution.py:139
  49.2 19.8 %copy-start.10 = (bf16[128,1024]{1,0:T(8,128)(2,1)}, bf16[128,1024]{1,0:T(8,128)(2,1)S(1)}, u32[]{:S(2)}) copy-start(bf16[128,1024]{1,0:T(8,128)(2,1)S(1)} %collective-permute-done.8.refs_6_) | copy-start | bytes 786436
  49.2 19.8 %collective-permute-start.13 = (bf16[128,1024]{1,0:T(8,128)(2,1)S(1)}, bf16[128,1024]{1,0:T(8,128)(2,1)S(1)}, u32[]{:S(2)}, u32[]{:S(2)}) collective-permute-start(bf16[128,1024]{1,0:T(8,128)(2,1)S(1)} %broadcast_select_fusion.refs_12_), channel_id=1, source_target_pairs={{0,1},{1,0},{2,3},{3,2},{4,5},{5,4},{6,7},{7,6},{8,9},{9,8},{10,11... | collective-permute-start | bytes 786440 | tf_op jit(solution)/shard_map/ppermute | solution.py:139
  50.6 18.4 %copy-start.11 = (bf16[128,1024]{1,0:T(8,128)(2,1)}, bf16[128,1024]{1,0:T(8,128)(2,1)S(1)}, u32[]{:S(2)}) copy-start(bf16[128,1024]{1,0:T(8,128)(2,1)S(1)} %collective-permute-done.7.refs_5_) | copy-start | bytes 786436
  50.6 18.4 %collective-permute-start.9 = (bf16[128,1024]{1,0:T(8,128)(2,1)S(1)}, bf16[128,1024]{1,0:T(8,128)(2,1)S(1)}, u32[]{:S(2)}, u32[]{:S(2)}) collective-permute-start(bf16[128,1024]{1,0:T(8,128)(2,1)S(1)} %collective-permute-done.8.refs_6_), channel_id=1, source_target_pairs={{0,1},{1,0},{2,3},{3,2},{4,5},{5,4},{6,7},{7,6},{8,9},{9,8},{10,11... | collective-permute-start | bytes 786440 | tf_op jit(solution)/shard_map/ppermute | solution.py:139
  57.4 11.6 %copy-start.12 = (bf16[128,1024]{1,0:T(8,128)(2,1)}, bf16[128,1024]{1,0:T(8,128)(2,1)S(1)}, u32[]{:S(2)}) copy-start(bf16[128,1024]{1,0:T(8,128)(2,1)S(1)} %collective-permute-done.11.refs_10_) | copy-start | bytes 786436
  57.4 11.6 %collective-permute-start.12 = (bf16[128,1024]{1,0:T(8,128)(2,1)S(1)}, bf16[128,1024]{1,0:T(8,128)(2,1)S(1)}, u32[]{:S(2)}, u32[]{:S(2)}) collective-permute-start(bf16[128,1024]{1,0:T(8,128)(2,1)S(1)} %collective-permute-done.11.refs_10_), channel_id=1, source_target_pairs={{0,1},{1,0},{2,3},{3,2},{4,5},{5,4},{6,7},{7,6},{8,9},{9,8},{10,11... | collective-permute-start | bytes 786440 | tf_op jit(solution)/shard_map/ppermute | solution.py:139
  68.1 7.4 %copy-start.14 = (bf16[128,1024]{1,0:T(8,128)(2,1)}, bf16[128,1024]{1,0:T(8,128)(2,1)S(1)}, u32[]{:S(2)}) copy-start(bf16[128,1024]{1,0:T(8,128)(2,1)S(1)} %collective-permute-done.14.refs_14_) | copy-start | bytes 786436
  68.1 2.4 %collective-permute-start.15 = (bf16[128,1024]{1,0:T(8,128)(2,1)S(1)}, bf16[128,1024]{1,0:T(8,128)(2,1)}, u32[]{:S(2)}, u32[]{:S(2)}) collective-permute-start(bf16[128,1024]{1,0:T(8,128)(2,1)S(1)} %collective-permute-done.14.refs_14_), channel_id=1, source_target_pairs={{0,1},{1,0},{2,3},{3,2},{4,5},{5,4},{6,7},{7,6},{8,9},{9,8},{10,11... | collective-permute-start | bytes 786440 | tf_op jit(solution)/shard_map/ppermute | solution.py:139
  69.0 6.5 %copy-start.15 = (bf16[128,1024]{1,0:T(8,128)(2,1)}, bf16[128,1024]{1,0:T(8,128)(2,1)S(1)}, u32[]{:S(2)}) copy-start(bf16[128,1024]{1,0:T(8,128)(2,1)S(1)} %collective-permute-done.10.refs_9_) | copy-start | bytes 786436
  69.0 6.5 %copy-start.17 = (bf16[128,1024]{1,0:T(8,128)(2,1)}, bf16[128,1024]{1,0:T(8,128)(2,1)S(1)}, u32[]{:S(2)}) copy-start(bf16[128,1024]{1,0:T(8,128)(2,1)S(1)} %collective-permute-done.9.refs_7_) | copy-start | bytes 786436
  69.0 0.7 copy-start.18
  69.7 0.7 copy-start.16
  75.5 1.3 %copy-start.4 = (bf16[16,464,128]{2,1,0:T(8,128)(2,1)}, bf16[16,464,128]{2,1,0:T(8,128)(2,1)S(1)}, u32[]{:S(2)}) copy-start(bf16[16,464,128]{2,1,0:T(8,128)(2,1)S(1)} %all-to-all-done.cols_any) | copy-start | bytes 5701636

commit v5 on v4

--- a/solution.py
+++ b/solution.py
@@ -57,10 +57,10 @@
     return hi, (square - hi.astype(jnp.float32)).astype(jnp.bfloat16)
 
 
-def merge_kernel(experts, cap, order, count, me_ref, cols_any, weight_ref, *refs):
-    fisher_ref, merged_ref, left_hi, left_lo, right_hi, right_lo = refs[-11:-5]
-    pick, left_pick, scale_ref, cols_ref, sem = refs[-5:]
-    blocks = refs[:-11]
+def merge_kernel(experts, cap, order, count, me_ref, cols_ref, weight_ref, *refs):
+    fisher_ref, merged_ref, left_hi, left_lo, right_hi, right_lo = refs[-9:-3]
+    pick, left_pick, scale_ref = refs[-3:]
+    blocks = refs[:-9]
     parts, tall, rows = cols_ref.shape
     depth = tall - 16
     span = parts * cap
@@ -68,9 +68,6 @@
     @pl.when(pl.program_id(0) == 0)
     def _():
         me = me_ref[0]
-        copy = pltpu.make_async_copy(cols_any, cols_ref, sem)
-        copy.start()
-        copy.wait()
         at = lax.broadcasted_iota(jnp.int32, (experts * cap, rows), 0).astype(jnp.float32)
         total = jnp.zeros((8, rows), jnp.float32)
         for place in range(parts):
@@ -180,7 +177,7 @@
         grid=(hidden // TILE,),
         in_specs=[
             pl.BlockSpec(memory_space=pltpu.SMEM),
-            pl.BlockSpec(memory_space=pl.ANY),
+            pl.BlockSpec((parts, depth + 16, rows), lambda f: (0, 0, 0), pipeline_mode=pl.Buffered(1)),
             pl.BlockSpec((experts, depth, TILE), lambda f: (0, 0, f)),
         ]
         + [pl.BlockSpec((rows, TILE), lambda f: (0, f))] * len(blocks),
@@ -200,8 +197,6 @@
             pltpu.VMEM((parts, experts * cap, rows), jnp.bfloat16),
             pltpu.VMEM((experts, TILE, (-(-TILE // cap) + 1) * rows), jnp.bfloat16),
             pltpu.VMEM((8, 128), jnp.float32),
-            pltpu.VMEM((parts, depth + 16, rows), jnp.bfloat16),
-            pltpu.SemaphoreType.DMA,
         ],
         compiler_params=pltpu.CompilerParams(vmem_limit_bytes=60 * 2**20),
         name="merge",

time: 95.9 us -> 95 us (level)
  Pallas kernels: 21.1 us -> 20.1 us
where the time goes in v5:
time: 95 us; the launch traced here: 94.6 us
  waiting for transfers between devices  42.6 us (45%)
  starting transfers between devices  24.3 us (26%)
  Pallas kernels  20.1 us (21%)
  local copies, waits for them, and re-layouts  5.79 us (6%)
  other arithmetic  0.98 us (1%)
    ppermute x14, waiting for transfers between devices, swap(): return lax.ppermute(value, 'tok', [(s, s ^ flip) for s in range(parts)])  37.6 us
    pallas_call x1, Pallas kernels, local(): pl.pallas_call(functools.partial(merge_kernel, experts, cap, tuple(order)...  17.9 us
    ppermute x14, starting transfers between devices, swap(): return lax.ppermute(value, 'tok', [(s, s ^ flip) for s in range(parts)])  10.3 us
    all_to_all x1, starting transfers between devices, local(): lax.all_to_all(turned, 'tok', split_axis=0, concat_axis=0, tiled=True)  9.37 us
    unnamed x38, local copies, waits for them, and re-layouts  5.79 us
    all_to_all x1, waiting for transfers between devices, local(): lax.all_to_all(turned, 'tok', split_axis=0, concat_axis=0, tiled=True)  5.01 us
    ppermute x1, starting transfers between devices, local(): out = lax.ppermute(second, 'tok', outward)  2.6 us
    pallas_call x1, Pallas kernels, local(): pl.pallas_call(functools.partial(turn_kernel, experts, cap), out_shape=pl...  2.2 us
  transfers between devices with their start and end apart: 17, of which 5 were waited for; matrix products, arithmetic and copies ran while one was open for 1% of the time, Pallas kernels for 2%

profile of v5, /device:TPU:13, one launch (start us, length us, event | category | flops | bytes accessed | tf_op | source)
XLA Modules:
  0.0 94.6 jit_solution(18333938094343960271)
XLA Ops:
  0.6 2.4 %collective-permute-start.3 = (bf16[128,1024]{1,0:T(8,128)(2,1)}, bf16[128,1024]{1,0:T(8,128)(2,1)S(1)}, u32[]{:S(2)}, u32[]{:S(2)}) collective-permute-start(bf16[128,1024]{1,0:T(8,128)(2,1)} %refs_0_.1), channel_id=1, source_target_pairs={{0,8},{1,9},{2,10},{3,11},{4,12},{5,13},{6,14},{7,15},{8,0},{9,1},... | collective-permute-start | bytes 786440 | tf_op jit(solution)/shard_map/ppermute | solution.py:136
  3.0 0.2 collective-permute-start.2
  3.2 0.2 collective-permute-start.1
  3.4 2.1 %collective-permute-start = (bf16[128,1024]{1,0:T(8,128)(2,1)}, bf16[128,1024]{1,0:T(8,128)(2,1)}, u32[]{:S(2)}, u32[]{:S(2)}) collective-permute-start(bf16[128,1024]{1,0:T(8,128)(2,1)} %refs_0_.1), channel_id=1, source_target_pairs={{4,8},{5,9},{6,10},{7,11},{8,4},{9,5},{10,6},{11,7},{20,24},{21,25... | collective-permute-start | bytes 786440 | tf_op jit(solution)/shard_map/ppermute | solution.py:154
  5.5 9.3 %collective-permute-done.3.refs_8_ = bf16[128,1024]{1,0:T(8,128)(2,1)S(1)} collective-permute-done((bf16[128,1024]{1,0:T(8,128)(2,1)}, bf16[128,1024]{1,0:T(8,128)(2,1)S(1)}, u32[]{:S(2)}, u32[]{:S(2)}) %collective-permute-start.3) | collective-permute-done | bytes 262176 | tf_op jit(solution)/shard_map/ppermute | solution.py:136
  14.9 0.0 collective-permute-done.2.refs_4_
  14.9 0.0 copy-start.7
  14.9 0.0 collective-permute-done.1.refs_2_
  14.9 0.0 copy-start.8
  14.9 2.6 %collective-permute-start.4 = (bf16[128,1024]{1,0:T(8,128)(2,1)S(1)}, bf16[128,1024]{1,0:T(8,128)(2,1)}, u32[]{:S(2)}, u32[]{:S(2)}) collective-permute-start(bf16[128,1024]{1,0:T(8,128)(2,1)S(1)} %collective-permute-done.3.refs_8_), channel_id=1, source_target_pairs={{4,0},{5,1},{6,2},{7,3},{8,12},{9,13},{10,14},{11,15},{20,16},{21,... | collective-permute-start | bytes 786440 | tf_op jit(solution)/shard_map/ppermute | solution.py:155
  17.5 0.0 copy-start
  17.5 1.5 %copy-done = bf16[128,7168]{1,0:T(8,128)(2,1)S(1)} copy-done((bf16[128,7168]{1,0:T(8,128)(2,1)S(1)}, bf16[128,7168]{1,0:T(8,128)(2,1)}, u32[]{:S(2)}) %copy-start) | copy-done | bytes 1835032
  19.0 0.0 copy-start.1
  19.0 0.9 %copy-done.1 = bf16[128,1024]{1,0:T(8,128)(2,1)S(1)} copy-done((bf16[128,1024]{1,0:T(8,128)(2,1)S(1)}, bf16[128,1024]{1,0:T(8,128)(2,1)}, u32[]{:S(2)}) %copy-start.1) | copy-done | bytes 262168
  19.9 0.7 copy-done.3
  20.6 2.2 %turn.1 = bf16[16,464,128]{2,1,0:T(8,128)(2,1)} custom-call(bf16[128,7168]{1,0:T(8,128)(2,1)S(1)} %copy-done, bf16[128,1024]{1,0:T(8,128)(2,1)S(1)} %copy-done.1, s32[1,128]{1,0:T(1,128)S(1)} %bitcast.2), custom_call_target="tpu_custom_call" | custom-call | tf_op jit(solution)/shard_map/turn/pallas_call | solution.py:138
  22.8 0.0 collective-permute-done
  22.8 0.0 collective-permute-done.4
  22.8 9.4 %all-to-all-start = ((bf16[16,464,128]{2,1,0:T(8,128)(2,1)}), bf16[16,464,128]{2,1,0:T(8,128)(2,1)S(1)}, u32[]{:S(2)}, u32[]{:S(2)}) async-start(bf16[16,464,128]{2,1,0:T(8,128)(2,1)} %turn.1), calls=%async_computation | async-start | bytes 3801088 | tf_op jit(solution)/shard_map/all_to_all | solution.py:173
  32.2 0.0 copy-done.2
  32.2 0.4 collective-permute-start.5
  32.6 0.3 collective-permute-start.8
  32.9 0.0 copy-done.7
  32.9 0.4 collective-permute-start.7
  33.3 1.2 %collective-permute-start.11 = (bf16[128,1024]{1,0:T(8,128)(2,1)S(1)}, bf16[128,1024]{1,0:T(8,128)(2,1)S(1)}, u32[]{:S(2)}, u32[]{:S(2)}) collective-permute-start(bf16[128,1024]{1,0:T(8,128)(2,1)S(1)} %collective-permute-done.3.refs_8_), channel_id=1, source_target_pairs={{0,2},{1,3},{2,0},{3,1},{4,6},{5,7},{6,4},{7,5},{8,10},{9,11},{10,... | collective-permute-start | bytes 786440 | tf_op jit(solution)/shard_map/ppermute | solution.py:136
  34.5 0.0 copy-done.8
  34.5 0.3 collective-permute-start.6
  34.9 1.0 %broadcast_select_fusion.refs_12_ = bf16[128,1024]{1,0:T(8,128)(2,1)S(1)} fusion(bf16[128,1024]{1,0:T(8,128)(2,1)} %collective-permute-done, bf16[128,1024]{1,0:T(8,128)(2,1)} %collective-permute-done.4, pred[]{:T(512)S(6)} %or.3), kind=kLoop, calls=%fused_computation | loop fusion | flops 131072 | bytes 786433 | tf_op jit(solution)/shard_map/jit(_where)/select_n | solution.py:160
  35.8 0.0 copy-start.5
  35.9 0.0 collective-permute-done.5.refs_1_
  35.9 0.0 copy-start.9
  35.9 0.3 collective-permute-start.14
  36.2 0.0 collective-permute-done.6.refs_3_
  36.2 0.0 copy-done.6
  36.2 0.5 collective-permute-start.10
  36.7 12.5 %collective-permute-done.8.refs_6_ = bf16[128,1024]{1,0:T(8,128)(2,1)S(1)} collective-permute-done((bf16[128,1024]{1,0:T(8,128)(2,1)S(1)}, bf16[128,1024]{1,0:T(8,128)(2,1)S(1)}, u32[]{:S(2)}, u32[]{:S(2)}) %collective-permute-start.8) | collective-permute-done | bytes 262176 | tf_op jit(solution)/shard_map/ppermute | solution.py:136
  49.2 1.4 %collective-permute-start.13 = (bf16[128,1024]{1,0:T(8,128)(2,1)S(1)}, bf16[128,1024]{1,0:T(8,128)(2,1)S(1)}, u32[]{:S(2)}, u32[]{:S(2)}) collective-permute-start(bf16[128,1024]{1,0:T(8,128)(2,1)S(1)} %broadcast_select_fusion.refs_12_), channel_id=1, source_target_pairs={{0,1},{1,0},{2,3},{3,2},{4,5},{5,4},{6,7},{7,6},{8,9},{9,8},{10,11... | collective-permute-start | bytes 786440 | tf_op jit(solution)/shard_map/ppermute | solution.py:136
  50.6 0.0 collective-permute-done.7.refs_5_
  50.6 0.1 collective-permute-start.9
  50.7 6.7 %collective-permute-done.11.refs_10_ = bf16[128,1024]{1,0:T(8,128)(2,1)S(1)} collective-permute-done((bf16[128,1024]{1,0:T(8,128)(2,1)S(1)}, bf16[128,1024]{1,0:T(8,128)(2,1)S(1)}, u32[]{:S(2)}, u32[]{:S(2)}) %collective-permute-start.11) | collective-permute-done | bytes 262176 | tf_op jit(solution)/shard_map/ppermute | solution.py:136
  57.4 1.6 %collective-permute-start.12 = (bf16[128,1024]{1,0:T(8,128)(2,1)S(1)}, bf16[128,1024]{1,0:T(8,128)(2,1)S(1)}, u32[]{:S(2)}, u32[]{:S(2)}) collective-permute-start(bf16[128,1024]{1,0:T(8,128)(2,1)S(1)} %collective-permute-done.11.refs_10_), channel_id=1, source_target_pairs={{0,1},{1,0},{2,3},{3,2},{4,5},{5,4},{6,7},{7,6},{8,9},{9,8},{10,11... | collective-permute-start | bytes 786440 | tf_op jit(solution)/shard_map/ppermute | solution.py:136
  59.1 9.0 %collective-permute-done.14.refs_14_ = bf16[128,1024]{1,0:T(8,128)(2,1)S(1)} collective-permute-done((bf16[128,1024]{1,0:T(8,128)(2,1)S(1)}, bf16[128,1024]{1,0:T(8,128)(2,1)S(1)}, u32[]{:S(2)}, u32[]{:S(2)}) %collective-permute-start.14) | collective-permute-done | bytes 262176 | tf_op jit(solution)/shard_map/ppermute | solution.py:136
  68.1 0.9 collective-permute-start.15
  69.0 0.0 collective-permute-done.10.refs_9_
  69.0 0.0 collective-permute-done.9.refs_7_
  69.0 0.0 copy-start.17
  69.0 0.0 collective-permute-done.12.refs_11_
  69.0 0.0 copy-start.18
  69.0 0.0 collective-permute-done.13.refs_13_
  69.0 0.0 copy-done.13
  69.0 0.0 copy-done.10
  69.0 0.0 copy-done.11
  69.0 0.0 copy-done.12
  69.1 0.7 copy-done.18
  69.7 0.7 copy-done.16
  70.4 0.0 collective-permute-done.15.refs_15_
  70.4 5.0 %all-to-all-done.cols_ref = bf16[16,464,128]{2,1,0:T(8,128)(2,1)S(1)} async-done(((bf16[16,464,128]{2,1,0:T(8,128)(2,1)}), bf16[16,464,128]{2,1,0:T(8,128)(2,1)S(1)}, u32[]{:S(2)}, u32[]{:S(2)}) %all-to-all-start) | async-done | bytes 1900576 | tf_op jit(solution)/shard_map/all_to_all | solution.py:173
  75.5 0.0 copy-done.5
  75.5 0.0 copy-done.9
  75.5 0.0 copy-done.14
  75.5 0.0 copy-done.15
  75.5 0.0 copy-done.17
  75.5 1.2 %copy-done.4 = bf16[16,464,128]{2,1,0:T(8,128)(2,1)} copy-done((bf16[16,464,128]{2,1,0:T(8,128)(2,1)}, bf16[16,464,128]{2,1,0:T(8,128)(2,1)S(1)}, u32[]{:S(2)}) %copy-start.4) | copy-done | bytes 1900568
  76.7 17.9 %merge.1 = (f32[4,448,1024]{2,1,0:T(8,128)}, bf16[448,1024]{1,0:T(8,128)(2,1)}) custom-call(s32[1]{0:T(128)} %bitcast.me_ref, bf16[16,464,128]{2,1,0:T(8,128)(2,1)} %copy-done.4, bf16[4,448,1024]{2,1,0:T(8,128)(2,1)} %weight_ref.1, bf16[128,1024]{1,0:T(8,128)(2,1)} %refs_0_.1, bf16[128,1024]{1,0:T(8,128)(2,1)} %copy-done.9, bf16[128,1024]{1,0:T(8,128)(2,1)} %copy-done.8, ...), custom_call_target="tpu_custom_call" | custom-call | tf_op jit(solution)/shard_map/merge/pallas_call | solution.py:175
  (11 shorter events, 0.0 us)
Async XLA Ops:
  0.6 14.2 %collective-permute-start.3 = (bf16[128,1024]{1,0:T(8,128)(2,1)}, bf16[128,1024]{1,0:T(8,128)(2,1)S(1)}, u32[]{:S(2)}, u32[]{:S(2)}) collective-permute-start(bf16[128,1024]{1,0:T(8,128)(2,1)} %refs_0_.1), channel_id=1, source_target_pairs={{0,8},{1,9},{2,10},{3,11},{4,12},{5,13},{6,14},{7,15},{8,0},{9,1},... | collective-permute-start | bytes 786440 | tf_op jit(solution)/shard_map/ppermute | solution.py:136
  3.0 11.9 %collective-permute-start.2 = (bf16[128,1024]{1,0:T(8,128)(2,1)}, bf16[128,1024]{1,0:T(8,128)(2,1)S(1)}, u32[]{:S(2)}, u32[]{:S(2)}) collective-permute-start(bf16[128,1024]{1,0:T(8,128)(2,1)} %refs_0_.1), channel_id=1, source_target_pairs={{0,4},{1,5},{2,6},{3,7},{4,0},{5,1},{6,2},{7,3},{8,12},{9,13},{10,... | collective-permute-start | bytes 786440 | tf_op jit(solution)/shard_map/ppermute | solution.py:136
  3.2 11.7 %collective-permute-start.1 = (bf16[128,1024]{1,0:T(8,128)(2,1)}, bf16[128,1024]{1,0:T(8,128)(2,1)S(1)}, u32[]{:S(2)}, u32[]{:S(2)}) collective-permute-start(bf16[128,1024]{1,0:T(8,128)(2,1)} %refs_0_.1), channel_id=1, source_target_pairs={{0,2},{1,3},{2,0},{3,1},{4,6},{5,7},{6,4},{7,5},{8,10},{9,11},{10,... | collective-permute-start | bytes 786440 | tf_op jit(solution)/shard_map/ppermute | solution.py:136
  3.4 19.4 %collective-permute-start = (bf16[128,1024]{1,0:T(8,128)(2,1)}, bf16[128,1024]{1,0:T(8,128)(2,1)}, u32[]{:S(2)}, u32[]{:S(2)}) collective-permute-start(bf16[128,1024]{1,0:T(8,128)(2,1)} %refs_0_.1), channel_id=1, source_target_pairs={{4,8},{5,9},{6,10},{7,11},{8,4},{9,5},{10,6},{11,7},{20,24},{21,25... | collective-permute-start | bytes 786440 | tf_op jit(solution)/shard_map/ppermute | solution.py:154
  14.9 21.4 %copy-start.6 = (bf16[128,1024]{1,0:T(8,128)(2,1)}, bf16[128,1024]{1,0:T(8,128)(2,1)S(1)}, u32[]{:S(2)}) copy-start(bf16[128,1024]{1,0:T(8,128)(2,1)S(1)} %collective-permute-done.3.refs_8_) | copy-start | bytes 786436
  14.9 18.0 %copy-start.7 = (bf16[128,1024]{1,0:T(8,128)(2,1)}, bf16[128,1024]{1,0:T(8,128)(2,1)S(1)}, u32[]{:S(2)}) copy-start(bf16[128,1024]{1,0:T(8,128)(2,1)S(1)} %collective-permute-done.2.refs_4_) | copy-start | bytes 786436
  14.9 19.6 %copy-start.8 = (bf16[128,1024]{1,0:T(8,128)(2,1)}, bf16[128,1024]{1,0:T(8,128)(2,1)S(1)}, u32[]{:S(2)}) copy-start(bf16[128,1024]{1,0:T(8,128)(2,1)S(1)} %collective-permute-done.1.refs_2_) | copy-start | bytes 786436
  14.9 7.9 %collective-permute-start.4 = (bf16[128,1024]{1,0:T(8,128)(2,1)S(1)}, bf16[128,1024]{1,0:T(8,128)(2,1)}, u32[]{:S(2)}, u32[]{:S(2)}) collective-permute-start(bf16[128,1024]{1,0:T(8,128)(2,1)S(1)} %collective-permute-done.3.refs_8_), channel_id=1, source_target_pairs={{4,0},{5,1},{6,2},{7,3},{8,12},{9,13},{10,14},{11,15},{20,16},{21,... | collective-permute-start | bytes 786440 | tf_op jit(solution)/shard_map/ppermute | solution.py:155
  17.5 1.5 %copy-start = (bf16[128,7168]{1,0:T(8,128)(2,1)S(1)}, bf16[128,7168]{1,0:T(8,128)(2,1)}, u32[]{:S(2)}) copy-start(bf16[128,7168]{1,0:T(8,128)(2,1)} %tok_ref.1) | copy-start | bytes 5505028
  19.0 0.9 %copy-start.1 = (bf16[128,1024]{1,0:T(8,128)(2,1)S(1)}, bf16[128,1024]{1,0:T(8,128)(2,1)}, u32[]{:S(2)}) copy-start(bf16[128,1024]{1,0:T(8,128)(2,1)} %refs_0_.1) | copy-start | bytes 786436
  19.9 0.7 copy-start.3
  22.8 9.4 %copy-start.2 = (bf16[128,1024]{1,0:T(8,128)(2,1)S(1)}, bf16[128,1024]{1,0:T(8,128)(2,1)}, u32[]{:S(2)}) copy-start(bf16[128,1024]{1,0:T(8,128)(2,1)} %refs_0_.1) | copy-start | bytes 786436
  22.8 52.7 %all-to-all-start = ((bf16[16,464,128]{2,1,0:T(8,128)(2,1)}), bf16[16,464,128]{2,1,0:T(8,128)(2,1)S(1)}, u32[]{:S(2)}, u32[]{:S(2)}) async-start(bf16[16,464,128]{2,1,0:T(8,128)(2,1)} %turn.1), calls=%async_computation | async-start | bytes 3801088 | tf_op jit(solution)/shard_map/all_to_all | solution.py:173
  32.2 3.7 %collective-permute-start.5 = (bf16[128,1024]{1,0:T(8,128)(2,1)S(1)}, bf16[128,1024]{1,0:T(8,128)(2,1)S(1)}, u32[]{:S(2)}, u32[]{:S(2)}) collective-permute-start(bf16[128,1024]{1,0:T(8,128)(2,1)S(1)} %copy-done.2), channel_id=1, source_target_pairs={{0,1},{1,0},{2,3},{3,2},{4,5},{5,4},{6,7},{7,6},{8,9},{9,8},{10,11... | collective-permute-start | bytes 786440 | tf_op jit(solution)/shard_map/ppermute | solution.py:136
  32.6 16.6 %collective-permute-start.8 = (bf16[128,1024]{1,0:T(8,128)(2,1)S(1)}, bf16[128,1024]{1,0:T(8,128)(2,1)S(1)}, u32[]{:S(2)}, u32[]{:S(2)}) collective-permute-start(bf16[128,1024]{1,0:T(8,128)(2,1)S(1)} %collective-permute-done.2.refs_4_), channel_id=1, source_target_pairs={{0,2},{1,3},{2,0},{3,1},{4,6},{5,7},{6,4},{7,5},{8,10},{9,11},{10,... | collective-permute-start | bytes 786440 | tf_op jit(solution)/shard_map/ppermute | solution.py:136
  32.9 17.7 %collective-permute-start.7 = (bf16[128,1024]{1,0:T(8,128)(2,1)S(1)}, bf16[128,1024]{1,0:T(8,128)(2,1)S(1)}, u32[]{:S(2)}, u32[]{:S(2)}) collective-permute-start(bf16[128,1024]{1,0:T(8,128)(2,1)S(1)} %collective-permute-done.2.refs_4_), channel_id=1, source_target_pairs={{0,1},{1,0},{2,3},{3,2},{4,5},{5,4},{6,7},{7,6},{8,9},{9,8},{10,11... | collective-permute-start | bytes 786440 | tf_op jit(solution)/shard_map/ppermute | solution.py:136
  33.3 24.1 %collective-permute-start.11 = (bf16[128,1024]{1,0:T(8,128)(2,1)S(1)}, bf16[128,1024]{1,0:T(8,128)(2,1)S(1)}, u32[]{:S(2)}, u32[]{:S(2)}) collective-permute-start(bf16[128,1024]{1,0:T(8,128)(2,1)S(1)} %collective-permute-done.3.refs_8_), channel_id=1, source_target_pairs={{0,2},{1,3},{2,0},{3,1},{4,6},{5,7},{6,4},{7,5},{8,10},{9,11},{10,... | collective-permute-start | bytes 786440 | tf_op jit(solution)/shard_map/ppermute | solution.py:136
  34.5 1.7 %collective-permute-start.6 = (bf16[128,1024]{1,0:T(8,128)(2,1)S(1)}, bf16[128,1024]{1,0:T(8,128)(2,1)S(1)}, u32[]{:S(2)}, u32[]{:S(2)}) collective-permute-start(bf16[128,1024]{1,0:T(8,128)(2,1)S(1)} %collective-permute-done.1.refs_2_), channel_id=1, source_target_pairs={{0,1},{1,0},{2,3},{3,2},{4,5},{5,4},{6,7},{7,6},{8,9},{9,8},{10,11... | collective-permute-start | bytes 786440 | tf_op jit(solution)/shard_map/ppermute | solution.py:136
  35.8 39.6 %copy-start.5 = (bf16[128,1024]{1,0:T(8,128)(2,1)}, bf16[128,1024]{1,0:T(8,128)(2,1)S(1)}, u32[]{:S(2)}) copy-start(bf16[128,1024]{1,0:T(8,128)(2,1)S(1)} %broadcast_select_fusion.refs_12_) | copy-start | bytes 786436
  35.9 39.6 %copy-start.9 = (bf16[128,1024]{1,0:T(8,128)(2,1)}, bf16[128,1024]{1,0:T(8,128)(2,1)S(1)}, u32[]{:S(2)}) copy-start(bf16[128,1024]{1,0:T(8,128)(2,1)S(1)} %collective-permute-done.5.refs_1_) | copy-start | bytes 786436
  35.9 32.2 %collective-permute-start.14 = (bf16[128,1024]{1,0:T(8,128)(2,1)S(1)}, bf16[128,1024]{1,0:T(8,128)(2,1)S(1)}, u32[]{:S(2)}, u32[]{:S(2)}) collective-permute-start(bf16[128,1024]{1,0:T(8,128)(2,1)S(1)} %broadcast_select_fusion.refs_12_), channel_id=1, source_target_pairs={{0,2},{1,3},{2,0},{3,1},{4,6},{5,7},{6,4},{7,5},{8,10},{9,11},{10,... | collective-permute-start | bytes 786440 | tf_op jit(solution)/shard_map/ppermute | solution.py:136
  36.2 32.8 %copy-start.13 = (bf16[128,1024]{1,0:T(8,128)(2,1)}, bf16[128,1024]{1,0:T(8,128)(2,1)S(1)}, u32[]{:S(2)}) copy-start(bf16[128,1024]{1,0:T(8,128)(2,1)S(1)} %collective-permute-done.6.refs_3_) | copy-start | bytes 786436
  36.2 32.7 %collective-permute-start.10 = (bf16[128,1024]{1,0:T(8,128)(2,1)S(1)}, bf16[128,1024]{1,0:T(8,128)(2,1)S(1)}, u32[]{:S(2)}, u32[]{:S(2)}) collective-permute-start(bf16[128,1024]{1,0:T(8,128)(2,1)S(1)} %collective-permute-done.3.refs_8_), channel_id=1, source_target_pairs={{0,1},{1,0},{2,3},{3,2},{4,5},{5,4},{6,7},{7,6},{8,9},{9,8},{10,11... | collective-permute-start | bytes 786440 | tf_op jit(solution)/shard_map/ppermute | solution.py:136
  49.2 19.8 %copy-start.10 = (bf16[128,1024]{1,0:T(8,128)(2,1)}, bf16[128,1024]{1,0:T(8,128)(2,1)S(1)}, u32[]{:S(2)}) copy-start(bf16[128,1024]{1,0:T(8,128)(2,1)S(1)} %collective-permute-done.8.refs_6_) | copy-start | bytes 786436
  49.2 19.8 %collective-permute-start.13 = (bf16[128,1024]{1,0:T(8,128)(2,1)S(1)}, bf16[128,1024]{1,0:T(8,128)(2,1)S(1)}, u32[]{:S(2)}, u32[]{:S(2)}) collective-permute-start(bf16[128,1024]{1,0:T(8,128)(2,1)S(1)} %broadcast_select_fusion.refs_12_), channel_id=1, source_target_pairs={{0,1},{1,0},{2,3},{3,2},{4,5},{5,4},{6,7},{7,6},{8,9},{9,8},{10,11... | collective-permute-start | bytes 786440 | tf_op jit(solution)/shard_map/ppermute | solution.py:136
  50.6 18.4 %copy-start.11 = (bf16[128,1024]{1,0:T(8,128)(2,1)}, bf16[128,1024]{1,0:T(8,128)(2,1)S(1)}, u32[]{:S(2)}) copy-start(bf16[128,1024]{1,0:T(8,128)(2,1)S(1)} %collective-permute-done.7.refs_5_) | copy-start | bytes 786436
  50.6 18.4 %collective-permute-start.9 = (bf16[128,1024]{1,0:T(8,128)(2,1)S(1)}, bf16[128,1024]{1,0:T(8,128)(2,1)S(1)}, u32[]{:S(2)}, u32[]{:S(2)}) collective-permute-start(bf16[128,1024]{1,0:T(8,128)(2,1)S(1)} %collective-permute-done.8.refs_6_), channel_id=1, source_target_pairs={{0,1},{1,0},{2,3},{3,2},{4,5},{5,4},{6,7},{7,6},{8,9},{9,8},{10,11... | collective-permute-start | bytes 786440 | tf_op jit(solution)/shard_map/ppermute | solution.py:136
  57.4 11.6 %copy-start.12 = (bf16[128,1024]{1,0:T(8,128)(2,1)}, bf16[128,1024]{1,0:T(8,128)(2,1)S(1)}, u32[]{:S(2)}) copy-start(bf16[128,1024]{1,0:T(8,128)(2,1)S(1)} %collective-permute-done.11.refs_10_) | copy-start | bytes 786436
  57.4 11.6 %collective-permute-start.12 = (bf16[128,1024]{1,0:T(8,128)(2,1)S(1)}, bf16[128,1024]{1,0:T(8,128)(2,1)S(1)}, u32[]{:S(2)}, u32[]{:S(2)}) collective-permute-start(bf16[128,1024]{1,0:T(8,128)(2,1)S(1)} %collective-permute-done.11.refs_10_), channel_id=1, source_target_pairs={{0,1},{1,0},{2,3},{3,2},{4,5},{5,4},{6,7},{7,6},{8,9},{9,8},{10,11... | collective-permute-start | bytes 786440 | tf_op jit(solution)/shard_map/ppermute | solution.py:136
  68.1 7.4 %copy-start.14 = (bf16[128,1024]{1,0:T(8,128)(2,1)}, bf16[128,1024]{1,0:T(8,128)(2,1)S(1)}, u32[]{:S(2)}) copy-start(bf16[128,1024]{1,0:T(8,128)(2,1)S(1)} %collective-permute-done.14.refs_14_) | copy-start | bytes 786436
  68.1 2.4 %collective-permute-start.15 = (bf16[128,1024]{1,0:T(8,128)(2,1)S(1)}, bf16[128,1024]{1,0:T(8,128)(2,1)}, u32[]{:S(2)}, u32[]{:S(2)}) collective-permute-start(bf16[128,1024]{1,0:T(8,128)(2,1)S(1)} %collective-permute-done.14.refs_14_), channel_id=1, source_target_pairs={{0,1},{1,0},{2,3},{3,2},{4,5},{5,4},{6,7},{7,6},{8,9},{9,8},{10,11... | collective-permute-start | bytes 786440 | tf_op jit(solution)/shard_map/ppermute | solution.py:136
  69.0 6.5 %copy-start.15 = (bf16[128,1024]{1,0:T(8,128)(2,1)}, bf16[128,1024]{1,0:T(8,128)(2,1)S(1)}, u32[]{:S(2)}) copy-start(bf16[128,1024]{1,0:T(8,128)(2,1)S(1)} %collective-permute-done.10.refs_9_) | copy-start | bytes 786436
  69.0 6.5 %copy-start.17 = (bf16[128,1024]{1,0:T(8,128)(2,1)}, bf16[128,1024]{1,0:T(8,128)(2,1)S(1)}, u32[]{:S(2)}) copy-start(bf16[128,1024]{1,0:T(8,128)(2,1)S(1)} %collective-permute-done.9.refs_7_) | copy-start | bytes 786436
  69.0 0.7 copy-start.18
  69.7 0.7 copy-start.16
  75.5 1.3 %copy-start.4 = (bf16[16,464,128]{2,1,0:T(8,128)(2,1)}, bf16[16,464,128]{2,1,0:T(8,128)(2,1)S(1)}, u32[]{:S(2)}) copy-start(bf16[16,464,128]{2,1,0:T(8,128)(2,1)S(1)} %all-to-all-done.cols_ref) | copy-start | bytes 5701636

commit v6 on v5

--- a/solution.py
+++ b/solution.py
@@ -177,7 +177,7 @@
         grid=(hidden // TILE,),
         in_specs=[
             pl.BlockSpec(memory_space=pltpu.SMEM),
-            pl.BlockSpec((parts, depth + 16, rows), lambda f: (0, 0, 0), pipeline_mode=pl.Buffered(1)),
+            pl.BlockSpec(memory_space=pltpu.VMEM),
             pl.BlockSpec((experts, depth, TILE), lambda f: (0, 0, f)),
         ]
         + [pl.BlockSpec((rows, TILE), lambda f: (0, f))] * len(blocks),
@@ -198,7 +198,7 @@
             pltpu.VMEM((experts, TILE, (-(-TILE // cap) + 1) * rows), jnp.bfloat16),
             pltpu.VMEM((8, 128), jnp.float32),
         ],
-        compiler_params=pltpu.CompilerParams(vmem_limit_bytes=60 * 2**20),
+        compiler_params=pltpu.CompilerParams(vmem_limit_bytes=52 * 2**20),
         name="merge",
     )(me.astype(jnp.int32)[None], columns, weights, *blocks)
     return (fisher, merged)

time: 95 us -> 93.6 us (0.985)
  waiting for transfers between devices: 42.6 us -> 44.7 us
  local copies, waits for them, and re-layouts: 5.79 us -> 3.96 us
    unnamed x38 -> x24, local copies, waits for them, and re-layouts: 5.79 us -> 3.96 us
    ppermute x14, waiting for transfers between devices: 37.6 us -> 39.4 us  [swap(): return lax.ppermute(value, 'tok', [(s, s ^ flip) for s in range(parts)])]
    select_n x1, other arithmetic: 0.98 us -> 0.03 us  [local(): third = jnp.where(inner, far, out)]
  transfers between devices with their start and end apart: 17 -> 17, of which waited for: 5 -> 7; matrix products, arithmetic and copies ran while one was open for 1% -> 0% of each run, Pallas kernels for 2% -> 2%
where the time goes in v6:
time: 93.6 us; the launch traced here: 93.3 us
  waiting for transfers between devices  44.7 us (48%)
  starting transfers between devices  23.8 us (25%)
  Pallas kernels  20 us (21%)
  local copies, waits for them, and re-layouts  3.96 us (4%)
    ppermute x14, waiting for transfers between devices, swap(): return lax.ppermute(value, 'tok', [(s, s ^ flip) for s in range(parts)])  39.4 us
    pallas_call x1, Pallas kernels, local(): pl.pallas_call(functools.partial(merge_kernel, experts, cap, tuple(order)...  17.8 us
    all_to_all x1, starting transfers between devices, local(): lax.all_to_all(turned, 'tok', split_axis=0, concat_axis=0, tiled=True)  9.95 us
    ppermute x14, starting transfers between devices, swap(): return lax.ppermute(value, 'tok', [(s, s ^ flip) for s in range(parts)])  9.87 us
    all_to_all x1, waiting for transfers between devices, local(): lax.all_to_all(turned, 'tok', split_axis=0, concat_axis=0, tiled=True)  5.31 us
    unnamed x24, local copies, waits for them, and re-layouts  3.96 us
    pallas_call x1, Pallas kernels, local(): pl.pallas_call(functools.partial(turn_kernel, experts, cap), out_shape=pl...  2.2 us
    ppermute x1, starting transfers between devices, local(): far = lax.ppermute(out_grads, 'tok', inward)  2.09 us
  transfers between devices with their start and end apart: 17, of which 7 were waited for; matrix products, arithmetic and copies ran while one was open for 0% of the time, Pallas kernels for 2%

profile of v6, /device:TPU:13, one launch (start us, length us, event | category | flops | bytes accessed | tf_op | source)
XLA Modules:
  0.0 93.3 jit_solution(9641847196849958116)
XLA Ops:
  0.6 2.4 %collective-permute-start.3 = (bf16[128,1024]{1,0:T(8,128)(2,1)}, bf16[128,1024]{1,0:T(8,128)(2,1)S(1)}, u32[]{:S(2)}, u32[]{:S(2)}) collective-permute-start(bf16[128,1024]{1,0:T(8,128)(2,1)} %refs_0_.1), channel_id=1, source_target_pairs={{0,8},{1,9},{2,10},{3,11},{4,12},{5,13},{6,14},{7,15},{8,0},{9,1},... | collective-permute-start | bytes 786440 | tf_op jit(solution)/shard_map/ppermute | solution.py:136
  3.0 0.2 collective-permute-start.2
  3.2 0.2 collective-permute-start.1
  3.4 2.1 %collective-permute-start = (bf16[128,1024]{1,0:T(8,128)(2,1)}, bf16[128,1024]{1,0:T(8,128)(2,1)S(1)}, u32[]{:S(2)}, u32[]{:S(2)}) collective-permute-start(bf16[128,1024]{1,0:T(8,128)(2,1)} %refs_0_.1), channel_id=1, source_target_pairs={{4,8},{5,9},{6,10},{7,11},{8,4},{9,5},{10,6},{11,7},{20,24},{21,25... | collective-permute-start | bytes 786440 | tf_op jit(solution)/shard_map/ppermute | solution.py:154
  5.5 9.3 %collective-permute-done.3.refs_8_ = bf16[128,1024]{1,0:T(8,128)(2,1)S(1)} collective-permute-done((bf16[128,1024]{1,0:T(8,128)(2,1)}, bf16[128,1024]{1,0:T(8,128)(2,1)S(1)}, u32[]{:S(2)}, u32[]{:S(2)}) %collective-permute-start.3) | collective-permute-done | bytes 262176 | tf_op jit(solution)/shard_map/ppermute | solution.py:136
  14.9 0.0 copy-start.5
  14.9 0.0 collective-permute-done.2.refs_4_
  14.9 0.0 collective-permute-done.1.refs_2_
  14.9 1.9 %collective-permute-start.4 = (bf16[128,1024]{1,0:T(8,128)(2,1)S(1)}, bf16[128,1024]{1,0:T(8,128)(2,1)S(1)}, u32[]{:S(2)}, u32[]{:S(2)}) collective-permute-start(bf16[128,1024]{1,0:T(8,128)(2,1)S(1)} %collective-permute-done.3.refs_8_), channel_id=1, source_target_pairs={{4,0},{5,1},{6,2},{7,3},{8,12},{9,13},{10,14},{11,15},{20,16},{21,... | collective-permute-start | bytes 786440 | tf_op jit(solution)/shard_map/ppermute | solution.py:155
  16.8 0.0 copy-start
  16.8 1.5 %copy-done = bf16[128,7168]{1,0:T(8,128)(2,1)S(1)} copy-done((bf16[128,7168]{1,0:T(8,128)(2,1)S(1)}, bf16[128,7168]{1,0:T(8,128)(2,1)}, u32[]{:S(2)}) %copy-start) | copy-done | bytes 1835032
  18.3 0.0 copy-start.1
  18.3 0.9 %copy-done.1 = bf16[128,1024]{1,0:T(8,128)(2,1)S(1)} copy-done((bf16[128,1024]{1,0:T(8,128)(2,1)S(1)}, bf16[128,1024]{1,0:T(8,128)(2,1)}, u32[]{:S(2)}) %copy-start.1) | copy-done | bytes 262168
  19.2 0.0 copy-start.3
  19.2 0.7 copy-done.3
  19.9 2.2 %turn.1 = bf16[16,464,128]{2,1,0:T(8,128)(2,1)} custom-call(bf16[128,7168]{1,0:T(8,128)(2,1)S(1)} %copy-done, bf16[128,1024]{1,0:T(8,128)(2,1)S(1)} %copy-done.1, s32[1,128]{1,0:T(1,128)S(1)} %bitcast.2), custom_call_target="tpu_custom_call" | custom-call | tf_op jit(solution)/shard_map/turn/pallas_call | solution.py:138
  22.1 0.0 copy-start.2
  22.1 0.0 collective-permute-done
  22.1 0.0 collective-permute-done.4
  22.1 9.9 %all-to-all-start = ((bf16[16,464,128]{2,1,0:T(8,128)(2,1)}), bf16[16,464,128]{2,1,0:T(8,128)(2,1)}, u32[]{:S(2)}, u32[]{:S(2)}) async-start(bf16[16,464,128]{2,1,0:T(8,128)(2,1)} %turn.1), calls=%async_computation | async-start | bytes 3801088 | tf_op jit(solution)/shard_map/all_to_all | solution.py:173
  32.0 0.0 copy-done.2
  32.0 0.4 collective-permute-start.5
  32.5 0.3 collective-permute-start.8
  32.8 0.4 collective-permute-start.7
  33.2 1.2 %collective-permute-start.11 = (bf16[128,1024]{1,0:T(8,128)(2,1)S(1)}, bf16[128,1024]{1,0:T(8,128)(2,1)S(1)}, u32[]{:S(2)}, u32[]{:S(2)}) collective-permute-start(bf16[128,1024]{1,0:T(8,128)(2,1)S(1)} %collective-permute-done.3.refs_8_), channel_id=1, source_target_pairs={{0,2},{1,3},{2,0},{3,1},{4,6},{5,7},{6,4},{7,5},{8,10},{9,11},{10,... | collective-permute-start | bytes 786440 | tf_op jit(solution)/shard_map/ppermute | solution.py:136
  34.4 0.3 collective-permute-start.6
  34.8 0.0 copy-start.4
  34.8 0.0 collective-permute-done.5.refs_1_
  34.8 0.3 collective-permute-start.14
  35.1 0.8 collective-permute-done.6.refs_3_
  35.9 0.0 copy-done.5
  35.9 0.3 collective-permute-start.10
  36.3 12.9 %collective-permute-done.8.refs_6_ = bf16[128,1024]{1,0:T(8,128)(2,1)S(1)} collective-permute-done((bf16[128,1024]{1,0:T(8,128)(2,1)S(1)}, bf16[128,1024]{1,0:T(8,128)(2,1)S(1)}, u32[]{:S(2)}, u32[]{:S(2)}) %collective-permute-start.8) | collective-permute-done | bytes 262176 | tf_op jit(solution)/shard_map/ppermute | solution.py:136
  49.2 1.3 %collective-permute-start.13 = (bf16[128,1024]{1,0:T(8,128)(2,1)S(1)}, bf16[128,1024]{1,0:T(8,128)(2,1)S(1)}, u32[]{:S(2)}, u32[]{:S(2)}) collective-permute-start(bf16[128,1024]{1,0:T(8,128)(2,1)S(1)} %broadcast_select_fusion.refs_12_), channel_id=1, source_target_pairs={{0,1},{1,0},{2,3},{3,2},{4,5},{5,4},{6,7},{7,6},{8,9},{9,8},{10,11... | collective-permute-start | bytes 786440 | tf_op jit(solution)/shard_map/ppermute | solution.py:136
  50.5 0.0 collective-permute-done.7.refs_5_
  50.5 0.0 collective-permute-start.9
  50.5 6.9 %collective-permute-done.11.refs_10_ = bf16[128,1024]{1,0:T(8,128)(2,1)S(1)} collective-permute-done((bf16[128,1024]{1,0:T(8,128)(2,1)S(1)}, bf16[128,1024]{1,0:T(8,128)(2,1)S(1)}, u32[]{:S(2)}, u32[]{:S(2)}) %collective-permute-start.11) | collective-permute-done | bytes 262176 | tf_op jit(solution)/shard_map/ppermute | solution.py:136
  57.4 0.0 copy-start.6
  57.4 1.6 %collective-permute-start.12 = (bf16[128,1024]{1,0:T(8,128)(2,1)S(1)}, bf16[128,1024]{1,0:T(8,128)(2,1)S(1)}, u32[]{:S(2)}, u32[]{:S(2)}) collective-permute-start(bf16[128,1024]{1,0:T(8,128)(2,1)S(1)} %collective-permute-done.11.refs_10_), channel_id=1, source_target_pairs={{0,1},{1,0},{2,3},{3,2},{4,5},{5,4},{6,7},{7,6},{8,9},{9,8},{10,11... | collective-permute-start | bytes 786440 | tf_op jit(solution)/shard_map/ppermute | solution.py:136
  58.9 9.0 %collective-permute-done.14.refs_14_ = bf16[128,1024]{1,0:T(8,128)(2,1)S(1)} collective-permute-done((bf16[128,1024]{1,0:T(8,128)(2,1)S(1)}, bf16[128,1024]{1,0:T(8,128)(2,1)S(1)}, u32[]{:S(2)}, u32[]{:S(2)}) %collective-permute-start.14) | collective-permute-done | bytes 262176 | tf_op jit(solution)/shard_map/ppermute | solution.py:136
  68.0 0.0 copy-start.7
  68.0 0.9 collective-permute-start.15
  68.8 0.0 collective-permute-done.10.refs_9_
  68.8 0.0 copy-start.8
  68.8 0.0 collective-permute-done.9.refs_7_
  68.9 0.0 copy-start.10
  68.9 0.0 collective-permute-done.12.refs_11_
  68.9 0.0 copy-start.11
  68.9 0.0 collective-permute-done.13.refs_13_
  68.9 0.7 copy-done.10
  69.6 0.1 copy-done.11
  69.7 0.0 copy-start.9
  69.7 0.4 collective-permute-done.15.refs_15_
  70.1 5.3 %all-to-all-done.cols_ref = bf16[16,464,128]{2,1,0:T(8,128)(2,1)} async-done(((bf16[16,464,128]{2,1,0:T(8,128)(2,1)}), bf16[16,464,128]{2,1,0:T(8,128)(2,1)}, u32[]{:S(2)}, u32[]{:S(2)}) %all-to-all-start) | async-done | bytes 1900576 | tf_op jit(solution)/shard_map/all_to_all | solution.py:173
  75.4 0.0 copy-done.4
  75.4 0.0 copy-done.6
  75.4 0.0 copy-done.7
  75.5 0.0 copy-done.8
  75.5 0.0 copy-done.9
  75.5 17.8 %merge.1 = (f32[4,448,1024]{2,1,0:T(8,128)}, bf16[448,1024]{1,0:T(8,128)(2,1)}) custom-call(s32[1]{0:T(128)} %bitcast.me_ref, bf16[16,464,128]{2,1,0:T(8,128)(2,1)} %all-to-all-done.cols_ref, bf16[4,448,1024]{2,1,0:T(8,128)(2,1)} %weight_ref.1, bf16[128,1024]{1,0:T(8,128)(2,1)S(1)} %copy-done.2, bf16[128,1024]{1,0:T(8,128)(2,1)S(1)} %collective-permute-done.5.refs_1_, ...), custom_call_target="tpu_custom_call" | custom-call | tf_op jit(solution)/shard_map/merge/pallas_call | solution.py:175
  (1 shorter events, 0.0 us)
Async XLA Ops:
  0.6 14.2 %collective-permute-start.3 = (bf16[128,1024]{1,0:T(8,128)(2,1)}, bf16[128,1024]{1,0:T(8,128)(2,1)S(1)}, u32[]{:S(2)}, u32[]{:S(2)}) collective-permute-start(bf16[128,1024]{1,0:T(8,128)(2,1)} %refs_0_.1), channel_id=1, source_target_pairs={{0,8},{1,9},{2,10},{3,11},{4,12},{5,13},{6,14},{7,15},{8,0},{9,1},... | collective-permute-start | bytes 786440 | tf_op jit(solution)/shard_map/ppermute | solution.py:136
  3.0 11.9 %collective-permute-start.2 = (bf16[128,1024]{1,0:T(8,128)(2,1)}, bf16[128,1024]{1,0:T(8,128)(2,1)S(1)}, u32[]{:S(2)}, u32[]{:S(2)}) collective-permute-start(bf16[128,1024]{1,0:T(8,128)(2,1)} %refs_0_.1), channel_id=1, source_target_pairs={{0,4},{1,5},{2,6},{3,7},{4,0},{5,1},{6,2},{7,3},{8,12},{9,13},{10,... | collective-permute-start | bytes 786440 | tf_op jit(solution)/shard_map/ppermute | solution.py:136
  3.2 11.7 %collective-permute-start.1 = (bf16[128,1024]{1,0:T(8,128)(2,1)}, bf16[128,1024]{1,0:T(8,128)(2,1)S(1)}, u32[]{:S(2)}, u32[]{:S(2)}) collective-permute-start(bf16[128,1024]{1,0:T(8,128)(2,1)} %refs_0_.1), channel_id=1, source_target_pairs={{0,2},{1,3},{2,0},{3,1},{4,6},{5,7},{6,4},{7,5},{8,10},{9,11},{10,... | collective-permute-start | bytes 786440 | tf_op jit(solution)/shard_map/ppermute | solution.py:136
  3.4 18.7 %collective-permute-start = (bf16[128,1024]{1,0:T(8,128)(2,1)}, bf16[128,1024]{1,0:T(8,128)(2,1)S(1)}, u32[]{:S(2)}, u32[]{:S(2)}) collective-permute-start(bf16[128,1024]{1,0:T(8,128)(2,1)} %refs_0_.1), channel_id=1, source_target_pairs={{4,8},{5,9},{6,10},{7,11},{8,4},{9,5},{10,6},{11,7},{20,24},{21,25... | collective-permute-start | bytes 786440 | tf_op jit(solution)/shard_map/ppermute | solution.py:154
  14.9 21.1 %copy-start.5 = (bf16[128,1024]{1,0:T(8,128)(2,1)}, bf16[128,1024]{1,0:T(8,128)(2,1)S(1)}, u32[]{:S(2)}) copy-start(bf16[128,1024]{1,0:T(8,128)(2,1)S(1)} %collective-permute-done.3.refs_8_) | copy-start | bytes 786436
  14.9 7.2 %collective-permute-start.4 = (bf16[128,1024]{1,0:T(8,128)(2,1)S(1)}, bf16[128,1024]{1,0:T(8,128)(2,1)S(1)}, u32[]{:S(2)}, u32[]{:S(2)}) collective-permute-start(bf16[128,1024]{1,0:T(8,128)(2,1)S(1)} %collective-permute-done.3.refs_8_), channel_id=1, source_target_pairs={{4,0},{5,1},{6,2},{7,3},{8,12},{9,13},{10,14},{11,15},{20,16},{21,... | collective-permute-start | bytes 786440 | tf_op jit(solution)/shard_map/ppermute | solution.py:155
  16.8 1.5 %copy-start = (bf16[128,7168]{1,0:T(8,128)(2,1)S(1)}, bf16[128,7168]{1,0:T(8,128)(2,1)}, u32[]{:S(2)}) copy-start(bf16[128,7168]{1,0:T(8,128)(2,1)} %tok_ref.1) | copy-start | bytes 5505028
  18.3 0.9 %copy-start.1 = (bf16[128,1024]{1,0:T(8,128)(2,1)S(1)}, bf16[128,1024]{1,0:T(8,128)(2,1)}, u32[]{:S(2)}) copy-start(bf16[128,1024]{1,0:T(8,128)(2,1)} %refs_0_.1) | copy-start | bytes 786436
  19.2 0.7 copy-start.3
  22.1 10.0 %copy-start.2 = (bf16[128,1024]{1,0:T(8,128)(2,1)S(1)}, bf16[128,1024]{1,0:T(8,128)(2,1)}, u32[]{:S(2)}) copy-start(bf16[128,1024]{1,0:T(8,128)(2,1)} %refs_0_.1) | copy-start | bytes 786436
  22.1 53.3 %all-to-all-start = ((bf16[16,464,128]{2,1,0:T(8,128)(2,1)}), bf16[16,464,128]{2,1,0:T(8,128)(2,1)}, u32[]{:S(2)}, u32[]{:S(2)}) async-start(bf16[16,464,128]{2,1,0:T(8,128)(2,1)} %turn.1), calls=%async_computation | async-start | bytes 3801088 | tf_op jit(solution)/shard_map/all_to_all | solution.py:173
  32.0 2.7 %collective-permute-start.5 = (bf16[128,1024]{1,0:T(8,128)(2,1)S(1)}, bf16[128,1024]{1,0:T(8,128)(2,1)S(1)}, u32[]{:S(2)}, u32[]{:S(2)}) collective-permute-start(bf16[128,1024]{1,0:T(8,128)(2,1)S(1)} %copy-done.2), channel_id=1, source_target_pairs={{0,1},{1,0},{2,3},{3,2},{4,5},{5,4},{6,7},{7,6},{8,9},{9,8},{10,11... | collective-permute-start | bytes 786440 | tf_op jit(solution)/shard_map/ppermute | solution.py:136
  32.5 16.7 %collective-permute-start.8 = (bf16[128,1024]{1,0:T(8,128)(2,1)S(1)}, bf16[128,1024]{1,0:T(8,128)(2,1)S(1)}, u32[]{:S(2)}, u32[]{:S(2)}) collective-permute-start(bf16[128,1024]{1,0:T(8,128)(2,1)S(1)} %collective-permute-done.2.refs_4_), channel_id=1, source_target_pairs={{0,2},{1,3},{2,0},{3,1},{4,6},{5,7},{6,4},{7,5},{8,10},{9,11},{10,... | collective-permute-start | bytes 786440 | tf_op jit(solution)/shard_map/ppermute | solution.py:136
  32.8 17.7 %collective-permute-start.7 = (bf16[128,1024]{1,0:T(8,128)(2,1)S(1)}, bf16[128,1024]{1,0:T(8,128)(2,1)S(1)}, u32[]{:S(2)}, u32[]{:S(2)}) collective-permute-start(bf16[128,1024]{1,0:T(8,128)(2,1)S(1)} %collective-permute-done.2.refs_4_), channel_id=1, source_target_pairs={{0,1},{1,0},{2,3},{3,2},{4,5},{5,4},{6,7},{7,6},{8,9},{9,8},{10,11... | collective-permute-start | bytes 786440 | tf_op jit(solution)/shard_map/ppermute | solution.py:136
  33.2 24.2 %collective-permute-start.11 = (bf16[128,1024]{1,0:T(8,128)(2,1)S(1)}, bf16[128,1024]{1,0:T(8,128)(2,1)S(1)}, u32[]{:S(2)}, u32[]{:S(2)}) collective-permute-start(bf16[128,1024]{1,0:T(8,128)(2,1)S(1)} %collective-permute-done.3.refs_8_), channel_id=1, source_target_pairs={{0,2},{1,3},{2,0},{3,1},{4,6},{5,7},{6,4},{7,5},{8,10},{9,11},{10,... | collective-permute-start | bytes 786440 | tf_op jit(solution)/shard_map/ppermute | solution.py:136
  34.4 1.5 %collective-permute-start.6 = (bf16[128,1024]{1,0:T(8,128)(2,1)S(1)}, bf16[128,1024]{1,0:T(8,128)(2,1)S(1)}, u32[]{:S(2)}, u32[]{:S(2)}) collective-permute-start(bf16[128,1024]{1,0:T(8,128)(2,1)S(1)} %collective-permute-done.1.refs_2_), channel_id=1, source_target_pairs={{0,1},{1,0},{2,3},{3,2},{4,5},{5,4},{6,7},{7,6},{8,9},{9,8},{10,11... | collective-permute-start | bytes 786440 | tf_op jit(solution)/shard_map/ppermute | solution.py:136
  34.8 40.7 %copy-start.4 = (bf16[128,1024]{1,0:T(8,128)(2,1)}, bf16[128,1024]{1,0:T(8,128)(2,1)S(1)}, u32[]{:S(2)}) copy-start(bf16[128,1024]{1,0:T(8,128)(2,1)S(1)} %broadcast_select_fusion.refs_12_) | copy-start | bytes 786436
  34.8 33.2 %collective-permute-start.14 = (bf16[128,1024]{1,0:T(8,128)(2,1)S(1)}, bf16[128,1024]{1,0:T(8,128)(2,1)S(1)}, u32[]{:S(2)}, u32[]{:S(2)}) collective-permute-start(bf16[128,1024]{1,0:T(8,128)(2,1)S(1)} %broadcast_select_fusion.refs_12_), channel_id=1, source_target_pairs={{0,2},{1,3},{2,0},{3,1},{4,6},{5,7},{6,4},{7,5},{8,10},{9,11},{10,... | collective-permute-start | bytes 786440 | tf_op jit(solution)/shard_map/ppermute | solution.py:136
  35.9 32.9 %collective-permute-start.10 = (bf16[128,1024]{1,0:T(8,128)(2,1)S(1)}, bf16[128,1024]{1,0:T(8,128)(2,1)S(1)}, u32[]{:S(2)}, u32[]{:S(2)}) collective-permute-start(bf16[128,1024]{1,0:T(8,128)(2,1)S(1)} %collective-permute-done.3.refs_8_), channel_id=1, source_target_pairs={{0,1},{1,0},{2,3},{3,2},{4,5},{5,4},{6,7},{7,6},{8,9},{9,8},{10,11... | collective-permute-start | bytes 786440 | tf_op jit(solution)/shard_map/ppermute | solution.py:136
  49.2 19.7 %collective-permute-start.13 = (bf16[128,1024]{1,0:T(8,128)(2,1)S(1)}, bf16[128,1024]{1,0:T(8,128)(2,1)S(1)}, u32[]{:S(2)}, u32[]{:S(2)}) collective-permute-start(bf16[128,1024]{1,0:T(8,128)(2,1)S(1)} %broadcast_select_fusion.refs_12_), channel_id=1, source_target_pairs={{0,1},{1,0},{2,3},{3,2},{4,5},{5,4},{6,7},{7,6},{8,9},{9,8},{10,11... | collective-permute-start | bytes 786440 | tf_op jit(solution)/shard_map/ppermute | solution.py:136
  50.5 18.4 %collective-permute-start.9 = (bf16[128,1024]{1,0:T(8,128)(2,1)S(1)}, bf16[128,1024]{1,0:T(8,128)(2,1)S(1)}, u32[]{:S(2)}, u32[]{:S(2)}) collective-permute-start(bf16[128,1024]{1,0:T(8,128)(2,1)S(1)} %collective-permute-done.8.refs_6_), channel_id=1, source_target_pairs={{0,1},{1,0},{2,3},{3,2},{4,5},{5,4},{6,7},{7,6},{8,9},{9,8},{10,11... | collective-permute-start | bytes 786440 | tf_op jit(solution)/shard_map/ppermute | solution.py:136
  57.4 18.1 %copy-start.6 = (bf16[128,1024]{1,0:T(8,128)(2,1)}, bf16[128,1024]{1,0:T(8,128)(2,1)S(1)}, u32[]{:S(2)}) copy-start(bf16[128,1024]{1,0:T(8,128)(2,1)S(1)} %collective-permute-done.11.refs_10_) | copy-start | bytes 786436
  57.4 11.5 %collective-permute-start.12 = (bf16[128,1024]{1,0:T(8,128)(2,1)S(1)}, bf16[128,1024]{1,0:T(8,128)(2,1)S(1)}, u32[]{:S(2)}, u32[]{:S(2)}) collective-permute-start(bf16[128,1024]{1,0:T(8,128)(2,1)S(1)} %collective-permute-done.11.refs_10_), channel_id=1, source_target_pairs={{0,1},{1,0},{2,3},{3,2},{4,5},{5,4},{6,7},{7,6},{8,9},{9,8},{10,11... | collective-permute-start | bytes 786440 | tf_op jit(solution)/shard_map/ppermute | solution.py:136
  68.0 7.5 %copy-start.7 = (bf16[128,1024]{1,0:T(8,128)(2,1)}, bf16[128,1024]{1,0:T(8,128)(2,1)S(1)}, u32[]{:S(2)}) copy-start(bf16[128,1024]{1,0:T(8,128)(2,1)S(1)} %collective-permute-done.14.refs_14_) | copy-start | bytes 786436
  68.0 2.2 %collective-permute-start.15 = (bf16[128,1024]{1,0:T(8,128)(2,1)S(1)}, bf16[128,1024]{1,0:T(8,128)(2,1)}, u32[]{:S(2)}, u32[]{:S(2)}) collective-permute-start(bf16[128,1024]{1,0:T(8,128)(2,1)S(1)} %collective-permute-done.14.refs_14_), channel_id=1, source_target_pairs={{0,1},{1,0},{2,3},{3,2},{4,5},{5,4},{6,7},{7,6},{8,9},{9,8},{10,11... | collective-permute-start | bytes 786440 | tf_op jit(solution)/shard_map/ppermute | solution.py:136
  68.8 6.6 %copy-start.8 = (bf16[128,1024]{1,0:T(8,128)(2,1)}, bf16[128,1024]{1,0:T(8,128)(2,1)S(1)}, u32[]{:S(2)}) copy-start(bf16[128,1024]{1,0:T(8,128)(2,1)S(1)} %collective-permute-done.10.refs_9_) | copy-start | bytes 786436
  68.9 0.8 copy-start.10
  68.9 0.9 copy-start.11
  69.7 5.7 %copy-start.9 = (bf16[128,1024]{1,0:T(8,128)(2,1)}, bf16[128,1024]{1,0:T(8,128)(2,1)S(1)}, u32[]{:S(2)}) copy-start(bf16[128,1024]{1,0:T(8,128)(2,1)S(1)} %collective-permute-done.13.refs_13_) | copy-start | bytes 786436
